TPU v7x, 256 devices: a whole 4x4x8 slice. The times are simulated.
256 devices in a mesh: shard: 64 (over z, x, core), clus: 4 (over y).
Axes of the slice: x: 4, y: 4, z: 8, core: 2. Of those that a mesh axis runs over, the one named last changes fastest.
Arguments:
- embeddings: bfloat16 [131072, 1024], P(('shard', 'clus')), may hold values from -600 to 600
- cluster: int32 [131072], P(('shard', 'clus')), may hold values from 0 to 255, as said below
- arrival: int32 [131072], P(('shard', 'clus')), may hold values from 0 to 131071, each once
Outputs:
- best_seen: float32 [131072], P(('shard', 'clus'))
Inputs may be any that keep to these rules, and one draw needn't show every extreme that they name: Among the 512 rows of one device at most 16 have cluster ids with the same remainder modulo 64; on every device some remainders reach 16.
All inputs are finite; a program needn't handle non-finite values.
Results may differ from a plain program's by a relative error of at most 0.0003.
Values may be sent and summed in bfloat16 or wider, within the bound.
No kernel may reach another device: no remote copies, remote signals or barrier semaphores. Data moves between devices by JAX's collectives and lax.ppermute only.
A program may use at most 64 MiB of HBM per device.

v0:
```python
import jax
import jax.numpy as jnp
from jax import lax
from jax.sharding import PartitionSpec as P

EPSILON = 1e-06


def passed_along(array, axis, by):
    size = lax.axis_size(axis)
    return lax.ppermute(array, axis, [(i, (i + by) % size) for i in range(size)])


def inverse_norms(block_rows):
    wide = block_rows.astype(jnp.float32)
    return lax.rsqrt(jnp.sum(wide * wide, axis=1) + EPSILON)


def fold_panel(best_seen, query_side, panel):
    query_rows, query_cluster, query_arrival, query_inverse = query_side
    panel_rows, panel_cluster, panel_arrival = panel
    panel_inverse = inverse_norms(panel_rows)
    total = query_rows.shape[0]
    width = min(512, total)
    pieces = []
    for start in range(0, total, width):
        scores = lax.dot_general(
            query_rows[start : start + width],
            panel_rows,
            (((1,), (1,)), ((), ())),
            preferred_element_type=jnp.float32,
        )
        cosine = scores * query_inverse[start : start + width, None] * panel_inverse[None, :]
        allowed = (
            (query_cluster[start : start + width, None] == panel_cluster[None, :])
            & (panel_cluster[None, :] >= 0)
            & (panel_arrival[None, :] < query_arrival[start : start + width, None])
        )
        pieces.append(jnp.max(jnp.where(allowed, cosine, jnp.float32(-1.0)), axis=1))
    return jnp.maximum(best_seen, jnp.concatenate(pieces, axis=0))


def per_device(embeddings, cluster, arrival):
    owners = lax.axis_size("shard")
    row_count = embeddings.shape[0]
    capacity = 2 * row_count // owners
    slot_count = owners * capacity
    owner_index = cluster % owners
    member = (owner_index[:, None] == jnp.arange(owners, dtype=jnp.int32)[None, :]).astype(
        jnp.int32
    )
    before = jnp.cumsum(member, axis=0) - member
    within = jnp.sum(before * member, axis=1)
    slot_index = owner_index * capacity + within
    source = (
        jnp.full((slot_count,), row_count, jnp.int32)
        .at[slot_index]
        .set(jnp.arange(row_count, dtype=jnp.int32))
    )
    send_rows = jnp.take(embeddings, source, axis=0, mode="fill", fill_value=0)
    send_cluster = jnp.take(cluster, source, axis=0, mode="fill", fill_value=-1)
    send_arrival = jnp.take(arrival, source, axis=0, mode="fill", fill_value=0)
    own_rows, own_cluster, own_arrival = (
        lax.all_to_all(send_rows, "shard", split_axis=0, concat_axis=0, tiled=True),
        lax.all_to_all(send_cluster, "shard", split_axis=0, concat_axis=0, tiled=True),
        lax.all_to_all(send_arrival, "shard", split_axis=0, concat_axis=0, tiled=True),
    )
    query_side = (own_rows, own_cluster, own_arrival, inverse_norms(own_rows))
    own_panel = (own_rows, own_cluster, own_arrival)
    best_seen = fold_panel(jnp.full((slot_count,), -1.0, jnp.float32), query_side, own_panel)
    panel_count = lax.axis_size("clus")
    moving = own_panel
    for hop_index in range(panel_count - 1):
        moving = passed_along((moving[0], moving[1], moving[2]), "clus", 1)
        best_seen = fold_panel(best_seen, query_side, moving)
    returned = lax.all_to_all(best_seen, "shard", split_axis=0, concat_axis=0, tiled=True)
    return jnp.take(returned, slot_index, axis=0)


def solution(mesh):
    in_specs = (P(("shard", "clus"), None), P(("shard", "clus")), P(("shard", "clus")))
    out_specs = P(("shard", "clus"))
    return jax.shard_map(
        per_device, mesh=mesh, in_specs=in_specs, out_specs=out_specs, check_vma=False
    )
```

profile of v0, /device:TPU:1, one launch (start us, length us, event | category | flops | bytes accessed | tf_op | source)
XLA Modules:
  0.0 257.6 jit_solution(9697041865949885626)
XLA Ops:
  0.0 0.8 add_select_fusion
  0.8 0.7 fusion.29
  1.5 1.2 reduce-window.6
  2.7 0.2 slice_reduce_fusion
  3.0 0.1 fusion.2
  3.1 0.7 compare_select_fusion.1
  3.8 2.4 scatter_custom_fusion
  6.3 6.9 %gather_fusion = s32[1024]{0:T(1024)S(1)} fusion(s32[512]{0:T(512)S(1)} %copy-done.1, s32[1024]{0:T(1024)S(1)} %fusion.7), kind=kCustom, calls=%fused_computation | custom fusion | bytes 12288 | tf_op jit(solution)/shard_map/jit(_take)/gather | solution.py:61
  13.2 4.1 %gather_fusion.2 = bf16[1024,1024]{1,0:T(8,128)(2,1)S(1)} fusion(bf16[512,1024]{1,0:T(8,128)(2,1)S(1)} %copy-done, s32[1024]{0:T(1024)S(1)} %fusion.7), kind=kCustom, calls=%fused_computation.2 | custom fusion | bytes 4198400 | tf_op jit(solution)/shard_map/jit(_take)/gather | solution.py:60
  17.3 0.1 broadcast_in_dim.47
  17.3 0.2 broadcast_select_fusion
  17.6 62.5 %all_to_all.30 = bf16[64,16,1024]{2,1,0:T(8,128)(2,1)S(1)} all-to-all(bf16[64,16,1024]{2,1,0:T(8,128)(2,1)S(1)} %broadcast_select_fusion), channel_id=1, replica_groups=mesh['shard'=64,'clus'=4] {'shard'}, dimensions={0} | all-to-all | bytes 4194304 | tf_op jit(solution)/shard_map/all_to_all | solution.py:64
  80.1 1.3 collective-permute-start.2
  81.3 0.7 select_n.88
  82.0 7.3 %all-to-all-start = ((s32[64,16,1]{1,2,0:T(1,128)}), s32[64,16,1]{1,2,0:T(1,128)S(1)}, u32[]{:S(2)}, u32[]{:S(2)}) async-start(s32[64,16,1]{1,2,0:T(1,128)} %bitcast.2), calls=%async_computation | async-start | bytes 65536 | tf_op jit(solution)/shard_map/all_to_all | solution.py:65
  89.3 6.9 %gather_fusion.1 = s32[1024]{0:T(1024)S(1)} fusion(s32[512]{0:T(512)S(1)} %copy-done.2, s32[1024]{0:T(1024)S(1)} %fusion.7), kind=kCustom, calls=%fused_computation.1 | custom fusion | bytes 12288 | tf_op jit(solution)/shard_map/jit(_take)/gather | solution.py:62
  96.2 0.7 select_n.90
  96.9 1.8 all-to-all-done
  98.7 8.5 %all-to-all-start.1 = ((s32[64,16,1]{1,2,0:T(1,128)}), s32[64,16,1]{1,2,0:T(1,128)S(1)}, u32[]{:S(2)}, u32[]{:S(2)}) async-start(s32[64,16,1]{1,2,0:T(1,128)} %bitcast.3), calls=%async_computation.1 | async-start | bytes 65536 | tf_op jit(solution)/shard_map/all_to_all | solution.py:66
  107.2 0.5 broadcast.146
  107.7 0.7 reduce.29
  108.5 1.3 collective-permute-start
  109.9 0.1 slice_reduce_fusion.4
  110.0 6.6 %all-to-all-done.1 = s32[64,16,1]{1,2,0:T(1,128)S(1)} async-done(((s32[64,16,1]{1,2,0:T(1,128)}), s32[64,16,1]{1,2,0:T(1,128)S(1)}, u32[]{:S(2)}, u32[]{:S(2)}) %all-to-all-start.1) | async-done | bytes 4128 | tf_op jit(solution)/shard_map/all_to_all | solution.py:66
  116.6 0.1 slice_reduce_fusion.3
  116.7 0.7 reduce.28
  117.7 0.1 eq.59
  117.8 1.3 collective-permute-start.1
  119.1 7.4 %collective-permute-done = s32[1024]{0:T(1024)S(1)} collective-permute-done((s32[1024]{0:T(1024)S(1)}, s32[1024]{0:T(1024)S(1)}, u32[]{:S(2)}, u32[]{:S(2)}) %collective-permute-start) | collective-permute-done | bytes 4128 | tf_op jit(solution)/shard_map/ppermute | solution.py:11
  126.6 1.3 collective-permute-start.4
  127.9 2.3 collective-permute-done.3
  130.2 0.1 collective-permute-done.4
  130.3 0.4 collective-permute-start.7
  130.8 3.2 %collective-permute-done.6 = s32[1024]{0:T(1024)S(1)} collective-permute-done((s32[1024]{0:T(1024)S(1)}, s32[1024]{0:T(1024)S(1)}, u32[]{:S(2)}, u32[]{:S(2)}) %collective-permute-start.6) | collective-permute-done | bytes 4128 | tf_op jit(solution)/shard_map/ppermute | solution.py:11
  134.0 0.5 multiply_reduce_fusion.3
  134.5 0.1 collective-permute-start.5
  134.7 0.1 slice.83
  134.7 1.2 fusion.11
  136.0 1.0 copy-done.3
  137.0 1.7 select_reduce_fusion.6
  138.7 0.1 concatenate.57
  138.7 0.1 slice.77
  138.8 2.9 %select_reduce_fusion.7 = f32[512]{0:T(512)S(1)} fusion(bf16[512,1024]{1,0:T(8,128)(2,1)} %bitcast.51, bf16[1024,1024]{1,0:T(8,128)(2,1)S(1)} %bitcast.49, f32[1024]{0:T(1024)S(1)} %rsqrt.33, f32[512]{0:T(512)S(1)} %slice.77, s32[1024]{0:T(1024)S(1)} %lt.62, s32[1024]{0:T(1024)S(1)} %eq.61, pred[1024]{0:T(1024)(128)(4,1)S(1)} %broadcast_compare_fusion.3, ...), kind=kOutput, calls=%fused_computation.16 | convolution fusion | flops 1077935616 | bytes 3167232 | tf_op jit(solution)/shard_map/dot_general | solution.py:27
  141.8 0.1 concatenate.56
  141.8 2.2 multiply_reduce_fusion.2
  144.0 34.1 %collective-permute-done.5 = bf16[1024,1024]{1,0:T(8,128)(2,1)} collective-permute-done((bf16[1024,1024]{1,0:T(8,128)(2,1)}, bf16[1024,1024]{1,0:T(8,128)(2,1)}, u32[]{:S(2)}, u32[]{:S(2)}) %collective-permute-start.5) | collective-permute-done | bytes 2097184 | tf_op jit(solution)/shard_map/ppermute | solution.py:11
  178.1 3.3 %select_reduce_fusion.4 = f32[512]{0:T(512)S(1)} fusion(bf16[512,1024]{1,0:T(8,128)(2,1)S(1)} %bitcast.56, bf16[1024,1024]{1,0:T(8,128)(2,1)} %collective-permute-done.2, f32[1024]{0:T(1024)S(1)} %add_rsqrt_fusion.3, s32[1024]{0:T(1024)S(1)} %collective-permute-done.1, s32[1024]{0:T(1024)S(1)} %collective-permute-done, f32[512]{0:T(512)S(1)} %slice.83, ...), kind=kOutput, calls=%fused_computation.13 | convolution fusion | flops 1077935616 | bytes 3167232 | tf_op jit(solution)/shard_map/dot_general | solution.py:27
  181.5 0.1 concatenate.60
  181.5 3.6 %select_reduce_fusion.5 = f32[512]{0:T(512)S(1)} fusion(bf16[512,1024]{1,0:T(8,128)(2,1)} %bitcast.52, bf16[1024,1024]{1,0:T(8,128)(2,1)} %collective-permute-done.2, f32[1024]{0:T(1024)S(1)} %add_rsqrt_fusion.3, s32[1024]{0:T(1024)S(1)} %collective-permute-done.1, s32[1024]{0:T(1024)S(1)} %collective-permute-done, f32[512]{0:T(512)S(1)} %slice.77, ...), kind=kOutput, calls=%fused_computation.14 | convolution fusion | flops 1077935616 | bytes 3167232 | tf_op jit(solution)/shard_map/dot_general | solution.py:27
  185.2 0.1 concatenate.59
  185.3 2.2 multiply_reduce_fusion.1
  187.5 3.4 %select_reduce_fusion.2 = f32[512]{0:T(512)S(1)} fusion(bf16[512,1024]{1,0:T(8,128)(2,1)S(1)} %bitcast.57, bf16[1024,1024]{1,0:T(8,128)(2,1)} %collective-permute-done.5, f32[1024]{0:T(1024)S(1)} %add_rsqrt_fusion.2, s32[1024]{0:T(1024)S(1)} %collective-permute-done.4, s32[1024]{0:T(1024)S(1)} %collective-permute-done.3, f32[512]{0:T(512)S(1)} %slice.83, ...), kind=kOutput, calls=%fused_computation.11 | convolution fusion | flops 1077935616 | bytes 3167232 | tf_op jit(solution)/shard_map/dot_general | solution.py:27
  190.9 3.6 %select_reduce_fusion.3 = f32[512]{0:T(512)S(1)} fusion(bf16[512,1024]{1,0:T(8,128)(2,1)} %bitcast.53, bf16[1024,1024]{1,0:T(8,128)(2,1)} %collective-permute-done.5, f32[1024]{0:T(1024)S(1)} %add_rsqrt_fusion.2, s32[1024]{0:T(1024)S(1)} %collective-permute-done.4, s32[1024]{0:T(1024)S(1)} %collective-permute-done.3, f32[512]{0:T(512)S(1)} %slice.77, ...), kind=kOutput, calls=%fused_computation.12 | convolution fusion | flops 1077935616 | bytes 3167232 | tf_op jit(solution)/shard_map/dot_general | solution.py:27
  194.6 27.5 %collective-permute-done.8 = bf16[1024,1024]{1,0:T(8,128)(2,1)S(1)} collective-permute-done((bf16[1024,1024]{1,0:T(8,128)(2,1)}, bf16[1024,1024]{1,0:T(8,128)(2,1)S(1)}, u32[]{:S(2)}, u32[]{:S(2)}) %collective-permute-start.8) | collective-permute-done | bytes 2097184 | tf_op jit(solution)/shard_map/ppermute | solution.py:11
  222.1 0.5 multiply_reduce_fusion
  222.6 1.7 select_reduce_fusion
  224.4 2.9 %select_reduce_fusion.1 = f32[512]{0:T(512)S(1)} fusion(bf16[512,1024]{1,0:T(8,128)(2,1)} %bitcast.54, bf16[1024,1024]{1,0:T(8,128)(2,1)S(1)} %collective-permute-done.8, f32[1024]{0:T(1024)S(1)} %add_rsqrt_fusion.1, s32[1024]{0:T(1024)S(1)} %collective-permute-done.7, s32[1024]{0:T(1024)S(1)} %collective-permute-done.6, f32[512]{0:T(512)S(1)} %slice.77, ...), kind=kOutput, calls=%fused_computation.10 | convolution fusion | flops 1077935616 | bytes 3167232 | tf_op jit(solution)/shard_map/dot_general | solution.py:27
  227.4 0.6 fusion.6
  228.0 16.0 %all-to-all-start.3 = ((f32[64,16,1]{1,2,0:T(1,128)}), f32[64,16,1]{1,2,0:T(1,128)S(1)}, u32[]{:S(2)}, u32[]{:S(2)}) async-start(f32[64,16,1]{1,2,0:T(1,128)} %bitcast.8), calls=%async_computation.3 | async-start | bytes 65536 | tf_op jit(solution)/shard_map/all_to_all | solution.py:76
  244.1 9.4 %all-to-all-done.3 = f32[64,16,1]{1,2,0:T(1,128)S(1)} async-done(((f32[64,16,1]{1,2,0:T(1,128)}), f32[64,16,1]{1,2,0:T(1,128)S(1)}, u32[]{:S(2)}, u32[]{:S(2)}) %all-to-all-start.3) | async-done | bytes 4128 | tf_op jit(solution)/shard_map/all_to_all | solution.py:76
  253.4 0.5 broadcast.148
  253.9 0.7 reduce.30
  254.7 2.3 gather_fusion.3
  257.0 0.6 and_select_fusion
  (47 shorter events, 1.1 us)
Async XLA Ops:
  0.0 13.2 %copy-start = (bf16[512,1024]{1,0:T(8,128)(2,1)S(1)}, bf16[512,1024]{1,0:T(8,128)(2,1)}, u32[]{:S(2)}) copy-start(bf16[512,1024]{1,0:T(8,128)(2,1)} %param.3) | copy-start | bytes 3145732
  0.0 6.3 %copy-start.1 = (s32[512]{0:T(512)S(1)}, s32[512]{0:T(512)}, u32[]{:S(2)}) copy-start(s32[512]{0:T(512)} %param.4) | copy-start | bytes 6148
  17.6 71.8 %copy-start.2 = (s32[512]{0:T(512)S(1)}, s32[512]{0:T(512)}, u32[]{:S(2)}) copy-start(s32[512]{0:T(512)} %param.5) | copy-start | bytes 6148
  80.1 54.4 %collective-permute-start.2 = (bf16[1024,1024]{1,0:T(8,128)(2,1)S(1)}, bf16[1024,1024]{1,0:T(8,128)(2,1)}, u32[]{:S(2)}, u32[]{:S(2)}) collective-permute-start(bf16[1024,1024]{1,0:T(8,128)(2,1)S(1)} %bitcast.47), channel_id=1, source_target_pairs={{0,1},{1,2},{2,3},{3,0},{4,5},{5,6},{6,7},{7,4},{8,9},{9,10},{10,1... | collective-permute-start | bytes 6291464 | tf_op jit(solution)/shard_map/ppermute | solution.py:11
  82.0 16.7 %all-to-all-start = ((s32[64,16,1]{1,2,0:T(1,128)}), s32[64,16,1]{1,2,0:T(1,128)S(1)}, u32[]{:S(2)}, u32[]{:S(2)}) async-start(s32[64,16,1]{1,2,0:T(1,128)} %bitcast.2), calls=%async_computation | async-start | bytes 65536 | tf_op jit(solution)/shard_map/all_to_all | solution.py:65
  98.7 17.9 %all-to-all-start.1 = ((s32[64,16,1]{1,2,0:T(1,128)}), s32[64,16,1]{1,2,0:T(1,128)S(1)}, u32[]{:S(2)}, u32[]{:S(2)}) async-start(s32[64,16,1]{1,2,0:T(1,128)} %bitcast.3), calls=%async_computation.1 | async-start | bytes 65536 | tf_op jit(solution)/shard_map/all_to_all | solution.py:66
  108.5 18.0 %collective-permute-start = (s32[1024]{0:T(1024)S(1)}, s32[1024]{0:T(1024)S(1)}, u32[]{:S(2)}, u32[]{:S(2)}) collective-permute-start(s32[1024]{0:T(1024)S(1)} %eq.61), channel_id=1, source_target_pairs={{0,1},{1,2},{2,3},{3,0},{4,5},{5,6},{6,7},{7,4},{8,9},{9,10},{10,1... | collective-permute-start | bytes 12296 | tf_op jit(solution)/shard_map/ppermute | solution.py:11
  117.8 8.8 %collective-permute-start.1 = (s32[1024]{0:T(1024)S(1)}, s32[1024]{0:T(1024)S(1)}, u32[]{:S(2)}, u32[]{:S(2)}) collective-permute-start(s32[1024]{0:T(1024)S(1)} %lt.62), channel_id=1, source_target_pairs={{0,1},{1,2},{2,3},{3,0},{4,5},{5,6},{6,7},{7,4},{8,9},{9,10},{10,1... | collective-permute-start | bytes 12296 | tf_op jit(solution)/shard_map/ppermute | solution.py:11
  126.6 3.7 %collective-permute-start.3 = (s32[1024]{0:T(1024)S(1)}, s32[1024]{0:T(1024)S(1)}, u32[]{:S(2)}, u32[]{:S(2)}) collective-permute-start(s32[1024]{0:T(1024)S(1)} %collective-permute-done), channel_id=1, source_target_pairs={{0,1},{1,2},{2,3},{3,0},{4,5},{5,6},{6,7},{7,4},{8,9},{9,10},{10,1... | collective-permute-start | bytes 12296 | tf_op jit(solution)/shard_map/ppermute | solution.py:11
  126.6 3.7 %collective-permute-start.4 = (s32[1024]{0:T(1024)S(1)}, s32[1024]{0:T(1024)S(1)}, u32[]{:S(2)}, u32[]{:S(2)}) collective-permute-start(s32[1024]{0:T(1024)S(1)} %collective-permute-done.1), channel_id=1, source_target_pairs={{0,1},{1,2},{2,3},{3,0},{4,5},{5,6},{6,7},{7,4},{8,9},{9,10},{10,1... | collective-permute-start | bytes 12296 | tf_op jit(solution)/shard_map/ppermute | solution.py:11
  130.2 3.8 %collective-permute-start.6 = (s32[1024]{0:T(1024)S(1)}, s32[1024]{0:T(1024)S(1)}, u32[]{:S(2)}, u32[]{:S(2)}) collective-permute-start(s32[1024]{0:T(1024)S(1)} %collective-permute-done.3), channel_id=1, source_target_pairs={{0,1},{1,2},{2,3},{3,0},{4,5},{5,6},{6,7},{7,4},{8,9},{9,10},{10,1... | collective-permute-start | bytes 12296 | tf_op jit(solution)/shard_map/ppermute | solution.py:11
  130.3 92.3 %collective-permute-start.7 = (s32[1024]{0:T(1024)S(1)}, s32[1024]{0:T(1024)S(1)}, u32[]{:S(2)}, u32[]{:S(2)}) collective-permute-start(s32[1024]{0:T(1024)S(1)} %collective-permute-done.4), channel_id=1, source_target_pairs={{0,1},{1,2},{2,3},{3,0},{4,5},{5,6},{6,7},{7,4},{8,9},{9,10},{10,1... | collective-permute-start | bytes 12296 | tf_op jit(solution)/shard_map/ppermute | solution.py:11
  134.5 43.6 %collective-permute-start.5 = (bf16[1024,1024]{1,0:T(8,128)(2,1)}, bf16[1024,1024]{1,0:T(8,128)(2,1)}, u32[]{:S(2)}, u32[]{:S(2)}) collective-permute-start(bf16[1024,1024]{1,0:T(8,128)(2,1)} %collective-permute-done.2), channel_id=1, source_target_pairs={{0,1},{1,2},{2,3},{3,0},{4,5},{5,6},{6,7},{7,4},{8,9},{9,10},{10,1... | collective-permute-start | bytes 6291464 | tf_op jit(solution)/shard_map/ppermute | solution.py:11
  136.0 1.0 copy-start.3
  141.8 36.3 %copy-start.4 = (bf16[32,16,1024]{2,1,0:T(8,128)(2,1)S(1)}, bf16[32,16,1024]{2,1,0:T(8,128)(2,1)}, u32[]{:S(2)}) copy-start(bf16[32,16,1024]{2,1,0:T(8,128)(2,1)} %copy-done.3) | copy-start | bytes 3145732
  178.1 44.0 %collective-permute-start.8 = (bf16[1024,1024]{1,0:T(8,128)(2,1)}, bf16[1024,1024]{1,0:T(8,128)(2,1)S(1)}, u32[]{:S(2)}, u32[]{:S(2)}) collective-permute-start(bf16[1024,1024]{1,0:T(8,128)(2,1)} %collective-permute-done.5), channel_id=1, source_target_pairs={{0,1},{1,2},{2,3},{3,0},{4,5},{5,6},{6,7},{7,4},{8,9},{9,10},{10,1... | collective-permute-start | bytes 6291464 | tf_op jit(solution)/shard_map/ppermute | solution.py:11
  185.3 2.2 copy-start.5
  194.6 28.0 %copy-start.6 = (bf16[32,16,1024]{2,1,0:T(8,128)(2,1)S(1)}, bf16[32,16,1024]{2,1,0:T(8,128)(2,1)}, u32[]{:S(2)}) copy-start(bf16[32,16,1024]{2,1,0:T(8,128)(2,1)} %copy-done.3) | copy-start | bytes 3145732
  228.0 25.4 %all-to-all-start.3 = ((f32[64,16,1]{1,2,0:T(1,128)}), f32[64,16,1]{1,2,0:T(1,128)S(1)}, u32[]{:S(2)}, u32[]{:S(2)}) async-start(f32[64,16,1]{1,2,0:T(1,128)} %bitcast.8), calls=%async_computation.3 | async-start | bytes 65536 | tf_op jit(solution)/shard_map/all_to_all | solution.py:76
where the time goes:
time: 258 us
  waiting for transfers between devices  92.6 us (36%)
  blocking collectives  62.5 us (24%)
  starting transfers between devices  37.5 us (15%)
  local copies, waits for them, and re-layouts  29.1 us (11%)
  matrix products  23.2 us (9%)
  other arithmetic  12.5 us (5%)
    ppermute x9, waiting for transfers between devices, passed_along(): lax.ppermute(array, axis, [(i, (i + by) % size) for i in range(size)])  74.7 us
    all_to_all x1, blocking collectives, per_device(): lax.all_to_all(send_rows, 'shard', split_axis=0, concat_axis=0, tiled=True)  62.5 us
    dot_general x8, matrix products, fold_panel(): lax.dot_general(query_rows[start:start + width], panel_rows, (((1,), (1,)...  23.2 us
    all_to_all x1, starting transfers between devices, per_device(): lax.all_to_all(best_seen, 'shard', split_axis=0, concat_axis=0, tiled=True)  16 us
    all_to_all x1, waiting for transfers between devices, per_device(): lax.all_to_all(best_seen, 'shard', split_axis=0, concat_axis=0, tiled=True)  9.36 us
    all_to_all x1, starting transfers between devices, per_device(): lax.all_to_all(send_arrival, 'shard', split_axis=0, concat_axis=0, tiled=...  8.48 us
    all_to_all x1, starting transfers between devices, per_device(): lax.all_to_all(send_cluster, 'shard', split_axis=0, concat_axis=0, tiled=...  7.3 us
    gather x1, local copies, waits for them, and re-layouts, per_device(): send_cluster = jnp.take(cluster, source, axis=0, mode='fill', fill_value=-1)  6.87 us
  transfers between devices with their start and end apart: 12, of which 10 were waited for; matrix products, arithmetic and copies ran while one was open for 14% of the time, Pallas kernels for 0%

commit v1 on v0

v1 whole, which is shorter than its diff:
```python
import jax
import jax.numpy as jnp
from jax import lax
from jax.experimental import pallas as pl
from jax.experimental.pallas import tpu as pltpu
from jax.sharding import PartitionSpec as P

EPSILON = 1e-06
OWNERS = 64
SLOTS = 16
ROWS = 512
D = 1024
PANEL = OWNERS * SLOTS
LANES = 128
TILES = D // LANES
META = TILES * SLOTS
HEIGHT = META + 8
SPAN = 131072
NONE = -3e38
VMEM = pl.BlockSpec(memory_space=pltpu.VMEM)


def iota(shape, dim):
    return lax.broadcasted_iota(jnp.int32, shape, dim)


def nt(a, b):
    return lax.dot_general(a, b, (((1,), (1,)), ((), ())), preferred_element_type=jnp.float32)


def pack_kernel(rows_ref, cluster_ref, arrival_ref, out_ref, slot_ref):
    cluster, arrival = cluster_ref[...], arrival_ref[...]
    owner = cluster % OWNERS
    member = iota((OWNERS, ROWS), 0) == owner
    member_bf = member.astype(jnp.bfloat16)
    earlier = (iota((ROWS, ROWS), 0) < iota((ROWS, ROWS), 1)).astype(jnp.bfloat16)
    before = jnp.dot(member_bf, earlier, preferred_element_type=jnp.float32)
    within = jnp.sum(jnp.where(member, before, 0.0), axis=0, keepdims=True).astype(jnp.int32)
    slot = owner * SLOTS + within
    slot_ref[...] = slot
    rows = rows_ref[...]
    group = 16
    for g in range(OWNERS // group):
        first = g * group * SLOTS
        pick = (iota((group * SLOTS, ROWS), 0) + first == slot).astype(jnp.bfloat16)
        moved = jnp.dot(pick, rows, preferred_element_type=jnp.float32).astype(jnp.bfloat16)
        moved = moved.reshape(group, SLOTS, D)
        for k in range(TILES):
            out_ref[g * group : (g + 1) * group, k * SLOTS : (k + 1) * SLOTS, :] = moved[
                :, :, k * LANES : (k + 1) * LANES
            ]
    digits = (cluster + 1, arrival % 256, arrival // 256 % 256, arrival // 65536)
    lane = iota((LANES, ROWS), 0)
    spread = jnp.zeros((LANES, ROWS), jnp.int32)
    for k, digit in enumerate(digits):
        spread = jnp.where(lane // SLOTS == k, digit, spread)
    spread = jnp.where(lane % SLOTS == within, spread, 0).astype(jnp.float32).astype(jnp.bfloat16)
    meta = nt(member_bf, spread).astype(jnp.bfloat16)
    out_ref[:, META:, :] = jnp.broadcast_to(meta[:, None, :], (OWNERS, HEIGHT - META, LANES))


def pack(rows, cluster, arrival):
    return pl.pallas_call(
        pack_kernel,
        out_shape=(
            jax.ShapeDtypeStruct((OWNERS, HEIGHT, LANES), jnp.bfloat16),
            jax.ShapeDtypeStruct((1, ROWS), jnp.int32),
        ),
        in_specs=[VMEM] * 3,
        out_specs=(VMEM, VMEM),
        compiler_params=pltpu.CompilerParams(vmem_limit_bytes=40 * 2**20),
    )(rows, cluster.reshape(1, ROWS), arrival.reshape(1, ROWS))


def weights(shape, lane_dim, slot_dim):
    lane = iota(shape, lane_dim)
    mine = lane % SLOTS == iota(shape, slot_dim) % SLOTS
    kind = lane // SLOTS
    place = jnp.where(kind == 1, 1.0, jnp.where(kind == 2, 256.0, jnp.where(kind == 3, 65536.0, 0.0)))
    return jnp.where(mine & (kind == 0), 1.0, 0.0), jnp.where(mine, place, 0.0)


def column_keys(meta):
    spread = (iota((PANEL, OWNERS), 0) // SLOTS == iota((PANEL, OWNERS), 1)).astype(jnp.bfloat16)
    mine = jnp.dot(spread, meta, preferred_element_type=jnp.float32)
    of_cluster, of_arrival = weights((PANEL, LANES), 1, 0)
    cluster = jnp.sum(mine * of_cluster, axis=1, keepdims=True).astype(jnp.int32) - 1
    arrival = jnp.sum(mine * of_arrival, axis=1, keepdims=True).astype(jnp.int32)
    return cluster * SPAN + arrival


def row_keys(meta):
    of_cluster, of_arrival = weights((LANES, PANEL), 0, 1)
    mine = iota((OWNERS, PANEL), 1) // SLOTS == iota((OWNERS, PANEL), 0)

    def line(weight):
        every = jnp.dot(meta, weight.astype(jnp.bfloat16), preferred_element_type=jnp.float32)
        return jnp.sum(jnp.where(mine, every, 0.0), axis=0, keepdims=True).astype(jnp.int32)

    base = (line(of_cluster) - 1) * SPAN
    return base, base + line(of_arrival)


def squares(panel):
    width = 128
    eye = iota((width, width), 0) == iota((width, width), 1)
    for start in range(0, PANEL, width):
        part = panel[start : start + width, :]
        yield jnp.where(eye, nt(part, part), 0.0)


def column_inverse(panel):
    return lax.rsqrt(
        jnp.concatenate([jnp.sum(s, axis=1, keepdims=True) for s in squares(panel)], axis=0) + EPSILON
    )


def row_inverse(panel):
    return lax.rsqrt(
        jnp.concatenate([jnp.sum(s, axis=0, keepdims=True) for s in squares(panel)], axis=1) + EPSILON
    )


def fold(best, queries, base, limit, keys, key, inverse):
    width = 256
    for start in range(0, PANEL, width):
        scores = nt(keys[start : start + width, :], queries[...])
        here = key[start : start + width]
        value = scores * inverse[start : start + width]
        allowed = (here < limit) & (here >= base)
        best = jnp.maximum(best, jnp.max(jnp.where(allowed, value, NONE), axis=0, keepdims=True))
    return best


def to_block(line):
    mine = iota((OWNERS, PANEL), 1) // SLOTS == iota((OWNERS, PANEL), 0)
    place = (iota((PANEL, LANES), 0) % SLOTS == iota((PANEL, LANES), 1)).astype(jnp.float32)
    return lax.dot_general(
        jnp.where(mine, line, 0.0),
        place,
        (((1,), (0,)), ((), ())),
        precision=lax.Precision.HIGHEST,
        preferred_element_type=jnp.float32,
    )


def score_kernel(own_ref, below_ref, above_ref, own_out, below_out, own, below, above):
    for source, target in ((own_ref, own), (below_ref, below), (above_ref, above)):
        for k in range(TILES):
            target[:, k * LANES : (k + 1) * LANES] = source[
                :, k * SLOTS : (k + 1) * SLOTS, :
            ].reshape(PANEL, LANES)
    own_meta, below_meta, above_meta = (
        ref[:, META:, :].astype(jnp.float32)[:, 0, :].astype(jnp.bfloat16)
        for ref in (own_ref, below_ref, above_ref)
    )
    above_key, above_inverse = column_keys(above_meta), column_inverse(above)
    nothing = jnp.full((1, PANEL), NONE, jnp.float32)

    base, limit = row_keys(own_meta)
    best = fold(nothing, own, base, limit, own, column_keys(own_meta), column_inverse(own))
    best = fold(best, own, base, limit, below, column_keys(below_meta), column_inverse(below))
    best = fold(best, own, base, limit, above, above_key, above_inverse)
    own_out[...] = to_block(jnp.where(best > 0.5 * NONE, jnp.maximum(best * row_inverse(own), -1.0), -1.0))

    base, limit = row_keys(below_meta)
    best = fold(nothing, below, base, limit, above, above_key, above_inverse)
    below_out[...] = to_block(jnp.where(best > 0.5 * NONE, jnp.maximum(best * row_inverse(below), -1.0), -1.0))


def score(own, below, above):
    return pl.pallas_call(
        score_kernel,
        out_shape=(jax.ShapeDtypeStruct((OWNERS, LANES), jnp.float32),) * 2,
        in_specs=[VMEM] * 3,
        out_specs=(VMEM, VMEM),
        scratch_shapes=[pltpu.VMEM((PANEL, D), jnp.bfloat16)] * 3,
        compiler_params=pltpu.CompilerParams(vmem_limit_bytes=56 * 2**20),
    )(own, below, above)


def unpack_kernel(block_ref, slot_ref, out_ref):
    slot = slot_ref[...]
    member = (iota((OWNERS, ROWS), 0) == slot // SLOTS).astype(jnp.float32)
    every = lax.dot_general(
        block_ref[...],
        member,
        (((0,), (0,)), ((), ())),
        precision=lax.Precision.HIGHEST,
        preferred_element_type=jnp.float32,
    )
    mine = iota((LANES, ROWS), 0) == slot % SLOTS
    out_ref[...] = jnp.sum(jnp.where(mine, every, 0.0), axis=0, keepdims=True)


def unpack(block, slot):
    return pl.pallas_call(
        unpack_kernel,
        out_shape=jax.ShapeDtypeStruct((1, ROWS), jnp.float32),
        in_specs=[VMEM] * 2,
        out_specs=VMEM,
    )(block, slot).reshape(ROWS)


def passed_along(array, by):
    size = lax.axis_size("clus")
    return lax.ppermute(array, "clus", [(i, (i + by) % size) for i in range(size)])


def to_owners(array):
    return lax.all_to_all(array, "shard", split_axis=0, concat_axis=0, tiled=True)


def per_device(embeddings, cluster, arrival):
    packed, slot = pack(embeddings, cluster, arrival)
    own = to_owners(packed)
    below, above = passed_along(own, 1), passed_along(own, -1)
    best, for_below = score(own, below, above)
    best = jnp.maximum(best, passed_along(for_below, -1))
    return unpack(to_owners(best), slot)


def solution(mesh):
    in_specs = (P(("shard", "clus"), None), P(("shard", "clus")), P(("shard", "clus")))
    out_specs = P(("shard", "clus"))
    return jax.shard_map(
        per_device, mesh=mesh, in_specs=in_specs, out_specs=out_specs, check_vma=False
    )
```

time: 258 us -> 166 us (0.64)
  waiting for transfers between devices: 92.6 us -> 51.9 us
  starting transfers between devices: 37.5 us -> 4.46 us
  local copies, waits for them, and re-layouts: 29.1 us -> 3.93 us
  matrix products: 23.2 us -> 0 us
  blocking collectives: 62.5 us -> 85.1 us
  Pallas kernels: 0 us -> 19.9 us
  other arithmetic: 12.5 us -> 0.77 us
    all_to_all x3 -> x0, starting transfers between devices: 31.8 us -> none  [the longest x1 16 us: per_device(): lax.all_to_all(best_seen, 'shard', split_axis=0, concat_axis=0, tiled=True)]
    dot_general x8 -> x0, matrix products: 23.2 us -> none  [fold_panel(): lax.dot_general(query_rows[start:start + width], panel_rows, (((1,), (1,)...]
    ppermute x9 -> x3, waiting for transfers between devices: 74.7 us -> 51.9 us  [passed_along(): lax.ppermute(array, 'clus', [(i, (i + by) % size) for i in range(size)])]
    all_to_all x1 -> x2, blocking collectives: 62.5 us -> 85.1 us  [to_owners(): lax.all_to_all(array, 'shard', split_axis=0, concat_axis=0, tiled=True)]
    gather x4 -> x0, local copies, waits for them, and re-layouts: 20.1 us -> none  [the longest x1 6.87 us: per_device(): send_cluster = jnp.take(cluster, source, axis=0, mode='fill', fill_value=-1)]
    pallas_call x0 -> x3, Pallas kernels: none -> 19.9 us  [the longest x1 16.6 us: score(): pl.pallas_call(score_kernel, out_shape=(jax.ShapeDtypeStruct((OWNERS, LAN...]
    all_to_all x3 -> x0, waiting for transfers between devices: 17.8 us -> none  [the longest x1 9.36 us: per_device(): lax.all_to_all(best_seen, 'shard', split_axis=0, concat_axis=0, tiled=True)]
    reduce_sum x5 -> x0, other arithmetic: 5.4 us -> none  [the longest x4 5.27 us: inverse_norms(): return lax.rsqrt(jnp.sum(wide * wide, axis=1) + EPSILON)]
  transfers between devices with their start and end apart: 12 -> 3, of which waited for: 10 -> 3; matrix products, arithmetic and copies ran while one was open for 14% -> 0% of each run, Pallas kernels for 0% -> 0%
where the time goes in v1:
time: 166 us
  blocking collectives  85.1 us (51%)
  waiting for transfers between devices  51.9 us (31%)
  Pallas kernels  19.9 us (12%)
  starting transfers between devices  4.46 us (3%)
  local copies, waits for them, and re-layouts  3.93 us (2%)
    all_to_all x2, blocking collectives, to_owners(): lax.all_to_all(array, 'shard', split_axis=0, concat_axis=0, tiled=True)  85.1 us
    ppermute x3, waiting for transfers between devices, passed_along(): lax.ppermute(array, 'clus', [(i, (i + by) % size) for i in range(size)])  51.9 us
    pallas_call x1, Pallas kernels, score(): pl.pallas_call(score_kernel, out_shape=(jax.ShapeDtypeStruct((OWNERS, LAN...  16.6 us
    ppermute x3, starting transfers between devices, passed_along(): lax.ppermute(array, 'clus', [(i, (i + by) % size) for i in range(size)])  4.46 us
    unnamed x14, local copies, waits for them, and re-layouts  3.93 us
  transfers between devices with their start and end apart: 3, of which 3 were waited for; matrix products, arithmetic and copies ran while one was open for 0% of the time, Pallas kernels for 0%

profile of v1, /device:TPU:1, one launch (start us, length us, event | category | flops | bytes accessed | tf_op | source)
XLA Modules:
  0.0 166.0 jit_solution(6995044365664128990)
XLA Ops:
  0.0 0.0 copy-start
  0.0 1.2 copy-done
  1.2 0.0 copy-start.1
  1.2 0.7 copy-done.1
  1.9 0.0 copy-start.2
  1.9 0.7 copy-done.2
  2.6 1.6 shard_map.37
  4.2 0.0 copy-start.3
  4.2 69.0 %all_to_all.16.own_ref = bf16[64,136,128]{2,1,0:T(8,128)(2,1)S(1)} all-to-all(bf16[64,136,128]{2,1,0:T(8,128)(2,1)S(1)} %get-tuple-element.9), channel_id=1, replica_groups=mesh['shard'=64,'clus'=4] {'shard'}, dimensions={0} | all-to-all | bytes 4456448 | tf_op jit(solution)/shard_map/all_to_all | solution.py:211
  73.2 0.0 copy-done.3
  73.2 0.0 copy-start.4
  73.2 2.7 %collective-permute-start.1 = (bf16[64,136,128]{2,1,0:T(8,128)(2,1)S(1)}, bf16[64,136,128]{2,1,0:T(8,128)(2,1)S(1)}, u32[]{:S(2)}, u32[]{:S(2)}) collective-permute-start(bf16[64,136,128]{2,1,0:T(8,128)(2,1)S(1)} %all_to_all.16.own_ref), channel_id=1, source_target_pairs={{0,3},{1,0},{2,1},{3,2},{4,7},{5,4},{6,5},{7,6},{8,11},{9,8},{10,9... | collective-permute-start | bytes 6684680 | tf_op jit(solution)/shard_map/ppermute | solution.py:207
  75.9 0.0 collective-permute-start
  75.9 47.4 %collective-permute-done.1.above_ref = bf16[64,136,128]{2,1,0:T(8,128)(2,1)S(1)} collective-permute-done((bf16[64,136,128]{2,1,0:T(8,128)(2,1)S(1)}, bf16[64,136,128]{2,1,0:T(8,128)(2,1)S(1)}, u32[]{:S(2)}, u32[]{:S(2)}) %collective-permute-start.1) | collective-permute-done | bytes 2228256 | tf_op jit(solution)/shard_map/ppermute | solution.py:207
  123.3 0.0 copy-start.5
  123.3 3.1 %collective-permute-done.below_ref = bf16[64,136,128]{2,1,0:T(8,128)(2,1)S(1)} collective-permute-done((bf16[64,136,128]{2,1,0:T(8,128)(2,1)S(1)}, bf16[64,136,128]{2,1,0:T(8,128)(2,1)S(1)}, u32[]{:S(2)}, u32[]{:S(2)}) %collective-permute-start) | collective-permute-done | bytes 2228256 | tf_op jit(solution)/shard_map/ppermute | solution.py:207
  126.4 0.0 copy-done.4
  126.4 0.0 copy-done.5
  126.4 0.0 copy-start.6
  126.4 1.3 copy-done.6
  127.8 16.6 %shard_map.38 = (f32[64,128]{1,0:T(8,128)}, f32[64,128]{1,0:T(8,128)}) custom-call(bf16[64,136,128]{2,1,0:T(8,128)(2,1)} %copy-done.4, bf16[64,136,128]{2,1,0:T(8,128)(2,1)} %copy-done.6, bf16[64,136,128]{2,1,0:T(8,128)(2,1)} %copy-done.5), custom_call_target="tpu_custom_call" | custom-call | tf_op jit(solution)/shard_map/pallas_call | solution.py:172
  144.3 1.7 %collective-permute-start.2 = (f32[64,128]{1,0:T(8,128)}, f32[64,128]{1,0:T(8,128)S(1)}, u32[]{:S(2)}, u32[]{:S(2)}) collective-permute-start(f32[64,128]{1,0:T(8,128)} %get-tuple-element.11), channel_id=1, source_target_pairs={{0,3},{1,0},{2,1},{3,2},{4,7},{5,4},{6,5},{7,6},{8,11},{9,8},{10,9... | collective-permute-start | bytes 98312 | tf_op jit(solution)/shard_map/ppermute | solution.py:207
  146.1 1.3 collective-permute-done.2
  147.4 0.8 max.3
  148.2 16.1 %all_to_all.17 = f32[64,1,128]{2,1,0:T(1,128)} all-to-all(f32[64,1,128]{2,1,0:T(1,128)S(1)} %bitcast.9), channel_id=1, replica_groups=mesh['shard'=64,'clus'=4] {'shard'}, dimensions={0} | all-to-all | bytes 65536 | tf_op jit(solution)/shard_map/all_to_all | solution.py:211
  164.3 1.8 %shard_map.39 = f32[1,512]{1,0:T(1,128)} custom-call(f32[64,128]{1,0:T(8,128)} %bitcast.10, s32[1,512]{1,0:T(1,128)} %copy-done.3), custom_call_target="tpu_custom_call" | custom-call | tf_op jit(solution)/shard_map/pallas_call | solution.py:197
Async XLA Ops:
  0.0 1.2 copy-start
  1.2 0.7 copy-start.1
  1.9 0.7 copy-start.2
  4.2 69.0 %copy-start.3 = (s32[1,512]{1,0:T(1,128)}, s32[1,512]{1,0:T(1,128)S(1)}, u32[]{:S(2)}) copy-start(s32[1,512]{1,0:T(1,128)S(1)} %get-tuple-element.12.slot_ref) | copy-start | bytes 6148
  73.2 53.3 %copy-start.4 = (bf16[64,136,128]{2,1,0:T(8,128)(2,1)}, bf16[64,136,128]{2,1,0:T(8,128)(2,1)S(1)}, u32[]{:S(2)}) copy-start(bf16[64,136,128]{2,1,0:T(8,128)(2,1)S(1)} %all_to_all.16.own_ref) | copy-start | bytes 6684676
  73.2 50.2 %collective-permute-start.1 = (bf16[64,136,128]{2,1,0:T(8,128)(2,1)S(1)}, bf16[64,136,128]{2,1,0:T(8,128)(2,1)S(1)}, u32[]{:S(2)}, u32[]{:S(2)}) collective-permute-start(bf16[64,136,128]{2,1,0:T(8,128)(2,1)S(1)} %all_to_all.16.own_ref), channel_id=1, source_target_pairs={{0,3},{1,0},{2,1},{3,2},{4,7},{5,4},{6,5},{7,6},{8,11},{9,8},{10,9... | collective-permute-start | bytes 6684680 | tf_op jit(solution)/shard_map/ppermute | solution.py:207
  75.9 50.5 %collective-permute-start = (bf16[64,136,128]{2,1,0:T(8,128)(2,1)S(1)}, bf16[64,136,128]{2,1,0:T(8,128)(2,1)S(1)}, u32[]{:S(2)}, u32[]{:S(2)}) collective-permute-start(bf16[64,136,128]{2,1,0:T(8,128)(2,1)S(1)} %all_to_all.16.own_ref), channel_id=1, source_target_pairs={{0,1},{1,2},{2,3},{3,0},{4,5},{5,6},{6,7},{7,4},{8,9},{9,10},{10,1... | collective-permute-start | bytes 6684680 | tf_op jit(solution)/shard_map/ppermute | solution.py:207
  123.3 3.1 %copy-start.5 = (bf16[64,136,128]{2,1,0:T(8,128)(2,1)}, bf16[64,136,128]{2,1,0:T(8,128)(2,1)S(1)}, u32[]{:S(2)}) copy-start(bf16[64,136,128]{2,1,0:T(8,128)(2,1)S(1)} %collective-permute-done.1.above_ref) | copy-start | bytes 6684676
  126.4 1.3 copy-start.6
  144.3 3.1 %collective-permute-start.2 = (f32[64,128]{1,0:T(8,128)}, f32[64,128]{1,0:T(8,128)S(1)}, u32[]{:S(2)}, u32[]{:S(2)}) collective-permute-start(f32[64,128]{1,0:T(8,128)} %get-tuple-element.11), channel_id=1, source_target_pairs={{0,3},{1,0},{2,1},{3,2},{4,7},{5,4},{6,5},{7,6},{8,11},{9,8},{10,9... | collective-permute-start | bytes 98312 | tf_op jit(solution)/shard_map/ppermute | solution.py:207

commit v2 on v1

v2 whole, which is shorter than its diff:
```python
import jax
import jax.numpy as jnp
from jax import lax
from jax.experimental import pallas as pl
from jax.experimental.pallas import tpu as pltpu
from jax.sharding import PartitionSpec as P

EPSILON = 1e-06
OWNERS = 64
CAPACITY = 16
ROWS = 512
D = 1024
GROUPS = 32
SLOTS = 2 * CAPACITY
PANEL = GROUPS * SLOTS
LANES = 128
TILES = D // LANES
META = TILES * SLOTS
HEIGHT = META + 8
SPAN = 131072
NONE = -3e38
Z, X, Y = 8, 4, 4
AXES = ("shard", "clus")
VMEM = pl.BlockSpec(memory_space=pltpu.VMEM)
SMEM = pl.BlockSpec(memory_space=pltpu.SMEM)


def iota(shape, dim):
    return lax.broadcasted_iota(jnp.int32, shape, dim)


def nt(a, b):
    return lax.dot_general(a, b, (((1,), (1,)), ((), ())), preferred_element_type=jnp.float32)


def pack_kernel(core_ref, rows_ref, label_ref, other_rows_ref, other_label_ref, out_ref, slot_ref):
    core = core_ref[0]
    earlier = (iota((ROWS, ROWS), 0) < iota((ROWS, ROWS), 1)).astype(jnp.bfloat16)
    meta = jnp.zeros((GROUPS, LANES), jnp.float32)
    for half, (rows, label) in enumerate(
        ((rows_ref[...], label_ref[...]), (other_rows_ref[...], other_label_ref[...]))
    ):
        cluster, arrival = label // SPAN, label % SPAN
        owner = cluster % OWNERS
        group = owner // 2
        member = iota((OWNERS, ROWS), 0) == owner
        before = jnp.dot(member.astype(jnp.bfloat16), earlier, preferred_element_type=jnp.float32)
        within = jnp.sum(jnp.where(member, before, 0.0), axis=0, keepdims=True).astype(jnp.int32)
        mine = owner % 2 == core
        slot = group * CAPACITY + within
        if half == 0:
            slot_ref[...] = jnp.where(mine, slot, slot + GROUPS * CAPACITY)
        slot = jnp.where(mine, slot, -1)
        step = 8
        for g in range(0, GROUPS, step):
            pick = (iota((step * CAPACITY, ROWS), 0) + g * CAPACITY == slot).astype(jnp.bfloat16)
            moved = jnp.dot(pick, rows, preferred_element_type=jnp.float32).astype(jnp.bfloat16)
            moved = moved.reshape(step, CAPACITY, D)
            for k in range(TILES):
                first = k * SLOTS + half * CAPACITY
                out_ref[g : g + step, first : first + CAPACITY, :] = moved[
                    :, :, k * LANES : (k + 1) * LANES
                ]
        lane = iota((LANES, ROWS), 0)
        kind = lane // SLOTS
        digits = (cluster + 1, arrival % 256, arrival // 256 % 256, arrival // 65536)
        spread = jnp.zeros((LANES, ROWS), jnp.int32)
        for k, digit in enumerate(digits):
            spread = jnp.where(kind == k, digit, spread)
        spread = jnp.where(lane % SLOTS == within + half * CAPACITY, spread, 0)
        to = ((iota((GROUPS, ROWS), 0) == group) & mine).astype(jnp.bfloat16)
        meta = meta + nt(to, spread.astype(jnp.float32).astype(jnp.bfloat16))
    meta = meta.astype(jnp.bfloat16)
    out_ref[:, META:, :] = jnp.broadcast_to(meta[:, None, :], (GROUPS, HEIGHT - META, LANES))


def pack(core, rows, label, other_rows, other_label):
    return pl.pallas_call(
        pack_kernel,
        out_shape=(
            jax.ShapeDtypeStruct((GROUPS, HEIGHT, LANES), jnp.bfloat16),
            jax.ShapeDtypeStruct((1, ROWS), jnp.int32),
        ),
        in_specs=[SMEM] + [VMEM] * 4,
        out_specs=(VMEM, VMEM),
        compiler_params=pltpu.CompilerParams(vmem_limit_bytes=20 * 2**20),
    )(core, rows, label, other_rows, other_label)


def weights(shape, lane_dim, slot_dim):
    lane = iota(shape, lane_dim)
    mine = lane % SLOTS == iota(shape, slot_dim) % SLOTS
    kind = lane // SLOTS
    place = jnp.where(kind == 1, 1.0, jnp.where(kind == 2, 256.0, jnp.where(kind == 3, 65536.0, 0.0)))
    return jnp.where(mine & (kind == 0), 1.0, 0.0), jnp.where(mine, place, 0.0)


def column_keys(meta):
    spread = (iota((PANEL, GROUPS), 0) // SLOTS == iota((PANEL, GROUPS), 1)).astype(jnp.bfloat16)
    mine = jnp.dot(spread, meta, preferred_element_type=jnp.float32)
    of_cluster, of_arrival = weights((PANEL, LANES), 1, 0)
    cluster = jnp.sum(mine * of_cluster, axis=1, keepdims=True).astype(jnp.int32) - 1
    arrival = jnp.sum(mine * of_arrival, axis=1, keepdims=True).astype(jnp.int32)
    return cluster * SPAN + arrival


def row_keys(meta):
    of_cluster, of_arrival = weights((LANES, PANEL), 0, 1)
    mine = iota((GROUPS, PANEL), 1) // SLOTS == iota((GROUPS, PANEL), 0)

    def line(weight):
        every = jnp.dot(meta, weight.astype(jnp.bfloat16), preferred_element_type=jnp.float32)
        return jnp.sum(jnp.where(mine, every, 0.0), axis=0, keepdims=True).astype(jnp.int32)

    base = (line(of_cluster) - 1) * SPAN
    return base, base + line(of_arrival)


def squares(panel):
    width = 128
    eye = iota((width, width), 0) == iota((width, width), 1)
    for start in range(0, PANEL, width):
        part = panel[start : start + width, :]
        yield jnp.where(eye, nt(part, part), 0.0)


def column_inverse(panel):
    return lax.rsqrt(
        jnp.concatenate([jnp.sum(s, axis=1, keepdims=True) for s in squares(panel)], axis=0) + EPSILON
    )


def row_inverse(panel):
    return lax.rsqrt(
        jnp.concatenate([jnp.sum(s, axis=0, keepdims=True) for s in squares(panel)], axis=1) + EPSILON
    )


def fold(best, queries, base, limit, keys, key, inverse):
    width = 256
    for start in range(0, PANEL, width):
        scores = nt(keys[start : start + width, :], queries[...])
        here = key[start : start + width]
        value = scores * inverse[start : start + width]
        allowed = (here < limit) & (here >= base)
        best = jnp.maximum(best, jnp.max(jnp.where(allowed, value, NONE), axis=0, keepdims=True))
    return best


def to_block(line):
    mine = iota((GROUPS, PANEL), 1) // SLOTS == iota((GROUPS, PANEL), 0)
    place = (iota((PANEL, LANES), 0) % SLOTS == iota((PANEL, LANES), 1)).astype(jnp.float32)
    return lax.dot_general(
        jnp.where(mine, line, 0.0),
        place,
        (((1,), (0,)), ((), ())),
        precision=lax.Precision.HIGHEST,
        preferred_element_type=jnp.float32,
    )


def finish(best, inverse):
    return to_block(jnp.where(best > 0.5 * NONE, jnp.maximum(best * inverse, -1.0), -1.0))


def unfold(source, target):
    for k in range(TILES):
        target[:, k * LANES : (k + 1) * LANES] = source[:, k * SLOTS : (k + 1) * SLOTS, :].reshape(
            PANEL, LANES
        )
    return source[:, META:, :].astype(jnp.float32)[:, 0, :].astype(jnp.bfloat16)


def own_kernel(own_ref, own, best_ref, inverse_ref):
    meta = unfold(own_ref, own)
    base, limit = row_keys(meta)
    nothing = jnp.full((1, PANEL), NONE, jnp.float32)
    best_ref[...] = fold(nothing, own, base, limit, own, column_keys(meta), column_inverse(own))
    inverse_ref[...] = row_inverse(own)


def score_own(own):
    return pl.pallas_call(
        own_kernel,
        out_shape=(
            jax.ShapeDtypeStruct((PANEL, D), jnp.bfloat16),
            jax.ShapeDtypeStruct((1, PANEL), jnp.float32),
            jax.ShapeDtypeStruct((1, PANEL), jnp.float32),
        ),
        in_specs=[VMEM],
        out_specs=(VMEM, VMEM, VMEM),
        compiler_params=pltpu.CompilerParams(vmem_limit_bytes=20 * 2**20),
        cost_estimate=pl.CostEstimate(flops=4 * 2**30, bytes_accessed=4 * 2**20, transcendentals=0),
    )(own)


def rest_kernel(
    packed_ref, own, best_ref, inverse_ref, below_ref, above_ref, own_out, below_out, below, above
):
    own_meta = packed_ref[:, META:, :].astype(jnp.float32)[:, 0, :].astype(jnp.bfloat16)
    below_meta, above_meta = unfold(below_ref, below), unfold(above_ref, above)
    above_key, above_inverse = column_keys(above_meta), column_inverse(above)

    base, limit = row_keys(own_meta)
    best = fold(best_ref[...], own, base, limit, below, column_keys(below_meta), column_inverse(below))
    best = fold(best, own, base, limit, above, above_key, above_inverse)
    own_out[...] = finish(best, inverse_ref[...])

    base, limit = row_keys(below_meta)
    nothing = jnp.full((1, PANEL), NONE, jnp.float32)
    best = fold(nothing, below, base, limit, above, above_key, above_inverse)
    below_out[...] = finish(best, row_inverse(below))


def score_rest(packed, own, best, inverse, below, above):
    return pl.pallas_call(
        rest_kernel,
        out_shape=(jax.ShapeDtypeStruct((GROUPS, LANES), jnp.float32),) * 2,
        in_specs=[VMEM] * 6,
        out_specs=(VMEM, VMEM),
        scratch_shapes=[pltpu.VMEM((PANEL, D), jnp.bfloat16)] * 2,
        compiler_params=pltpu.CompilerParams(vmem_limit_bytes=24 * 2**20),
    )(packed, own, best, inverse, below, above)


def unpack_kernel(block_ref, other_ref, slot_ref, out_ref):
    slot = slot_ref[...]
    half = slot // (GROUPS * CAPACITY)
    member = (iota((GROUPS, ROWS), 0) == slot // CAPACITY % GROUPS).astype(jnp.float32)

    def every(ref):
        return lax.dot_general(
            ref[...],
            member,
            (((0,), (0,)), ((), ())),
            precision=lax.Precision.HIGHEST,
            preferred_element_type=jnp.float32,
        )

    mine = iota((LANES, ROWS), 0) == slot % CAPACITY + half * CAPACITY
    value = jnp.where(half == 0, every(block_ref), every(other_ref))
    out_ref[...] = jnp.sum(jnp.where(mine, value, 0.0), axis=0, keepdims=True)


def unpack(block, other, slot):
    return pl.pallas_call(
        unpack_kernel,
        out_shape=jax.ShapeDtypeStruct((1, ROWS), jnp.float32),
        in_specs=[VMEM] * 3,
        out_specs=VMEM,
    )(block, other, slot).reshape(ROWS)


def device(z, x, core, y):
    return ((z * X + x) * 2 + core) * Y + y


OWNER_GROUPS = [[device(z, x, 0, y) for z in range(Z) for x in range(X)] for y in range(Y)] + [
    [device(z, x, 1, y) for z in range(Z) for y in range(Y)] for x in range(X)
]


def to_owners(array):
    return lax.all_to_all(
        array, AXES, split_axis=0, concat_axis=0, tiled=True, axis_index_groups=OWNER_GROUPS
    )


def passed_along(array, by):
    pairs = []
    for z in range(Z):
        for x in range(X):
            for y in range(Y):
                pairs.append((device(z, x, 0, y), device(z, x, 0, (y + by) % Y)))
                pairs.append((device(z, x, 1, y), device(z, (x + by) % X, 1, y)))
    return lax.ppermute(array, AXES, pairs)


def other_core(array):
    size = lax.axis_size("shard")
    return lax.ppermute(array, "shard", [(i, i ^ 1) for i in range(size)])


def per_device(embeddings, cluster, arrival):
    label = (cluster * SPAN + arrival).reshape(1, ROWS)
    core = (lax.axis_index("shard") % 2).reshape(1)
    packed, slot = pack(core, embeddings, label, other_core(embeddings), other_core(label))
    own = to_owners(packed)
    below, above = passed_along(own, 1), passed_along(own, -1)
    rows, best, inverse = score_own(own)
    best, for_below = score_rest(own, rows, best, inverse, below, above)
    best = jnp.maximum(best, passed_along(for_below, -1))
    returned = to_owners(best)
    return unpack(returned, other_core(returned), slot)


def solution(mesh):
    in_specs = (P(("shard", "clus"), None), P(("shard", "clus")), P(("shard", "clus")))
    out_specs = P(("shard", "clus"))
    return jax.shard_map(
        per_device, mesh=mesh, in_specs=in_specs, out_specs=out_specs, check_vma=False
    )
```

time: 166 us -> 134 us (0.81)
  waiting for transfers between devices: 51.9 us -> 28.2 us
  blocking collectives: 85.1 us -> 74.4 us
  starting transfers between devices: 4.46 us -> 10.9 us
  local copies, waits for them, and re-layouts: 3.93 us -> 1.83 us
  Pallas kernels: 19.9 us -> 17.9 us
    ppermute x3 -> x6, waiting for transfers between devices: 51.9 us -> 28.2 us  [the longest x3 25.5 us: passed_along(): return lax.ppermute(array, AXES, pairs)]
    all_to_all x2, blocking collectives: 85.1 us -> 74.4 us  [to_owners(): lax.all_to_all(array, AXES, split_axis=0, concat_axis=0, tiled=True, axis...]
    ppermute x3 -> x6, starting transfers between devices: 4.46 us -> 10.9 us  [the longest x3 7.92 us: other_core(): return lax.ppermute(array, 'shard', [(i, i ^ 1) for i in range(size)])]
    pallas_call x2 -> x3, Pallas kernels: 18.2 us -> 15.9 us  [the longest x1 9.97 us: score_rest(): pl.pallas_call(rest_kernel, out_shape=(jax.ShapeDtypeStruct((GROUPS, LANE...]
    unnamed x14 -> x8, local copies, waits for them, and re-layouts: 3.93 us -> 1.83 us
  transfers between devices with their start and end apart: 3 -> 6, of which waited for: 3 -> 6; matrix products, arithmetic and copies ran while one was open for 0% -> 1% of each run, Pallas kernels for 0% -> 3%
where the time goes in v2:
time: 134 us
  blocking collectives  74.4 us (56%)
  waiting for transfers between devices  28.2 us (21%)
  Pallas kernels  17.9 us (13%)
  starting transfers between devices  10.9 us (8%)
  local copies, waits for them, and re-layouts  1.83 us (1%)
    all_to_all x2, blocking collectives, to_owners(): lax.all_to_all(array, AXES, split_axis=0, concat_axis=0, tiled=True, axis...  74.4 us
    ppermute x3, waiting for transfers between devices, passed_along(): return lax.ppermute(array, AXES, pairs)  25.5 us
    pallas_call x1, Pallas kernels, score_rest(): pl.pallas_call(rest_kernel, out_shape=(jax.ShapeDtypeStruct((GROUPS, LANE...  9.97 us
    ppermute x3, starting transfers between devices, other_core(): return lax.ppermute(array, 'shard', [(i, i ^ 1) for i in range(size)])  7.92 us
    pallas_call x1, Pallas kernels, score_own(): pl.pallas_call(own_kernel, out_shape=(jax.ShapeDtypeStruct((PANEL, D), jn...  4.12 us
    ppermute x3, starting transfers between devices, passed_along(): return lax.ppermute(array, AXES, pairs)  2.99 us
  transfers between devices with their start and end apart: 6, of which 6 were waited for; matrix products, arithmetic and copies ran while one was open for 1% of the time, Pallas kernels for 3%

profile of v2, /device:TPU:1, one launch (start us, length us, event | category | flops | bytes accessed | tf_op | source)
XLA Modules:
  0.0 134.0 jit_solution(4218769692245137486)
XLA Ops:
  0.0 3.2 %collective-permute-start = (bf16[512,1024]{1,0:T(8,128)(2,1)}, bf16[512,1024]{1,0:T(8,128)(2,1)S(1)}, u32[]{:S(2)}, u32[]{:S(2)}) collective-permute-start(bf16[512,1024]{1,0:T(8,128)(2,1)} %rows_ref.1), channel_id=1, source_target_pairs={{0,4},{4,0},{8,12},{12,8},{16,20},{20,16},{24,28},{28,24},{32,36},... | collective-permute-start | bytes 3145736 | tf_op jit(solution)/shard_map/ppermute | solution.py:281
  3.2 0.7 multiply_add_fusion
  3.9 0.0 collective-permute-start.1
  3.9 1.6 %collective-permute-done.1.other_label_ref = s32[1,512]{1,0:T(1,128)S(1)} collective-permute-done((s32[1,512]{1,0:T(1,128)S(1)}, s32[1,512]{1,0:T(1,128)S(1)}, u32[]{:S(2)}, u32[]{:S(2)}) %collective-permute-start.1) | collective-permute-done | bytes 2080 | tf_op jit(solution)/shard_map/ppermute | solution.py:281
  5.5 0.2 collective-permute-done.other_rows_ref
  5.7 0.0 copy-start
  5.7 1.2 copy-done
  7.0 1.8 %shard_map.37 = (bf16[32,264,128]{2,1,0:T(8,128)(2,1)S(1)}, s32[1,512]{1,0:T(1,128)S(1)}) custom-call(s32[1]{0:T(128)} %bitcast.core_ref, bf16[512,1024]{1,0:T(8,128)(2,1)S(1)} %copy-done, s32[1,512]{1,0:T(1,128)S(1)} %bitcast.8, bf16[512,1024]{1,0:T(8,128)(2,1)S(1)} %collective-permute-done.other_rows_ref, s32[1,512]{1,0:T(1,128)S(1)} %collective-permute-done.1.other_label_ref), custom_call_target="tpu_custom_call" | custom-call | tf_op jit(solution)/shard_map/pallas_call | solution.py:78
  8.8 0.0 copy-start.1
  8.8 61.9 %all_to_all.16.own_ref.packed_ref = bf16[32,264,128]{2,1,0:T(8,128)(2,1)S(1)} all-to-all(bf16[32,264,128]{2,1,0:T(8,128)(2,1)S(1)} %get-tuple-element.12), channel_id=1, replica_groups={{0,8,16,24,32,40,48,56,64,72,80,88,96,104,112,120,128,136,144,152,160,1..., dimensions={0} | all-to-all | bytes 4325376 | tf_op jit(solution)/shard_map/all_to_all | solution.py:264
  70.8 0.0 copy-done.1
  70.8 2.9 %collective-permute-start.3 = (bf16[32,264,128]{2,1,0:T(8,128)(2,1)S(1)}, bf16[32,264,128]{2,1,0:T(8,128)(2,1)S(1)}, u32[]{:S(2)}, u32[]{:S(2)}) collective-permute-start(bf16[32,264,128]{2,1,0:T(8,128)(2,1)S(1)} %all_to_all.16.own_ref.packed_ref), channel_id=1, source_target_pairs={{0,3},{4,28},{1,0},{5,29},{2,1},{6,30},{3,2},{7,31},{8,11},{12,4},... | collective-permute-start | bytes 6488072 | tf_op jit(solution)/shard_map/ppermute | solution.py:276
  73.7 0.0 collective-permute-start.2
  73.7 4.1 %shard_map.38 = (bf16[1024,1024]{1,0:T(8,128)(2,1)S(1)}, f32[1,1024]{1,0:T(1,128)S(1)}, f32[1,1024]{1,0:T(1,128)S(1)}) custom-call(bf16[32,264,128]{2,1,0:T(8,128)(2,1)S(1)} %all_to_all.16.own_ref.packed_ref), custom_call_target="tpu_custom_call" | custom-call | flops 4294967296 | bytes 4194304 | tf_op jit(solution)/shard_map/pallas_call | solution.py:183
  77.8 19.6 %collective-permute-done.3.above_ref = bf16[32,264,128]{2,1,0:T(8,128)(2,1)S(1)} collective-permute-done((bf16[32,264,128]{2,1,0:T(8,128)(2,1)S(1)}, bf16[32,264,128]{2,1,0:T(8,128)(2,1)S(1)}, u32[]{:S(2)}, u32[]{:S(2)}) %collective-permute-start.3) | collective-permute-done | bytes 2162720 | tf_op jit(solution)/shard_map/ppermute | solution.py:276
  97.3 3.4 %collective-permute-done.2.below_ref = bf16[32,264,128]{2,1,0:T(8,128)(2,1)S(1)} collective-permute-done((bf16[32,264,128]{2,1,0:T(8,128)(2,1)S(1)}, bf16[32,264,128]{2,1,0:T(8,128)(2,1)S(1)}, u32[]{:S(2)}, u32[]{:S(2)}) %collective-permute-start.2) | collective-permute-done | bytes 2162720 | tf_op jit(solution)/shard_map/ppermute | solution.py:276
  100.8 10.0 %shard_map.39 = (f32[32,128]{1,0:T(8,128)S(1)}, f32[32,128]{1,0:T(8,128)S(1)}) custom-call(bf16[32,264,128]{2,1,0:T(8,128)(2,1)S(1)} %all_to_all.16.own_ref.packed_ref, bf16[1024,1024]{1,0:T(8,128)(2,1)S(1)} %get-tuple-element.13.own, f32[1,1024]{1,0:T(1,128)S(1)} %get-tuple-element.14.best_ref, f32[1,1024]{1,0:T(1,128)S(1)} %get-tuple-element.15.inverse_ref, ...), custom_call_target="tpu_custom_call" | custom-call | tf_op jit(solution)/shard_map/pallas_call | solution.py:216
  110.7 0.1 collective-permute-start.4
  110.8 2.6 %collective-permute-done.4 = f32[32,128]{1,0:T(8,128)S(1)} collective-permute-done((f32[32,128]{1,0:T(8,128)S(1)}, f32[32,128]{1,0:T(8,128)S(1)}, u32[]{:S(2)}, u32[]{:S(2)}) %collective-permute-start.4) | collective-permute-done | bytes 16416 | tf_op jit(solution)/shard_map/ppermute | solution.py:276
  113.4 12.5 %all_to_all.17 = f32[32,1,128]{2,1,0:T(1,128)S(1)} all-to-all(f32[32,1,128]{2,1,0:T(1,128)S(1)} %bitcast.9), channel_id=1, replica_groups={{0,8,16,24,32,40,48,56,64,72,80,88,96,104,112,120,128,136,144,152,160,1..., dimensions={0} | all-to-all | bytes 32768 | tf_op jit(solution)/shard_map/all_to_all | solution.py:264
  125.9 0.0 copy-start.2
  125.9 4.7 %collective-permute-start.5 = (f32[32,128]{1,0:T(8,128)S(1)}, f32[32,128]{1,0:T(8,128)S(1)}, u32[]{:S(2)}, u32[]{:S(2)}) collective-permute-start(f32[32,128]{1,0:T(8,128)S(1)} %bitcast.10), channel_id=1, source_target_pairs={{0,4},{4,0},{8,12},{12,8},{16,20},{20,16},{24,28},{28,24},{32,36},... | collective-permute-start | bytes 49160 | tf_op jit(solution)/shard_map/ppermute | solution.py:281
  130.6 0.8 collective-permute-done.5.other_ref
  131.4 0.0 copy-start.3
  131.4 0.0 copy-done.2
  131.4 0.6 copy-done.3
  132.0 1.9 %shard_map.40 = f32[1,512]{1,0:T(1,128)} custom-call(f32[32,128]{1,0:T(8,128)} %bitcast.11, f32[32,128]{1,0:T(8,128)} %copy-done.3, s32[1,512]{1,0:T(1,128)} %copy-done.1), custom_call_target="tpu_custom_call" | custom-call | tf_op jit(solution)/shard_map/pallas_call | solution.py:246
  (1 shorter events, 0.0 us)
Async XLA Ops:
  0.0 5.7 %collective-permute-start = (bf16[512,1024]{1,0:T(8,128)(2,1)}, bf16[512,1024]{1,0:T(8,128)(2,1)S(1)}, u32[]{:S(2)}, u32[]{:S(2)}) collective-permute-start(bf16[512,1024]{1,0:T(8,128)(2,1)} %rows_ref.1), channel_id=1, source_target_pairs={{0,4},{4,0},{8,12},{12,8},{16,20},{20,16},{24,28},{28,24},{32,36},... | collective-permute-start | bytes 3145736 | tf_op jit(solution)/shard_map/ppermute | solution.py:281
  3.9 1.6 %collective-permute-start.1 = (s32[1,512]{1,0:T(1,128)S(1)}, s32[1,512]{1,0:T(1,128)S(1)}, u32[]{:S(2)}, u32[]{:S(2)}) collective-permute-start(s32[1,512]{1,0:T(1,128)S(1)} %bitcast.7), channel_id=1, source_target_pairs={{0,4},{4,0},{8,12},{12,8},{16,20},{20,16},{24,28},{28,24},{32,36},... | collective-permute-start | bytes 6152 | tf_op jit(solution)/shard_map/ppermute | solution.py:281
  5.7 1.2 copy-start
  8.8 61.9 %copy-start.1 = (s32[1,512]{1,0:T(1,128)}, s32[1,512]{1,0:T(1,128)S(1)}, u32[]{:S(2)}) copy-start(s32[1,512]{1,0:T(1,128)S(1)} %get-tuple-element.18.slot_ref) | copy-start | bytes 6148
  70.8 26.6 %collective-permute-start.3 = (bf16[32,264,128]{2,1,0:T(8,128)(2,1)S(1)}, bf16[32,264,128]{2,1,0:T(8,128)(2,1)S(1)}, u32[]{:S(2)}, u32[]{:S(2)}) collective-permute-start(bf16[32,264,128]{2,1,0:T(8,128)(2,1)S(1)} %all_to_all.16.own_ref.packed_ref), channel_id=1, source_target_pairs={{0,3},{4,28},{1,0},{5,29},{2,1},{6,30},{3,2},{7,31},{8,11},{12,4},... | collective-permute-start | bytes 6488072 | tf_op jit(solution)/shard_map/ppermute | solution.py:276
  73.7 27.1 %collective-permute-start.2 = (bf16[32,264,128]{2,1,0:T(8,128)(2,1)S(1)}, bf16[32,264,128]{2,1,0:T(8,128)(2,1)S(1)}, u32[]{:S(2)}, u32[]{:S(2)}) collective-permute-start(bf16[32,264,128]{2,1,0:T(8,128)(2,1)S(1)} %all_to_all.16.own_ref.packed_ref), channel_id=1, source_target_pairs={{0,1},{4,12},{1,2},{5,13},{2,3},{6,14},{3,0},{7,15},{8,9},{12,20},... | collective-permute-start | bytes 6488072 | tf_op jit(solution)/shard_map/ppermute | solution.py:276
  110.7 2.7 %collective-permute-start.4 = (f32[32,128]{1,0:T(8,128)S(1)}, f32[32,128]{1,0:T(8,128)S(1)}, u32[]{:S(2)}, u32[]{:S(2)}) collective-permute-start(f32[32,128]{1,0:T(8,128)S(1)} %get-tuple-element.17), channel_id=1, source_target_pairs={{0,3},{4,28},{1,0},{5,29},{2,1},{6,30},{3,2},{7,31},{8,11},{12,4},... | collective-permute-start | bytes 49160 | tf_op jit(solution)/shard_map/ppermute | solution.py:276
  125.9 5.5 %copy-start.2 = (f32[32,1,128]{2,1,0:T(1,128)}, f32[32,1,128]{2,1,0:T(1,128)S(1)}, u32[]{:S(2)}) copy-start(f32[32,1,128]{2,1,0:T(1,128)S(1)} %all_to_all.17) | copy-start | bytes 49156
  125.9 5.5 %collective-permute-start.5 = (f32[32,128]{1,0:T(8,128)S(1)}, f32[32,128]{1,0:T(8,128)S(1)}, u32[]{:S(2)}, u32[]{:S(2)}) collective-permute-start(f32[32,128]{1,0:T(8,128)S(1)} %bitcast.10), channel_id=1, source_target_pairs={{0,4},{4,0},{8,12},{12,8},{16,20},{20,16},{24,28},{28,24},{32,36},... | collective-permute-start | bytes 49160 | tf_op jit(solution)/shard_map/ppermute | solution.py:281
  131.4 0.6 copy-start.3

commit v3 on v2

--- a/solution.py
+++ b/solution.py
@@ -15,8 +15,9 @@
 PANEL = GROUPS * SLOTS
 LANES = 128
 TILES = D // LANES
-META = TILES * SLOTS
-HEIGHT = META + 8
+PARTS = (6, 2)
+META = PARTS[1] * SLOTS
+HEIGHTS = (PARTS[0] * SLOTS, META + 8)
 SPAN = 131072
 NONE = -3e38
 Z, X, Y = 8, 4, 4
@@ -33,7 +34,7 @@
     return lax.dot_general(a, b, (((1,), (1,)), ((), ())), preferred_element_type=jnp.float32)
 
 
-def pack_kernel(core_ref, rows_ref, label_ref, other_rows_ref, other_label_ref, out_ref, slot_ref):
+def pack_kernel(core_ref, rows_ref, label_ref, other_rows_ref, other_label_ref, first_ref, second_ref, slot_ref):
     core = core_ref[0]
     earlier = (iota((ROWS, ROWS), 0) < iota((ROWS, ROWS), 1)).astype(jnp.bfloat16)
     meta = jnp.zeros((GROUPS, LANES), jnp.float32)
@@ -57,8 +58,9 @@
             moved = jnp.dot(pick, rows, preferred_element_type=jnp.float32).astype(jnp.bfloat16)
             moved = moved.reshape(step, CAPACITY, D)
             for k in range(TILES):
-                first = k * SLOTS + half * CAPACITY
-                out_ref[g : g + step, first : first + CAPACITY, :] = moved[
+                out_ref, tile = (first_ref, k) if k < PARTS[0] else (second_ref, k - PARTS[0])
+                place = tile * SLOTS + half * CAPACITY
+                out_ref[g : g + step, place : place + CAPACITY, :] = moved[
                     :, :, k * LANES : (k + 1) * LANES
                 ]
         lane = iota((LANES, ROWS), 0)
@@ -71,18 +73,18 @@
         to = ((iota((GROUPS, ROWS), 0) == group) & mine).astype(jnp.bfloat16)
         meta = meta + nt(to, spread.astype(jnp.float32).astype(jnp.bfloat16))
     meta = meta.astype(jnp.bfloat16)
-    out_ref[:, META:, :] = jnp.broadcast_to(meta[:, None, :], (GROUPS, HEIGHT - META, LANES))
+    second_ref[:, META:, :] = jnp.broadcast_to(meta[:, None, :], (GROUPS, HEIGHTS[1] - META, LANES))
 
 
 def pack(core, rows, label, other_rows, other_label):
     return pl.pallas_call(
         pack_kernel,
-        out_shape=(
-            jax.ShapeDtypeStruct((GROUPS, HEIGHT, LANES), jnp.bfloat16),
-            jax.ShapeDtypeStruct((1, ROWS), jnp.int32),
-        ),
+        out_shape=tuple(
+            jax.ShapeDtypeStruct((GROUPS, height, LANES), jnp.bfloat16) for height in HEIGHTS
+        )
+        + (jax.ShapeDtypeStruct((1, ROWS), jnp.int32),),
         in_specs=[SMEM] + [VMEM] * 4,
-        out_specs=(VMEM, VMEM),
+        out_specs=(VMEM,) * 3,
         compiler_params=pltpu.CompilerParams(vmem_limit_bytes=20 * 2**20),
     )(core, rows, label, other_rows, other_label)
 
@@ -116,35 +118,65 @@
     return base, base + line(of_arrival)
 
 
-def squares(panel):
+def eye(width):
+    return iota((width, width), 0) == iota((width, width), 1)
+
+
+def as_row(column):
     width = 128
-    eye = iota((width, width), 0) == iota((width, width), 1)
-    for start in range(0, PANEL, width):
-        part = panel[start : start + width, :]
-        yield jnp.where(eye, nt(part, part), 0.0)
-
-
-def column_inverse(panel):
-    return lax.rsqrt(
-        jnp.concatenate([jnp.sum(s, axis=1, keepdims=True) for s in squares(panel)], axis=0) + EPSILON
-    )
-
-
-def row_inverse(panel):
-    return lax.rsqrt(
-        jnp.concatenate([jnp.sum(s, axis=0, keepdims=True) for s in squares(panel)], axis=1) + EPSILON
-    )
-
-
-def fold(best, queries, base, limit, keys, key, inverse):
+    return jnp.concatenate(
+        [
+            jnp.sum(jnp.where(eye(width), column[start : start + width], 0.0), axis=0, keepdims=True)
+            for start in range(0, PANEL, width)
+        ],
+        axis=1,
+    )
+
+
+def as_column(row):
+    width = 128
+    return jnp.concatenate(
+        [
+            jnp.sum(jnp.where(eye(width), row[:, start : start + width], 0.0), axis=1, keepdims=True)
+            for start in range(0, PANEL, width)
+        ],
+        axis=0,
+    )
+
+
+def tiles_of(source, count):
+    return [source[:, k * SLOTS : (k + 1) * SLOTS, :].reshape(PANEL, LANES) for k in range(count)]
+
+
+def squares(source, count):
+    total = jnp.zeros((PANEL, LANES), jnp.float32)
+    for tile in tiles_of(source, count):
+        wide = tile.astype(jnp.float32)
+        total = total + wide * wide
+    return jnp.sum(total, axis=1, keepdims=True)
+
+
+def unfold(source, target, count, at=0):
+    for k, tile in enumerate(tiles_of(source, count)):
+        target[:, (at + k) * LANES : (at + k + 1) * LANES] = tile
+
+
+def labels(source):
+    return source[:, META:, :].astype(jnp.float32)[:, 0, :].astype(jnp.bfloat16)
+
+
+def fold(best, tile_of, base, limit, key, inverse):
     width = 256
     for start in range(0, PANEL, width):
-        scores = nt(keys[start : start + width, :], queries[...])
         here = key[start : start + width]
-        value = scores * inverse[start : start + width]
+        value = tile_of(slice(start, start + width)) * inverse[start : start + width]
         allowed = (here < limit) & (here >= base)
         best = jnp.maximum(best, jnp.max(jnp.where(allowed, value, NONE), axis=0, keepdims=True))
     return best
+
+
+def nothing():
+    return jnp.full((1, PANEL), NONE, jnp.float32)
 
 
 def to_block(line):
@@ -163,64 +195,144 @@
     return to_block(jnp.where(best > 0.5 * NONE, jnp.maximum(best * inverse, -1.0), -1.0))
 
 
-def unfold(source, target):
-    for k in range(TILES):
-        target[:, k * LANES : (k + 1) * LANES] = source[:, k * SLOTS : (k + 1) * SLOTS, :].reshape(
-            PANEL, LANES
-        )
-    return source[:, META:, :].astype(jnp.float32)[:, 0, :].astype(jnp.bfloat16)
-
-
-def own_kernel(own_ref, own, best_ref, inverse_ref):
-    meta = unfold(own_ref, own)
+LINE = jax.ShapeDtypeStruct((1, PANEL), jnp.float32)
+SQUARE = jax.ShapeDtypeStruct((PANEL, PANEL), jnp.float32)
+HEAD = PARTS[0] * LANES
+TAIL = PARTS[1] * LANES
+
+
+def norms_kernel(below_ref, above_ref, below_out, above_out):
+    below_out[...] = as_row(squares(below_ref, PARTS[0]))
+    above_out[...] = as_row(squares(above_ref, PARTS[0]))
+
+
+def norms(below, above):
+    return pl.pallas_call(
+        norms_kernel,
+        out_shape=(LINE, LINE),
+        in_specs=[VMEM] * 2,
+        out_specs=(VMEM,) * 2,
+        compiler_params=pltpu.CompilerParams(vmem_limit_bytes=16 * 2**20),
+        cost_estimate=pl.CostEstimate(flops=32 * 2**30, bytes_accessed=2**25, transcendentals=0),
+    )(below, above)
+
+
+def head_kernel(
+    first_ref,
+    second_ref,
+    below_ref,
+    above_ref,
+    best_ref,
+    inverse_ref,
+    own_below,
+    own_above,
+    below_above,
+    own,
+    below,
+    above,
+):
+    unfold(first_ref, own, PARTS[0])
+    unfold(second_ref, own, PARTS[1], PARTS[0])
+    unfold(below_ref, below, PARTS[0])
+    unfold(above_ref, above, PARTS[0])
+    meta = labels(second_ref)
     base, limit = row_keys(meta)
-    nothing = jnp.full((1, PANEL), NONE, jnp.float32)
-    best_ref[...] = fold(nothing, own, base, limit, own, column_keys(meta), column_inverse(own))
-    inverse_ref[...] = row_inverse(own)
-
-
-def score_own(own):
+    inverse = lax.rsqrt(squares(first_ref, PARTS[0]) + squares(second_ref, PARTS[1]) + EPSILON)
+    inverse_ref[...] = as_row(inverse)
+    best_ref[...] = fold(
+        nothing(), lambda at: nt(own[at, :], own[...]), base, limit, column_keys(meta), inverse
+    )
+    width = 256
+    for start in range(0, PANEL, width):
+        at = slice(start, start + width)
+        own_below[at, :] = nt(below[at, :], own[:, :HEAD])
+        own_above[at, :] = nt(above[at, :], own[:, :HEAD])
+        below_above[at, :] = nt(above[at, :], below[...])
+
+
+def score_head(first, second, below, above):
     return pl.pallas_call(
-        own_kernel,
-        out_shape=(
-            jax.ShapeDtypeStruct((PANEL, D), jnp.bfloat16),
-            jax.ShapeDtypeStruct((1, PANEL), jnp.float32),
-            jax.ShapeDtypeStruct((1, PANEL), jnp.float32),
-        ),
-        in_specs=[VMEM],
-        out_specs=(VMEM, VMEM, VMEM),
-        compiler_params=pltpu.CompilerParams(vmem_limit_bytes=20 * 2**20),
-        cost_estimate=pl.CostEstimate(flops=4 * 2**30, bytes_accessed=4 * 2**20, transcendentals=0),
-    )(own)
-
-
-def rest_kernel(
-    packed_ref, own, best_ref, inverse_ref, below_ref, above_ref, own_out, below_out, below, above
+        head_kernel,
+        out_shape=(LINE, LINE, SQUARE, SQUARE, SQUARE),
+        in_specs=[VMEM] * 4,
+        out_specs=(VMEM,) * 5,
+        scratch_shapes=[pltpu.VMEM((PANEL, D), jnp.bfloat16)]
+        + [pltpu.VMEM((PANEL, HEAD), jnp.bfloat16)] * 2,
+        compiler_params=pltpu.CompilerParams(vmem_limit_bytes=32 * 2**20),
+        cost_estimate=pl.CostEstimate(flops=8 * 2**30, bytes_accessed=2**24, transcendentals=0),
+    )(first, second, below, above)
+
+
+def tail_kernel(
+    second_ref,
+    best_ref,
+    inverse_ref,
+    own_below,
+    own_above,
+    below_above,
+    below_norm_ref,
+    above_norm_ref,
+    below_ref,
+    above_ref,
+    own_out,
+    below_out,
+    own,
+    below,
+    above,
 ):
-    own_meta = packed_ref[:, META:, :].astype(jnp.float32)[:, 0, :].astype(jnp.bfloat16)
-    below_meta, above_meta = unfold(below_ref, below), unfold(above_ref, above)
-    above_key, above_inverse = column_keys(above_meta), column_inverse(above)
+    for source, target in ((second_ref, own), (below_ref, below), (above_ref, above)):
+        unfold(source, target, PARTS[1])
+    own_meta, below_meta, above_meta = labels(second_ref), labels(below_ref), labels(above_ref)
+
+    def inverse_of(norm_ref, source):
+        return lax.rsqrt(as_column(norm_ref[...]) + squares(source, PARTS[1]) + EPSILON)
+
+    below_inverse, above_inverse = (
+        inverse_of(below_norm_ref, below_ref),
+        inverse_of(above_norm_ref, above_ref),
+    )
+    above_key = column_keys(above_meta)
 
     base, limit = row_keys(own_meta)
-    best = fold(best_ref[...], own, base, limit, below, column_keys(below_meta), column_inverse(below))
-    best = fold(best, own, base, limit, above, above_key, above_inverse)
+    best = fold(
+        best_ref[...],
+        lambda at: own_below[at, :] + nt(below[at, :], own[...]),
+        base,
+        limit,
+        column_keys(below_meta),
+        below_inverse,
+    )
+    best = fold(
+        best,
+        lambda at: own_above[at, :] + nt(above[at, :], own[...]),
+        base,
+        limit,
+        above_key,
+        above_inverse,
+    )
     own_out[...] = finish(best, inverse_ref[...])
 
     base, limit = row_keys(below_meta)
-    nothing = jnp.full((1, PANEL), NONE, jnp.float32)
-    best = fold(nothing, below, base, limit, above, above_key, above_inverse)
-    below_out[...] = finish(best, row_inverse(below))
-
-
-def score_rest(packed, own, best, inverse, below, above):
+    best = fold(
+        nothing(),
+        lambda at: below_above[at, :] + nt(above[at, :], below[...]),
+        base,
+        limit,
+        above_key,
+        above_inverse,
+    )
+    below_out[...] = finish(best, as_row(below_inverse))
+
+
+def score_tail(second, head, below_norm, above_norm, below, above):
     return pl.pallas_call(
-        rest_kernel,
+        tail_kernel,
         out_shape=(jax.ShapeDtypeStruct((GROUPS, LANES), jnp.float32),) * 2,
-        in_specs=[VMEM] * 6,
+        in_specs=[VMEM] * 10,
         out_specs=(VMEM, VMEM),
-        scratch_shapes=[pltpu.VMEM((PANEL, D), jnp.bfloat16)] * 2,
-        compiler_params=pltpu.CompilerParams(vmem_limit_bytes=24 * 2**20),
-    )(packed, own, best, inverse, below, above)
+        scratch_shapes=[pltpu.VMEM((PANEL, TAIL), jnp.bfloat16)] * 3,
+        compiler_params=pltpu.CompilerParams(vmem_limit_bytes=28 * 2**20),
+    )(second, *head, below_norm, above_norm, below, above)
 
 
 def unpack_kernel(block_ref, other_ref, slot_ref, out_ref):
@@ -248,6 +360,7 @@
         out_shape=jax.ShapeDtypeStruct((1, ROWS), jnp.float32),
         in_specs=[VMEM] * 3,
         out_specs=VMEM,
+        compiler_params=pltpu.CompilerParams(vmem_limit_bytes=4 * 2**20),
     )(block, other, slot).reshape(ROWS)
 
 
@@ -284,11 +397,14 @@
 def per_device(embeddings, cluster, arrival):
     label = (cluster * SPAN + arrival).reshape(1, ROWS)
     core = (lax.axis_index("shard") % 2).reshape(1)
-    packed, slot = pack(core, embeddings, label, other_core(embeddings), other_core(label))
-    own = to_owners(packed)
-    below, above = passed_along(own, 1), passed_along(own, -1)
-    rows, best, inverse = score_own(own)
-    best, for_below = score_rest(own, rows, best, inverse, below, above)
+    first, second, slot = pack(core, embeddings, label, other_core(embeddings), other_core(label))
+    own_first = to_owners(first)
+    below_first, above_first = passed_along(own_first, 1), passed_along(own_first, -1)
+    own_second = to_owners(second)
+    below_second, above_second = passed_along(own_second, 1), passed_along(own_second, -1)
+    below_norm, above_norm = norms(below_first, above_first)
+    head = score_head(own_first, own_second, below_first, above_first)
+    best, for_below = score_tail(own_second, head, below_norm, above_norm, below_second, above_second)
     best = jnp.maximum(best, passed_along(for_below, -1))
     returned = to_owners(best)
     return unpack(returned, other_core(returned), slot)

time: 134 us -> 123 us (0.918)
  waiting for transfers between devices: 28.2 us -> 3.85 us
  blocking collectives: 74.4 us -> 83.4 us
  starting transfers between devices: 10.9 us -> 14.7 us
    ppermute x3 -> x5, waiting for transfers between devices: 25.5 us -> 1.22 us  [passed_along(): return lax.ppermute(array, AXES, pairs)]
    all_to_all x2 -> x3, blocking collectives: 74.4 us -> 83.4 us  [to_owners(): lax.all_to_all(array, AXES, split_axis=0, concat_axis=0, tiled=True, axis...]
    ppermute x3 -> x5, starting transfers between devices: 2.99 us -> 7.28 us  [passed_along(): return lax.ppermute(array, AXES, pairs)]
    pallas_call x3 -> x4, Pallas kernels: 15.9 us -> 17.2 us  [the longest x1 8.13 us: score_head(): pl.pallas_call(head_kernel, out_shape=(LINE, LINE, SQUARE, SQUARE, SQUARE...]
  transfers between devices with their start and end apart: 6 -> 8, of which waited for: 6 -> 4; matrix products, arithmetic and copies ran while one was open for 1% -> 1% of each run, Pallas kernels for 3% -> 7%
where the time goes in v3:
time: 123 us; the launch traced here: 122 us
  blocking collectives  83.4 us (68%)
  Pallas kernels  18.4 us (15%)
  starting transfers between devices  14.7 us (12%)
  waiting for transfers between devices  3.85 us (3%)
    all_to_all x3, blocking collectives, to_owners(): lax.all_to_all(array, AXES, split_axis=0, concat_axis=0, tiled=True, axis...  83.4 us
    pallas_call x1, Pallas kernels, score_head(): pl.pallas_call(head_kernel, out_shape=(LINE, LINE, SQUARE, SQUARE, SQUARE...  8.13 us
    ppermute x3, starting transfers between devices, other_core(): return lax.ppermute(array, 'shard', [(i, i ^ 1) for i in range(size)])  7.4 us
    ppermute x5, starting transfers between devices, passed_along(): return lax.ppermute(array, AXES, pairs)  7.28 us
    pallas_call x1, Pallas kernels, score_tail(): pl.pallas_call(tail_kernel, out_shape=(jax.ShapeDtypeStruct((GROUPS, LANE...  6.57 us
    ppermute x3, waiting for transfers between devices, other_core(): return lax.ppermute(array, 'shard', [(i, i ^ 1) for i in range(size)])  2.63 us
  transfers between devices with their start and end apart: 8, of which 4 were waited for; matrix products, arithmetic and copies ran while one was open for 1% of the time, Pallas kernels for 7%

profile of v3, /device:TPU:1, one launch (start us, length us, event | category | flops | bytes accessed | tf_op | source)
XLA Modules:
  0.0 122.4 jit_solution(15444027759108951205)
XLA Ops:
  0.0 3.2 %collective-permute-start = (bf16[512,1024]{1,0:T(8,128)(2,1)}, bf16[512,1024]{1,0:T(8,128)(2,1)S(1)}, u32[]{:S(2)}, u32[]{:S(2)}) collective-permute-start(bf16[512,1024]{1,0:T(8,128)(2,1)} %rows_ref.1), channel_id=1, source_target_pairs={{0,4},{4,0},{8,12},{12,8},{16,20},{20,16},{24,28},{28,24},{32,36},... | collective-permute-start | bytes 3145736 | tf_op jit(solution)/shard_map/ppermute | solution.py:394
  3.2 0.7 multiply_add_fusion
  3.9 0.0 collective-permute-start.1
  3.9 1.6 %collective-permute-done.1.other_label_ref = s32[1,512]{1,0:T(1,128)S(1)} collective-permute-done((s32[1,512]{1,0:T(1,128)S(1)}, s32[1,512]{1,0:T(1,128)S(1)}, u32[]{:S(2)}, u32[]{:S(2)}) %collective-permute-start.1) | collective-permute-done | bytes 2080 | tf_op jit(solution)/shard_map/ppermute | solution.py:394
  5.5 0.2 collective-permute-done.other_rows_ref
  5.7 0.0 copy-start
  5.7 1.2 copy-done
  7.0 1.8 %shard_map.37 = (bf16[32,192,128]{2,1,0:T(8,128)(2,1)S(1)}, bf16[32,72,128]{2,1,0:T(8,128)(2,1)S(1)}, s32[1,512]{1,0:T(1,128)S(1)}) custom-call(s32[1]{0:T(128)} %bitcast.core_ref, bf16[512,1024]{1,0:T(8,128)(2,1)S(1)} %copy-done, s32[1,512]{1,0:T(1,128)S(1)} %bitcast.10, bf16[512,1024]{1,0:T(8,128)(2,1)S(1)} %collective-permute-done.other_rows_ref, ...), custom_call_target="tpu_custom_call" | custom-call | tf_op jit(solution)/shard_map/pallas_call | solution.py:80
  8.8 47.6 %all_to_all.21.first_ref = bf16[32,192,128]{2,1,0:T(8,128)(2,1)S(1)} all-to-all(bf16[32,192,128]{2,1,0:T(8,128)(2,1)S(1)} %get-tuple-element.18), channel_id=1, replica_groups={{0,8,16,24,32,40,48,56,64,72,80,88,96,104,112,120,128,136,144,152,160,1..., dimensions={0} | all-to-all | bytes 3145728 | tf_op jit(solution)/shard_map/all_to_all | solution.py:377
  56.4 1.7 %collective-permute-start.2 = (bf16[32,192,128]{2,1,0:T(8,128)(2,1)S(1)}, bf16[32,192,128]{2,1,0:T(8,128)(2,1)S(1)}, u32[]{:S(2)}, u32[]{:S(2)}) collective-permute-start(bf16[32,192,128]{2,1,0:T(8,128)(2,1)S(1)} %all_to_all.21.first_ref), channel_id=1, source_target_pairs={{0,1},{4,12},{1,2},{5,13},{2,3},{6,14},{3,0},{7,15},{8,9},{12,20},... | collective-permute-start | bytes 4718600 | tf_op jit(solution)/shard_map/ppermute | solution.py:389
  58.1 1.4 %collective-permute-start.3 = (bf16[32,192,128]{2,1,0:T(8,128)(2,1)S(1)}, bf16[32,192,128]{2,1,0:T(8,128)(2,1)S(1)}, u32[]{:S(2)}, u32[]{:S(2)}) collective-permute-start(bf16[32,192,128]{2,1,0:T(8,128)(2,1)S(1)} %all_to_all.21.first_ref), channel_id=1, source_target_pairs={{0,3},{4,28},{1,0},{5,29},{2,1},{6,30},{3,2},{7,31},{8,11},{12,4},... | collective-permute-start | bytes 4718600 | tf_op jit(solution)/shard_map/ppermute | solution.py:389
  59.6 21.4 %all_to_all.22.second_ref = bf16[32,72,128]{2,1,0:T(8,128)(2,1)S(1)} all-to-all(bf16[32,72,128]{2,1,0:T(8,128)(2,1)S(1)} %get-tuple-element.17), channel_id=1, replica_groups={{0,8,16,24,32,40,48,56,64,72,80,88,96,104,112,120,128,136,144,152,160,1..., dimensions={0} | all-to-all | bytes 1179648 | tf_op jit(solution)/shard_map/all_to_all | solution.py:377
  81.0 0.0 collective-permute-start.4
  81.0 2.7 %collective-permute-start.5 = (bf16[32,72,128]{2,1,0:T(8,128)(2,1)S(1)}, bf16[32,72,128]{2,1,0:T(8,128)(2,1)S(1)}, u32[]{:S(2)}, u32[]{:S(2)}) collective-permute-start(bf16[32,72,128]{2,1,0:T(8,128)(2,1)S(1)} %all_to_all.22.second_ref), channel_id=1, source_target_pairs={{0,3},{4,28},{1,0},{5,29},{2,1},{6,30},{3,2},{7,31},{8,11},{12,4},... | collective-permute-start | bytes 1769480 | tf_op jit(solution)/shard_map/ppermute | solution.py:389
  83.7 0.0 collective-permute-done.2.below_ref
  83.7 0.0 collective-permute-done.3.above_ref
  83.7 0.7 shard_map.39
  84.4 8.1 %shard_map.38 = (f32[1,1024]{1,0:T(1,128)S(1)}, f32[1,1024]{1,0:T(1,128)S(1)}, f32[1024,1024]{1,0:T(8,128)S(1)}, f32[1024,1024]{1,0:T(8,128)S(1)}, f32[1024,1024]{1,0:T(8,128)S(1)}) custom-call(bf16[32,192,128]{2,1,0:T(8,128)(2,1)S(1)} %all_to_all.21.first_ref, bf16[32,72,128]{2,1,0:T(8,128)(2,1)S(1)} %all_to_all.22.second_ref, ...), custom_call_target="tpu_custom_call" | custom-call | flops 8589934592 | bytes 16777216 | tf_op jit(solution)/shard_map/pallas_call | solution.py:254
  92.5 0.0 collective-permute-done.4.below_ref
  92.5 0.0 collective-permute-done.5.above_ref
  92.5 6.6 %shard_map.40 = (f32[32,128]{1,0:T(8,128)S(1)}, f32[32,128]{1,0:T(8,128)S(1)}) custom-call(bf16[32,72,128]{2,1,0:T(8,128)(2,1)S(1)} %all_to_all.22.second_ref, f32[1,1024]{1,0:T(1,128)S(1)} %get-tuple-element.19.best_ref, f32[1,1024]{1,0:T(1,128)S(1)} %get-tuple-element.20.inverse_ref, f32[1024,1024]{1,0:T(8,128)S(1)} %get-tuple-element.21.own_below, ...), custom_call_target="tpu_custom_call" | custom-call | tf_op jit(solution)/shard_map/pallas_call | solution.py:328
  99.1 1.5 %collective-permute-start.6 = (f32[32,128]{1,0:T(8,128)S(1)}, f32[32,128]{1,0:T(8,128)S(1)}, u32[]{:S(2)}, u32[]{:S(2)}) collective-permute-start(f32[32,128]{1,0:T(8,128)S(1)} %get-tuple-element.27), channel_id=1, source_target_pairs={{0,3},{4,28},{1,0},{5,29},{2,1},{6,30},{3,2},{7,31},{8,11},{12,4},... | collective-permute-start | bytes 49160 | tf_op jit(solution)/shard_map/ppermute | solution.py:389
  100.6 1.2 collective-permute-done.6
  101.8 14.4 %all_to_all.23 = f32[32,1,128]{2,1,0:T(1,128)S(1)} all-to-all(f32[32,1,128]{2,1,0:T(1,128)S(1)} %bitcast.11), channel_id=1, replica_groups={{0,8,16,24,32,40,48,56,64,72,80,88,96,104,112,120,128,136,144,152,160,1..., dimensions={0} | all-to-all | bytes 32768 | tf_op jit(solution)/shard_map/all_to_all | solution.py:377
  116.2 4.2 %collective-permute-start.7 = (f32[32,128]{1,0:T(8,128)S(1)}, f32[32,128]{1,0:T(8,128)S(1)}, u32[]{:S(2)}, u32[]{:S(2)}) collective-permute-start(f32[32,128]{1,0:T(8,128)S(1)} %bitcast.7), channel_id=1, source_target_pairs={{0,4},{4,0},{8,12},{12,8},{16,20},{20,16},{24,28},{28,24},{32,36},... | collective-permute-start | bytes 49160 | tf_op jit(solution)/shard_map/ppermute | solution.py:394
  120.3 0.8 collective-permute-done.7.other_ref
  121.2 1.2 shard_map.41
  (1 shorter events, 0.0 us)
Async XLA Ops:
  0.0 5.7 %collective-permute-start = (bf16[512,1024]{1,0:T(8,128)(2,1)}, bf16[512,1024]{1,0:T(8,128)(2,1)S(1)}, u32[]{:S(2)}, u32[]{:S(2)}) collective-permute-start(bf16[512,1024]{1,0:T(8,128)(2,1)} %rows_ref.1), channel_id=1, source_target_pairs={{0,4},{4,0},{8,12},{12,8},{16,20},{20,16},{24,28},{28,24},{32,36},... | collective-permute-start | bytes 3145736 | tf_op jit(solution)/shard_map/ppermute | solution.py:394
  3.9 1.6 %collective-permute-start.1 = (s32[1,512]{1,0:T(1,128)S(1)}, s32[1,512]{1,0:T(1,128)S(1)}, u32[]{:S(2)}, u32[]{:S(2)}) collective-permute-start(s32[1,512]{1,0:T(1,128)S(1)} %bitcast.9), channel_id=1, source_target_pairs={{0,4},{4,0},{8,12},{12,8},{16,20},{20,16},{24,28},{28,24},{32,36},... | collective-permute-start | bytes 6152 | tf_op jit(solution)/shard_map/ppermute | solution.py:394
  5.7 1.2 %copy-start = (bf16[512,1024]{1,0:T(8,128)(2,1)S(1)}, bf16[512,1024]{1,0:T(8,128)(2,1)}, u32[]{:S(2)}) copy-start(bf16[512,1024]{1,0:T(8,128)(2,1)} %rows_ref.1) | copy-start | bytes 3145732
  56.4 27.2 %collective-permute-start.2 = (bf16[32,192,128]{2,1,0:T(8,128)(2,1)S(1)}, bf16[32,192,128]{2,1,0:T(8,128)(2,1)S(1)}, u32[]{:S(2)}, u32[]{:S(2)}) collective-permute-start(bf16[32,192,128]{2,1,0:T(8,128)(2,1)S(1)} %all_to_all.21.first_ref), channel_id=1, source_target_pairs={{0,1},{4,12},{1,2},{5,13},{2,3},{6,14},{3,0},{7,15},{8,9},{12,20},... | collective-permute-start | bytes 4718600 | tf_op jit(solution)/shard_map/ppermute | solution.py:389
  58.1 25.5 %collective-permute-start.3 = (bf16[32,192,128]{2,1,0:T(8,128)(2,1)S(1)}, bf16[32,192,128]{2,1,0:T(8,128)(2,1)S(1)}, u32[]{:S(2)}, u32[]{:S(2)}) collective-permute-start(bf16[32,192,128]{2,1,0:T(8,128)(2,1)S(1)} %all_to_all.21.first_ref), channel_id=1, source_target_pairs={{0,3},{4,28},{1,0},{5,29},{2,1},{6,30},{3,2},{7,31},{8,11},{12,4},... | collective-permute-start | bytes 4718600 | tf_op jit(solution)/shard_map/ppermute | solution.py:389
  81.0 11.5 %collective-permute-start.4 = (bf16[32,72,128]{2,1,0:T(8,128)(2,1)S(1)}, bf16[32,72,128]{2,1,0:T(8,128)(2,1)S(1)}, u32[]{:S(2)}, u32[]{:S(2)}) collective-permute-start(bf16[32,72,128]{2,1,0:T(8,128)(2,1)S(1)} %all_to_all.22.second_ref), channel_id=1, source_target_pairs={{0,1},{4,12},{1,2},{5,13},{2,3},{6,14},{3,0},{7,15},{8,9},{12,20},... | collective-permute-start | bytes 1769480 | tf_op jit(solution)/shard_map/ppermute | solution.py:389
  81.0 11.5 %collective-permute-start.5 = (bf16[32,72,128]{2,1,0:T(8,128)(2,1)S(1)}, bf16[32,72,128]{2,1,0:T(8,128)(2,1)S(1)}, u32[]{:S(2)}, u32[]{:S(2)}) collective-permute-start(bf16[32,72,128]{2,1,0:T(8,128)(2,1)S(1)} %all_to_all.22.second_ref), channel_id=1, source_target_pairs={{0,3},{4,28},{1,0},{5,29},{2,1},{6,30},{3,2},{7,31},{8,11},{12,4},... | collective-permute-start | bytes 1769480 | tf_op jit(solution)/shard_map/ppermute | solution.py:389
  99.1 2.7 %collective-permute-start.6 = (f32[32,128]{1,0:T(8,128)S(1)}, f32[32,128]{1,0:T(8,128)S(1)}, u32[]{:S(2)}, u32[]{:S(2)}) collective-permute-start(f32[32,128]{1,0:T(8,128)S(1)} %get-tuple-element.27), channel_id=1, source_target_pairs={{0,3},{4,28},{1,0},{5,29},{2,1},{6,30},{3,2},{7,31},{8,11},{12,4},... | collective-permute-start | bytes 49160 | tf_op jit(solution)/shard_map/ppermute | solution.py:389
  116.2 5.0 %collective-permute-start.7 = (f32[32,128]{1,0:T(8,128)S(1)}, f32[32,128]{1,0:T(8,128)S(1)}, u32[]{:S(2)}, u32[]{:S(2)}) collective-permute-start(f32[32,128]{1,0:T(8,128)S(1)} %bitcast.7), channel_id=1, source_target_pairs={{0,4},{4,0},{8,12},{12,8},{16,20},{20,16},{24,28},{28,24},{32,36},... | collective-permute-start | bytes 49160 | tf_op jit(solution)/shard_map/ppermute | solution.py:394

commit v4 on v0

v4 whole, which is shorter than its diff:
```python
import jax
import jax.numpy as jnp
from jax import lax
from jax.experimental import pallas as pl
from jax.experimental.pallas import tpu as pltpu
from jax.sharding import PartitionSpec as P

EPSILON = 1e-06
OWNERS = 64
CAPACITY = 16
ROWS = 512
D = 1024
GROUPS = 32
SLOTS = 2 * CAPACITY
PANEL = GROUPS * SLOTS
HALF = GROUPS * CAPACITY
LANES = 128
PER_TILE = LANES // SLOTS
TILES = D // LANES
PARTS = (6, 2)
LABELS = PARTS[0] * SLOTS
HEIGHTS = (LABELS + 8, PARTS[1] * SLOTS)
HEAD = PARTS[0] * LANES
TAIL = PARTS[1] * LANES
SPAN = 131072
NONE = float("-inf")
Z, X, Y = 8, 4, 4
AXES = ("shard", "clus")
VMEM = pl.BlockSpec(memory_space=pltpu.VMEM)
SMEM = pl.BlockSpec(memory_space=pltpu.SMEM)
LINE = jax.ShapeDtypeStruct((1, PANEL), jnp.float32)
SQUARE = jax.ShapeDtypeStruct((PANEL, PANEL), jnp.float32)


def iota(shape, dim):
    return lax.broadcasted_iota(jnp.int32, shape, dim)


def nt(a, b):
    return lax.dot_general(a, b, (((1,), (1,)), ((), ())), preferred_element_type=jnp.float32)


def eye(width):
    return iota((width, width), 0) == iota((width, width), 1)


def as_row(column):
    return jnp.concatenate(
        [
            jnp.sum(jnp.where(eye(LANES), column[i : i + LANES], 0.0), axis=0, keepdims=True)
            for i in range(0, column.shape[0], LANES)
        ],
        axis=1,
    )


def as_column(row):
    return jnp.concatenate(
        [
            jnp.sum(jnp.where(eye(LANES), row[:, i : i + LANES], 0.0), axis=1, keepdims=True)
            for i in range(0, row.shape[1], LANES)
        ],
        axis=0,
    )


def narrow(value):
    return value.astype(jnp.bfloat16).astype(jnp.float32)


def pack_half(half, core, place, rows, label, put):
    cluster, arrival = label // SPAN, label % SPAN
    owner = cluster % OWNERS
    earlier = (iota((ROWS, ROWS), 0) < iota((ROWS, ROWS), 1)).astype(jnp.bfloat16)
    member = iota((OWNERS, ROWS), 0) == owner
    before = jnp.dot(member.astype(jnp.bfloat16), earlier, preferred_element_type=jnp.float32)
    within = jnp.sum(jnp.where(member, before, 0.0), axis=0, keepdims=True).astype(jnp.int32)
    mine = owner % 2 == core
    slot = owner // 2 * CAPACITY + within

    wide = rows[...].astype(jnp.float32)
    norm = as_row(jnp.sum(wide * wide, axis=1, keepdims=True))
    high = narrow(norm)
    middle = narrow(norm - high)
    digits = (cluster + 1, arrival % 256, arrival // 256 % 256, arrival // 65536)
    digits = [digit.astype(jnp.float32) for digit in digits] + [high, middle, norm - high - middle]
    digits = jnp.concatenate(digits + [jnp.zeros((1, ROWS), jnp.float32)], axis=0).astype(jnp.bfloat16)

    lane = iota((8, LANES), 1)
    begin = place * SLOTS + half * CAPACITY
    window = (lane >= begin) & (lane < begin + CAPACITY)
    labels = []
    step = LANES // CAPACITY
    for g in range(0, GROUPS, step):
        pick = (iota((LANES, ROWS), 0) + g * CAPACITY == jnp.where(mine, slot, -1)).astype(jnp.bfloat16)
        moved = jnp.dot(pick, rows[...], preferred_element_type=jnp.float32).astype(jnp.bfloat16)
        moved = moved.reshape(step, CAPACITY, D)
        for k in range(TILES):
            put(g, step, k, moved[:, :, k * LANES : (k + 1) * LANES])
        line = nt(digits, pick)
        for j in range(step):
            turn = (begin + LANES - j * CAPACITY) % LANES
            labels.append(jnp.where(window, pltpu.roll(line, turn, 1), 0.0))
    return jnp.where(mine, slot, slot + HALF), labels


def pack_own_kernel(where_ref, rows_ref, label_ref, half_ref, labels_ref, slot_ref):
    def put(g, step, k, value):
        half_ref[g : g + step, k * CAPACITY : (k + 1) * CAPACITY, :] = value

    slot, labels = pack_half(0, where_ref[0], where_ref[1], rows_ref, label_ref[...], put)
    slot_ref[...] = slot
    for g in range(GROUPS):
        labels_ref[g] = labels[g]


def pack_own(where, rows, label):
    return pl.pallas_call(
        pack_own_kernel,
        out_shape=(
            jax.ShapeDtypeStruct((GROUPS, TILES * CAPACITY, LANES), jnp.bfloat16),
            jax.ShapeDtypeStruct((GROUPS, 8, LANES), jnp.float32),
            jax.ShapeDtypeStruct((1, ROWS), jnp.int32),
        ),
        in_specs=[SMEM] + [VMEM] * 2,
        out_specs=(VMEM,) * 3,
        compiler_params=pltpu.CompilerParams(vmem_limit_bytes=16 * 2**20),
        cost_estimate=pl.CostEstimate(flops=2**30, bytes_accessed=2**21, transcendentals=0),
    )(where, rows, label)


def pack_other_kernel(where_ref, rows_ref, label_ref, half_ref, labels_ref, first_ref, second_ref):
    def place(k, half):
        out_ref, tile = (first_ref, k) if k < PARTS[0] else (second_ref, k - PARTS[0])
        return out_ref, tile * SLOTS + half * CAPACITY

    def put(g, step, k, value):
        out_ref, at = place(k, 1)
        out_ref[g : g + step, at : at + CAPACITY, :] = value

    for k in range(TILES):
        out_ref, at = place(k, 0)
        out_ref[:, at : at + CAPACITY, :] = half_ref[:, k * CAPACITY : (k + 1) * CAPACITY, :]
    _, labels = pack_half(1, where_ref[0], where_ref[1], rows_ref, label_ref[...], put)
    for g in range(GROUPS):
        first_ref[g, LABELS:, :] = (labels[g] + labels_ref[g]).astype(jnp.bfloat16)


def pack_other(where, rows, label, half, labels):
    return pl.pallas_call(
        pack_other_kernel,
        out_shape=tuple(
            jax.ShapeDtypeStruct((GROUPS, height, LANES), jnp.bfloat16) for height in HEIGHTS
        ),
        in_specs=[SMEM] + [VMEM] * 4,
        out_specs=(VMEM,) * 2,
        compiler_params=pltpu.CompilerParams(vmem_limit_bytes=16 * 2**20),
    )(where, rows, label, half, labels)


def info(ref):
    tiles = ref[:, LABELS:, :].astype(jnp.float32).reshape(GROUPS // PER_TILE, PER_TILE, 8, LANES)
    rows = jnp.concatenate([jnp.sum(tiles[t], axis=0) for t in range(GROUPS // PER_TILE)], axis=1)
    cluster = rows[0:1] - 1.0
    arrival = rows[1:2] + 256.0 * rows[2:3] + 65536.0 * rows[3:4]
    inverse = lax.rsqrt(rows[4:5] + rows[5:6] + rows[6:7] + EPSILON)
    return cluster, arrival, inverse


def row_keys(cluster, arrival):
    base = cluster.astype(jnp.int32) * SPAN
    return base, base + arrival.astype(jnp.int32)


def column_keys(cluster, arrival):
    return as_column(cluster).astype(jnp.int32) * SPAN + as_column(arrival).astype(jnp.int32)


def unfold(source, target, count, at=0):
    for k in range(count):
        target[:, (at + k) * LANES : (at + k + 1) * LANES] = source[
            :, k * SLOTS : (k + 1) * SLOTS, :
        ].reshape(PANEL, LANES)


WIDTH = 256
CUTS = [slice(start, start + WIDTH) for start in range(0, PANEL, WIDTH)]


def head_kernel(
    first_ref, below_ref, above_ref, own_below, own_above, below_above, inverse_ref, own, below, above
):
    unfold(first_ref, own, PARTS[0])
    unfold(below_ref, below, PARTS[0])
    unfold(above_ref, above, PARTS[0])
    cluster, arrival, inverse_ref[0:1] = info(first_ref)
    own_base, own_limit = row_keys(cluster, arrival)
    cluster, arrival, inverse_ref[1:2] = info(below_ref)
    below_base, below_limit = row_keys(cluster, arrival)
    below_key = column_keys(cluster, arrival)
    cluster, arrival, inverse_ref[2:3] = info(above_ref)
    above_key = column_keys(cluster, arrival)

    def masked(key, base, limit, scores):
        return jnp.where((key < limit) & (key >= base), scores, NONE)

    for at in CUTS:
        own_below[at, :] = masked(below_key[at], own_base, own_limit, nt(below[at, :], own[...]))
        own_above[at, :] = masked(above_key[at], own_base, own_limit, nt(above[at, :], own[...]))
        below_above[at, :] = masked(above_key[at], below_base, below_limit, nt(above[at, :], below[...]))


def score_head(first, below, above):
    return pl.pallas_call(
        head_kernel,
        out_shape=(SQUARE, SQUARE, SQUARE, jax.ShapeDtypeStruct((8, PANEL), jnp.float32)),
        in_specs=[VMEM] * 3,
        out_specs=(VMEM,) * 4,
        scratch_shapes=[pltpu.VMEM((PANEL, HEAD), jnp.bfloat16)] * 3,
        compiler_params=pltpu.CompilerParams(vmem_limit_bytes=32 * 2**20),
        cost_estimate=pl.CostEstimate(flops=6 * 2**30, bytes_accessed=2**24, transcendentals=0),
    )(first, below, above)


def own_kernel(first_ref, second_ref, best_ref, own):
    unfold(first_ref, own, PARTS[0])
    unfold(second_ref, own, PARTS[1], PARTS[0])
    cluster, arrival, inverse = info(first_ref)
    base, limit = row_keys(cluster, arrival)
    key, scale = column_keys(cluster, arrival), as_column(inverse)
    best = jnp.full((1, PANEL), NONE, jnp.float32)
    for at in CUTS:
        value = nt(own[at, :], own[...]) * scale[at]
        value = jnp.where((key[at] < limit) & (key[at] >= base), value, NONE)
        best = jnp.maximum(best, jnp.max(value, axis=0, keepdims=True))
    best_ref[...] = best


def score_own(first, second):
    return pl.pallas_call(
        own_kernel,
        out_shape=LINE,
        in_specs=[VMEM] * 2,
        out_specs=VMEM,
        scratch_shapes=[pltpu.VMEM((PANEL, D), jnp.bfloat16)],
        compiler_params=pltpu.CompilerParams(vmem_limit_bytes=20 * 2**20),
        cost_estimate=pl.CostEstimate(flops=3 * 2**30, bytes_accessed=2**22, transcendentals=0),
    )(first, second)


def tail_kernel(
    best_ref,
    own_below,
    own_above,
    below_above,
    inverse_ref,
    second_ref,
    below_ref,
    above_ref,
    out_ref,
    own,
    below,
    above,
):
    for source, target in ((second_ref, own), (below_ref, below), (above_ref, above)):
        unfold(source, target, PARTS[1])
    below_scale, above_scale = as_column(inverse_ref[1:2]), as_column(inverse_ref[2:3])
    own_best, below_best = best_ref[...], jnp.full((1, PANEL), NONE, jnp.float32)

    def fold(best, value):
        return jnp.maximum(best, jnp.max(value, axis=0, keepdims=True))

    for at in CUTS:
        value = (own_below[at, :] + nt(below[at, :], own[...])) * below_scale[at]
        own_best = fold(own_best, value)
        value = (own_above[at, :] + nt(above[at, :], own[...])) * above_scale[at]
        own_best = fold(own_best, value)
        value = (below_above[at, :] + nt(above[at, :], below[...])) * above_scale[at]
        below_best = fold(below_best, value)
    own_best = jnp.maximum(own_best * inverse_ref[0:1], -1.0)
    below_best = jnp.maximum(below_best * inverse_ref[1:2], -1.0)

    shape = (PER_TILE, LANES)
    window, turn = iota(shape, 1) // SLOTS, iota(shape, 0)
    for t in range(GROUPS // PER_TILE):
        at = slice(t * LANES, (t + 1) * LANES)
        near = jnp.broadcast_to(own_best[:, at], shape)
        far = jnp.broadcast_to(pltpu.roll(below_best[:, at], LANES // 2, 1), shape)
        out_ref[t * PER_TILE : (t + 1) * PER_TILE, :] = jnp.where(
            window == turn, near, jnp.where(window == (turn + PER_TILE // 2) % PER_TILE, far, -1.0)
        )


def score_tail(best, head, second, below, above):
    return pl.pallas_call(
        tail_kernel,
        out_shape=jax.ShapeDtypeStruct((GROUPS, LANES), jnp.float32),
        in_specs=[VMEM] * 8,
        out_specs=VMEM,
        scratch_shapes=[pltpu.VMEM((PANEL, TAIL), jnp.bfloat16)] * 3,
        compiler_params=pltpu.CompilerParams(vmem_limit_bytes=28 * 2**20),
    )(best, *head, second, below, above)


def unpack_kernel(where_ref, own_ref, own_far_ref, other_ref, other_far_ref, slot_ref, out_ref):
    slot = slot_ref[...]
    half = slot // HALF
    blocks = jnp.concatenate(
        [
            jnp.maximum(near[...], pltpu.roll(far[...], LANES // 2, 1))
            for near, far in ((own_ref, own_far_ref), (other_ref, other_far_ref))
        ],
        axis=0,
    )
    high = narrow(blocks)
    middle = narrow(blocks - high)
    parts = jnp.concatenate([high, middle, blocks - high - middle], axis=1).astype(jnp.bfloat16)
    member = (iota((2 * GROUPS, ROWS), 0) == slot // CAPACITY).astype(jnp.bfloat16)
    every = lax.dot_general(
        parts, member, (((0,), (0,)), ((), ())), preferred_element_type=jnp.float32
    )
    place = jnp.where(half == 0, where_ref[1], where_ref[2])
    lane = place * SLOTS + half * CAPACITY + slot % CAPACITY
    out_ref[...] = jnp.sum(
        jnp.where(iota((3 * LANES, ROWS), 0) % LANES == lane, every, 0.0), axis=0, keepdims=True
    )


def unpack(where, own, own_far, other, other_far, slot):
    return pl.pallas_call(
        unpack_kernel,
        out_shape=jax.ShapeDtypeStruct((1, ROWS), jnp.float32),
        in_specs=[SMEM] + [VMEM] * 5,
        out_specs=VMEM,
        compiler_params=pltpu.CompilerParams(vmem_limit_bytes=4 * 2**20),
    )(where, own, own_far, other, other_far, slot).reshape(ROWS)


def device(z, x, core, y):
    return ((z * X + x) * 2 + core) * Y + y


PLACES = [(z, x, y) for z in range(Z) for x in range(X) for y in range(Y)]
OWNER_GROUPS = [[device(z, x, 0, y) for z in range(Z) for x in range(X)] for y in range(Y)] + [
    [device(z, x, 1, y) for z in range(Z) for y in range(Y)] for x in range(X)
]


def to_owners(array):
    return lax.all_to_all(
        array, AXES, split_axis=0, concat_axis=0, tiled=True, axis_index_groups=OWNER_GROUPS
    )


def passed_along(array, by, cross=0):
    pairs = []
    for z, x, y in PLACES:
        pairs.append((device(z, x, 0, y), device(z, x, cross, (y + by) % Y)))
        pairs.append((device(z, x, 1, y), device(z, (x + by) % X, 1 - cross, y)))
    return lax.ppermute(array, AXES, pairs)


def other_core(array):
    size = lax.axis_size("shard")
    return lax.ppermute(array, "shard", [(i, i ^ 1) for i in range(size)])


def per_device(embeddings, cluster, arrival):
    label = (cluster * SPAN + arrival).reshape(1, ROWS)
    shard, y = lax.axis_index("shard"), lax.axis_index("clus")
    core, x = shard % 2, shard // 2 % X
    where = jnp.stack([core, jnp.where(core == 0, x, y), jnp.where(core == 0, y, x)])
    half, labels, slot = pack_own(where, embeddings, label)
    first, second = pack_other(where, other_core(embeddings), other_core(label), half, labels)
    own_first = to_owners(first)
    below_first, above_first = passed_along(own_first, 1), passed_along(own_first, -1)
    own_second = to_owners(second)
    below_second, above_second = passed_along(own_second, 1), passed_along(own_second, -1)
    head = score_head(own_first, below_first, above_first)
    best = score_own(own_first, own_second)
    block = to_owners(score_tail(best, head, own_second, below_second, above_second))
    near, far, across = other_core(block), passed_along(block, -1), passed_along(block, -1, 1)
    return unpack(where, block, far, near, across, slot)


def solution(mesh):
    in_specs = (P(("shard", "clus"), None), P(("shard", "clus")), P(("shard", "clus")))
    out_specs = P(("shard", "clus"))
    return jax.shard_map(
        per_device, mesh=mesh, in_specs=in_specs, out_specs=out_specs, check_vma=False
    )
```

time: 258 us -> 119 us (0.46)
  waiting for transfers between devices: 92.6 us -> 2.35 us
  local copies, waits for them, and re-layouts: 29.1 us -> 1.23 us
  matrix products: 23.2 us -> 0 us
  starting transfers between devices: 37.5 us -> 14.7 us
  blocking collectives: 62.5 us -> 83.5 us
  Pallas kernels: 0 us -> 16.1 us
  other arithmetic: 12.5 us -> 0.78 us
    ppermute x9, waiting for transfers between devices: 74.7 us -> 2.35 us  [the longest x6 2.34 us: passed_along(): return lax.ppermute(array, AXES, pairs)]
    all_to_all x3 -> x0, starting transfers between devices: 31.8 us -> none  [the longest x1 16 us: per_device(): lax.all_to_all(best_seen, 'shard', split_axis=0, concat_axis=0, tiled=True)]
    dot_general x8 -> x0, matrix products: 23.2 us -> none  [fold_panel(): lax.dot_general(query_rows[start:start + width], panel_rows, (((1,), (1,)...]
    all_to_all x1 -> x3, blocking collectives: 62.5 us -> 83.5 us  [to_owners(): lax.all_to_all(array, AXES, split_axis=0, concat_axis=0, tiled=True, axis...]
    gather x4 -> x0, local copies, waits for them, and re-layouts: 20.1 us -> none  [the longest x1 6.87 us: per_device(): send_cluster = jnp.take(cluster, source, axis=0, mode='fill', fill_value=-1)]
    all_to_all x3 -> x0, waiting for transfers between devices: 17.8 us -> none  [the longest x1 9.36 us: per_device(): lax.all_to_all(best_seen, 'shard', split_axis=0, concat_axis=0, tiled=True)]
    pallas_call x0 -> x6, Pallas kernels: none -> 16.1 us  [the longest x1 5.59 us: score_head(): pl.pallas_call(head_kernel, out_shape=(SQUARE, SQUARE, SQUARE, jax.ShapeD...]
    ppermute x9, starting transfers between devices: 5.7 us -> 14.7 us  [the longest x3 7.54 us: other_core(): return lax.ppermute(array, 'shard', [(i, i ^ 1) for i in range(size)])]
  transfers between devices with their start and end apart: 12 -> 9, of which waited for: 10 -> 1; matrix products, arithmetic and copies ran while one was open for 14% -> 1% of each run, Pallas kernels for 0% -> 9%
where the time goes in v4:
time: 119 us
  blocking collectives  83.5 us (70%)
  Pallas kernels  16.1 us (14%)
  starting transfers between devices  14.7 us (12%)
  waiting for transfers between devices  2.35 us (2%)
  local copies, waits for them, and re-layouts  1.23 us (1%)
    all_to_all x3, blocking collectives, to_owners(): lax.all_to_all(array, AXES, split_axis=0, concat_axis=0, tiled=True, axis...  83.5 us
    ppermute x3, starting transfers between devices, other_core(): return lax.ppermute(array, 'shard', [(i, i ^ 1) for i in range(size)])  7.54 us
    ppermute x6, starting transfers between devices, passed_along(): return lax.ppermute(array, AXES, pairs)  7.17 us
    pallas_call x1, Pallas kernels, score_head(): pl.pallas_call(head_kernel, out_shape=(SQUARE, SQUARE, SQUARE, jax.ShapeD...  5.59 us
    pallas_call x1, Pallas kernels, score_own(): pl.pallas_call(own_kernel, out_shape=LINE, in_specs=[VMEM] * 2, out_specs...  2.86 us
    pallas_call x1, Pallas kernels, score_tail(): pl.pallas_call(tail_kernel, out_shape=jax.ShapeDtypeStruct((GROUPS, LANES...  2.52 us
  transfers between devices with their start and end apart: 9, of which 1 were waited for; matrix products, arithmetic and copies ran while one was open for 1% of the time, Pallas kernels for 9%

profile of v4, /device:TPU:1, one launch (start us, length us, event | category | flops | bytes accessed | tf_op | source)
XLA Modules:
  0.0 118.8 jit_solution(2056547552836530853)
XLA Ops:
  0.0 3.2 %collective-permute-start = (bf16[512,1024]{1,0:T(8,128)(2,1)}, bf16[512,1024]{1,0:T(8,128)(2,1)S(1)}, u32[]{:S(2)}, u32[]{:S(2)}) collective-permute-start(bf16[512,1024]{1,0:T(8,128)(2,1)} %rows_ref.1), channel_id=1, source_target_pairs={{0,4},{4,0},{8,12},{12,8},{16,20},{20,16},{24,28},{28,24},{32,36},... | collective-permute-start | bytes 3145736 | tf_op jit(solution)/shard_map/ppermute | solution.py:365
  3.2 0.7 multiply_add_fusion
  3.9 0.0 collective-permute-start.1
  3.9 0.1 pad_add_fusion.where_ref
  4.0 0.0 copy-start
  4.0 1.2 %copy-done = bf16[512,1024]{1,0:T(8,128)(2,1)S(1)} copy-done((bf16[512,1024]{1,0:T(8,128)(2,1)S(1)}, bf16[512,1024]{1,0:T(8,128)(2,1)}, u32[]{:S(2)}) %copy-start) | copy-done | bytes 1048600
  5.2 1.8 %shard_map.37 = (bf16[32,128,128]{2,1,0:T(8,128)(2,1)S(1)}, f32[32,8,128]{2,1,0:T(8,128)S(1)}, s32[1,512]{1,0:T(1,128)S(1)}) custom-call(s32[3]{0:T(128)S(1)} %pad_add_fusion.where_ref, bf16[512,1024]{1,0:T(8,128)(2,1)S(1)} %copy-done, s32[1,512]{1,0:T(1,128)S(1)} %bitcast.15), custom_call_target="tpu_custom_call" | custom-call | flops 1073741824 | bytes 2097152 | tf_op jit(solution)/shard_map/pallas_call | solution.py:118
  7.0 0.0 collective-permute-done.1.label_ref
  7.1 0.0 collective-permute-done.rows_ref
  7.1 1.9 %shard_map.38 = (bf16[32,200,128]{2,1,0:T(8,128)(2,1)S(1)}, bf16[32,64,128]{2,1,0:T(8,128)(2,1)S(1)}) custom-call(s32[3]{0:T(128)S(1)} %pad_add_fusion.where_ref, bf16[512,1024]{1,0:T(8,128)(2,1)S(1)} %collective-permute-done.rows_ref, s32[1,512]{1,0:T(1,128)S(1)} %collective-permute-done.1.label_ref, bf16[32,128,128]{2,1,0:T(8,128)(2,1)S(1)} %get-tuple-element.14.half_ref, ...), custom_call_target="tpu_custom_call" | custom-call | tf_op jit(solution)/shard_map/pallas_call | solution.py:150
  8.9 48.6 %all_to_all.21.first_ref = bf16[32,200,128]{2,1,0:T(8,128)(2,1)S(1)} all-to-all(bf16[32,200,128]{2,1,0:T(8,128)(2,1)S(1)} %get-tuple-element.16), channel_id=1, replica_groups={{0,8,16,24,32,40,48,56,64,72,80,88,96,104,112,120,128,136,144,152,160,1..., dimensions={0} | all-to-all | bytes 3276800 | tf_op jit(solution)/shard_map/all_to_all | solution.py:350
  57.5 1.6 %collective-permute-start.2 = (bf16[32,200,128]{2,1,0:T(8,128)(2,1)S(1)}, bf16[32,200,128]{2,1,0:T(8,128)(2,1)S(1)}, u32[]{:S(2)}, u32[]{:S(2)}) collective-permute-start(bf16[32,200,128]{2,1,0:T(8,128)(2,1)S(1)} %all_to_all.21.first_ref), channel_id=1, source_target_pairs={{0,1},{4,12},{1,2},{5,13},{2,3},{6,14},{3,0},{7,15},{8,9},{12,20},... | collective-permute-start | bytes 4915208 | tf_op jit(solution)/shard_map/ppermute | solution.py:360
  59.1 1.3 %collective-permute-start.3 = (bf16[32,200,128]{2,1,0:T(8,128)(2,1)S(1)}, bf16[32,200,128]{2,1,0:T(8,128)(2,1)S(1)}, u32[]{:S(2)}, u32[]{:S(2)}) collective-permute-start(bf16[32,200,128]{2,1,0:T(8,128)(2,1)S(1)} %all_to_all.21.first_ref), channel_id=1, source_target_pairs={{0,3},{4,28},{1,0},{5,29},{2,1},{6,30},{3,2},{7,31},{8,11},{12,4},... | collective-permute-start | bytes 4915208 | tf_op jit(solution)/shard_map/ppermute | solution.py:360
  60.5 20.8 %all_to_all.22.second_ref = bf16[32,64,128]{2,1,0:T(8,128)(2,1)S(1)} all-to-all(bf16[32,64,128]{2,1,0:T(8,128)(2,1)S(1)} %get-tuple-element.17), channel_id=1, replica_groups={{0,8,16,24,32,40,48,56,64,72,80,88,96,104,112,120,128,136,144,152,160,1..., dimensions={0} | all-to-all | bytes 1048576 | tf_op jit(solution)/shard_map/all_to_all | solution.py:350
  81.3 0.0 collective-permute-start.4
  81.3 2.7 %collective-permute-start.5 = (bf16[32,64,128]{2,1,0:T(8,128)(2,1)S(1)}, bf16[32,64,128]{2,1,0:T(8,128)(2,1)S(1)}, u32[]{:S(2)}, u32[]{:S(2)}) collective-permute-start(bf16[32,64,128]{2,1,0:T(8,128)(2,1)S(1)} %all_to_all.22.second_ref), channel_id=1, source_target_pairs={{0,3},{4,28},{1,0},{5,29},{2,1},{6,30},{3,2},{7,31},{8,11},{12,4},... | collective-permute-start | bytes 1572872 | tf_op jit(solution)/shard_map/ppermute | solution.py:360
  84.0 2.9 %shard_map.39.best_ref = f32[1,1024]{1,0:T(1,128)S(1)} custom-call(bf16[32,200,128]{2,1,0:T(8,128)(2,1)S(1)} %all_to_all.21.first_ref, bf16[32,64,128]{2,1,0:T(8,128)(2,1)S(1)} %all_to_all.22.second_ref), custom_call_target="tpu_custom_call" | custom-call | flops 3221225472 | bytes 4194304 | tf_op jit(solution)/shard_map/pallas_call | solution.py:240
  86.8 0.0 collective-permute-done.2.below_ref
  86.8 0.0 collective-permute-done.3.above_ref
  86.9 5.6 %shard_map.40 = (f32[1024,1024]{1,0:T(8,128)S(1)}, f32[1024,1024]{1,0:T(8,128)S(1)}, f32[1024,1024]{1,0:T(8,128)S(1)}, f32[8,1024]{1,0:T(8,128)S(1)}) custom-call(bf16[32,200,128]{2,1,0:T(8,128)(2,1)S(1)} %all_to_all.21.first_ref, bf16[32,200,128]{2,1,0:T(8,128)(2,1)S(1)} %collective-permute-done.2.below_ref, ...), custom_call_target="tpu_custom_call" | custom-call | flops 6442450944 | bytes 16777216 | tf_op jit(solution)/shard_map/pallas_call | solution.py:214
  92.4 0.0 collective-permute-done.4.below_ref
  92.5 0.0 collective-permute-done.5.above_ref
  92.5 2.5 %shard_map.41 = f32[32,128]{1,0:T(8,128)S(1)} custom-call(f32[1,1024]{1,0:T(1,128)S(1)} %shard_map.39.best_ref, f32[1024,1024]{1,0:T(8,128)S(1)} %get-tuple-element.18.own_below, f32[1024,1024]{1,0:T(8,128)S(1)} %get-tuple-element.19.own_above, f32[1024,1024]{1,0:T(8,128)S(1)} %get-tuple-element.20.below_above, f32[8,1024]{1,0:T(8,128)S(1)} %get-tuple-element.21.inverse_ref, ...), custom_call_target="tpu_custom_call" | custom-call | tf_op jit(solution)/shard_map/pallas_call | solution.py:295
  95.0 14.1 %all_to_all.23 = f32[32,1,128]{2,1,0:T(1,128)S(1)} all-to-all(f32[32,1,128]{2,1,0:T(1,128)S(1)} %bitcast.9), channel_id=1, replica_groups={{0,8,16,24,32,40,48,56,64,72,80,88,96,104,112,120,128,136,144,152,160,1..., dimensions={0} | all-to-all | bytes 32768 | tf_op jit(solution)/shard_map/all_to_all | solution.py:350
  109.1 0.7 collective-permute-start.6
  109.8 4.3 %collective-permute-start.7 = (f32[32,128]{1,0:T(8,128)S(1)}, f32[32,128]{1,0:T(8,128)S(1)}, u32[]{:S(2)}, u32[]{:S(2)}) collective-permute-start(f32[32,128]{1,0:T(8,128)S(1)} %bitcast.11), channel_id=1, source_target_pairs={{0,4},{4,0},{8,12},{12,8},{16,20},{20,16},{24,28},{28,24},{32,36},... | collective-permute-start | bytes 49160 | tf_op jit(solution)/shard_map/ppermute | solution.py:365
  114.1 0.8 collective-permute-start.8
  114.9 0.0 collective-permute-done.6.own_far_ref
  114.9 0.0 collective-permute-done.7.other_ref
  115.0 2.3 %collective-permute-done.8.other_far_ref = f32[32,128]{1,0:T(8,128)S(1)} collective-permute-done((f32[32,128]{1,0:T(8,128)S(1)}, f32[32,128]{1,0:T(8,128)S(1)}, u32[]{:S(2)}, u32[]{:S(2)}) %collective-permute-start.8) | collective-permute-done | bytes 16416 | tf_op jit(solution)/shard_map/ppermute | solution.py:360
  117.3 1.5 %shard_map.42 = f32[1,512]{1,0:T(1,128)} custom-call(s32[3]{0:T(128)S(1)} %pad_add_fusion.where_ref, f32[32,128]{1,0:T(8,128)S(1)} %bitcast.13, f32[32,128]{1,0:T(8,128)S(1)} %collective-permute-done.6.own_far_ref, f32[32,128]{1,0:T(8,128)S(1)} %collective-permute-done.7.other_ref, f32[32,128]{1,0:T(8,128)S(1)} %collective-permute-done.8.other_far_ref, ...), custom_call_target="tpu_custom_call" | custom-call | tf_op jit(solution)/shard_map/pallas_call | solution.py:330
Async XLA Ops:
  0.0 7.1 %collective-permute-start = (bf16[512,1024]{1,0:T(8,128)(2,1)}, bf16[512,1024]{1,0:T(8,128)(2,1)S(1)}, u32[]{:S(2)}, u32[]{:S(2)}) collective-permute-start(bf16[512,1024]{1,0:T(8,128)(2,1)} %rows_ref.1), channel_id=1, source_target_pairs={{0,4},{4,0},{8,12},{12,8},{16,20},{20,16},{24,28},{28,24},{32,36},... | collective-permute-start | bytes 3145736 | tf_op jit(solution)/shard_map/ppermute | solution.py:365
  3.9 3.1 %collective-permute-start.1 = (s32[1,512]{1,0:T(1,128)S(1)}, s32[1,512]{1,0:T(1,128)S(1)}, u32[]{:S(2)}, u32[]{:S(2)}) collective-permute-start(s32[1,512]{1,0:T(1,128)S(1)} %bitcast.14), channel_id=1, source_target_pairs={{0,4},{4,0},{8,12},{12,8},{16,20},{20,16},{24,28},{28,24},{32,36},... | collective-permute-start | bytes 6152 | tf_op jit(solution)/shard_map/ppermute | solution.py:365
  4.0 1.2 %copy-start = (bf16[512,1024]{1,0:T(8,128)(2,1)S(1)}, bf16[512,1024]{1,0:T(8,128)(2,1)}, u32[]{:S(2)}) copy-start(bf16[512,1024]{1,0:T(8,128)(2,1)} %rows_ref.1) | copy-start | bytes 3145732
  57.5 29.3 %collective-permute-start.2 = (bf16[32,200,128]{2,1,0:T(8,128)(2,1)S(1)}, bf16[32,200,128]{2,1,0:T(8,128)(2,1)S(1)}, u32[]{:S(2)}, u32[]{:S(2)}) collective-permute-start(bf16[32,200,128]{2,1,0:T(8,128)(2,1)S(1)} %all_to_all.21.first_ref), channel_id=1, source_target_pairs={{0,1},{4,12},{1,2},{5,13},{2,3},{6,14},{3,0},{7,15},{8,9},{12,20},... | collective-permute-start | bytes 4915208 | tf_op jit(solution)/shard_map/ppermute | solution.py:360
  59.1 27.7 %collective-permute-start.3 = (bf16[32,200,128]{2,1,0:T(8,128)(2,1)S(1)}, bf16[32,200,128]{2,1,0:T(8,128)(2,1)S(1)}, u32[]{:S(2)}, u32[]{:S(2)}) collective-permute-start(bf16[32,200,128]{2,1,0:T(8,128)(2,1)S(1)} %all_to_all.21.first_ref), channel_id=1, source_target_pairs={{0,3},{4,28},{1,0},{5,29},{2,1},{6,30},{3,2},{7,31},{8,11},{12,4},... | collective-permute-start | bytes 4915208 | tf_op jit(solution)/shard_map/ppermute | solution.py:360
  81.3 11.2 %collective-permute-start.4 = (bf16[32,64,128]{2,1,0:T(8,128)(2,1)S(1)}, bf16[32,64,128]{2,1,0:T(8,128)(2,1)S(1)}, u32[]{:S(2)}, u32[]{:S(2)}) collective-permute-start(bf16[32,64,128]{2,1,0:T(8,128)(2,1)S(1)} %all_to_all.22.second_ref), channel_id=1, source_target_pairs={{0,1},{4,12},{1,2},{5,13},{2,3},{6,14},{3,0},{7,15},{8,9},{12,20},... | collective-permute-start | bytes 1572872 | tf_op jit(solution)/shard_map/ppermute | solution.py:360
  81.3 11.2 %collective-permute-start.5 = (bf16[32,64,128]{2,1,0:T(8,128)(2,1)S(1)}, bf16[32,64,128]{2,1,0:T(8,128)(2,1)S(1)}, u32[]{:S(2)}, u32[]{:S(2)}) collective-permute-start(bf16[32,64,128]{2,1,0:T(8,128)(2,1)S(1)} %all_to_all.22.second_ref), channel_id=1, source_target_pairs={{0,3},{4,28},{1,0},{5,29},{2,1},{6,30},{3,2},{7,31},{8,11},{12,4},... | collective-permute-start | bytes 1572872 | tf_op jit(solution)/shard_map/ppermute | solution.py:360
  109.1 5.9 %collective-permute-start.6 = (f32[32,128]{1,0:T(8,128)S(1)}, f32[32,128]{1,0:T(8,128)S(1)}, u32[]{:S(2)}, u32[]{:S(2)}) collective-permute-start(f32[32,128]{1,0:T(8,128)S(1)} %bitcast.10), channel_id=1, source_target_pairs={{0,3},{4,28},{1,0},{5,29},{2,1},{6,30},{3,2},{7,31},{8,11},{12,4},... | collective-permute-start | bytes 49160 | tf_op jit(solution)/shard_map/ppermute | solution.py:360
  109.8 5.1 %collective-permute-start.7 = (f32[32,128]{1,0:T(8,128)S(1)}, f32[32,128]{1,0:T(8,128)S(1)}, u32[]{:S(2)}, u32[]{:S(2)}) collective-permute-start(f32[32,128]{1,0:T(8,128)S(1)} %bitcast.11), channel_id=1, source_target_pairs={{0,4},{4,0},{8,12},{12,8},{16,20},{20,16},{24,28},{28,24},{32,36},... | collective-permute-start | bytes 49160 | tf_op jit(solution)/shard_map/ppermute | solution.py:365
  114.1 3.2 %collective-permute-start.8 = (f32[32,128]{1,0:T(8,128)S(1)}, f32[32,128]{1,0:T(8,128)S(1)}, u32[]{:S(2)}, u32[]{:S(2)}) collective-permute-start(f32[32,128]{1,0:T(8,128)S(1)} %bitcast.12), channel_id=1, source_target_pairs={{0,7},{4,24},{1,4},{5,25},{2,5},{6,26},{3,6},{7,27},{8,15},{12,0},... | collective-permute-start | bytes 49160 | tf_op jit(solution)/shard_map/ppermute | solution.py:360

commit v5 on v4

--- a/solution.py
+++ b/solution.py
@@ -248,11 +248,48 @@
     )(first, second)
 
 
-def tail_kernel(
+def finish(best, inverse):
+    line = jnp.maximum(best * inverse, -1.0)
+    return jnp.concatenate(
+        [
+            jnp.broadcast_to(line[:, t * LANES : (t + 1) * LANES], (PER_TILE, LANES))
+            for t in range(GROUPS // PER_TILE)
+        ],
+        axis=0,
+    )
+
+
+def fold(best, head, keys, queries, scale):
+    for at in CUTS:
+        value = (head[at, :] + nt(keys[at, :], queries[...])) * scale[at]
+        best = jnp.maximum(best, jnp.max(value, axis=0, keepdims=True))
+    return best
+
+
+def far_kernel(below_above, inverse_ref, below_ref, above_ref, out_ref, below, above):
+    unfold(below_ref, below, PARTS[1])
+    unfold(above_ref, above, PARTS[1])
+    best = jnp.full((1, PANEL), NONE, jnp.float32)
+    best = fold(best, below_above, above, below, as_column(inverse_ref[2:3]))
+    out_ref[...] = finish(best, inverse_ref[1:2])
+
+
+def score_far(below_above, inverse, below, above):
+    return pl.pallas_call(
+        far_kernel,
+        out_shape=jax.ShapeDtypeStruct((GROUPS, LANES), jnp.float32),
+        in_specs=[VMEM] * 4,
+        out_specs=VMEM,
+        scratch_shapes=[pltpu.VMEM((PANEL, TAIL), jnp.bfloat16)] * 2,
+        compiler_params=pltpu.CompilerParams(vmem_limit_bytes=16 * 2**20),
+        cost_estimate=pl.CostEstimate(flops=2**29, bytes_accessed=2**23, transcendentals=0),
+    )(below_above, inverse, below, above)
+
+
+def near_kernel(
     best_ref,
     own_below,
     own_above,
-    below_above,
     inverse_ref,
     second_ref,
     below_ref,
@@ -264,54 +301,27 @@
 ):
     for source, target in ((second_ref, own), (below_ref, below), (above_ref, above)):
         unfold(source, target, PARTS[1])
-    below_scale, above_scale = as_column(inverse_ref[1:2]), as_column(inverse_ref[2:3])
-    own_best, below_best = best_ref[...], jnp.full((1, PANEL), NONE, jnp.float32)
-
-    def fold(best, value):
-        return jnp.maximum(best, jnp.max(value, axis=0, keepdims=True))
-
-    for at in CUTS:
-        value = (own_below[at, :] + nt(below[at, :], own[...])) * below_scale[at]
-        own_best = fold(own_best, value)
-        value = (own_above[at, :] + nt(above[at, :], own[...])) * above_scale[at]
-        own_best = fold(own_best, value)
-        value = (below_above[at, :] + nt(above[at, :], below[...])) * above_scale[at]
-        below_best = fold(below_best, value)
-    own_best = jnp.maximum(own_best * inverse_ref[0:1], -1.0)
-    below_best = jnp.maximum(below_best * inverse_ref[1:2], -1.0)
-
-    shape = (PER_TILE, LANES)
-    window, turn = iota(shape, 1) // SLOTS, iota(shape, 0)
-    for t in range(GROUPS // PER_TILE):
-        at = slice(t * LANES, (t + 1) * LANES)
-        near = jnp.broadcast_to(own_best[:, at], shape)
-        far = jnp.broadcast_to(pltpu.roll(below_best[:, at], LANES // 2, 1), shape)
-        out_ref[t * PER_TILE : (t + 1) * PER_TILE, :] = jnp.where(
-            window == turn, near, jnp.where(window == (turn + PER_TILE // 2) % PER_TILE, far, -1.0)
-        )
-
-
-def score_tail(best, head, second, below, above):
-    return pl.pallas_call(
-        tail_kernel,
+    best = fold(best_ref[...], own_below, below, own, as_column(inverse_ref[1:2]))
+    best = fold(best, own_above, above, own, as_column(inverse_ref[2:3]))
+    out_ref[...] = finish(best, inverse_ref[0:1])
+
+
+def score_near(best, own_below, own_above, inverse, second, below, above):
+    return pl.pallas_call(
+        near_kernel,
         out_shape=jax.ShapeDtypeStruct((GROUPS, LANES), jnp.float32),
-        in_specs=[VMEM] * 8,
+        in_specs=[VMEM] * 7,
         out_specs=VMEM,
         scratch_shapes=[pltpu.VMEM((PANEL, TAIL), jnp.bfloat16)] * 3,
-        compiler_params=pltpu.CompilerParams(vmem_limit_bytes=28 * 2**20),
-    )(best, *head, second, below, above)
-
-
-def unpack_kernel(where_ref, own_ref, own_far_ref, other_ref, other_far_ref, slot_ref, out_ref):
+        compiler_params=pltpu.CompilerParams(vmem_limit_bytes=24 * 2**20),
+        cost_estimate=pl.CostEstimate(flops=2**30, bytes_accessed=2**24, transcendentals=0),
+    )(best, own_below, own_above, inverse, second, below, above)
+
+
+def unpack_kernel(where_ref, own_ref, other_ref, slot_ref, out_ref):
     slot = slot_ref[...]
     half = slot // HALF
-    blocks = jnp.concatenate(
-        [
-            jnp.maximum(near[...], pltpu.roll(far[...], LANES // 2, 1))
-            for near, far in ((own_ref, own_far_ref), (other_ref, other_far_ref))
-        ],
-        axis=0,
-    )
+    blocks = jnp.concatenate([own_ref[...], other_ref[...]], axis=0)
     high = narrow(blocks)
     middle = narrow(blocks - high)
     parts = jnp.concatenate([high, middle, blocks - high - middle], axis=1).astype(jnp.bfloat16)
@@ -326,14 +336,14 @@
     )
 
 
-def unpack(where, own, own_far, other, other_far, slot):
+def unpack(where, own, other, slot):
     return pl.pallas_call(
         unpack_kernel,
         out_shape=jax.ShapeDtypeStruct((1, ROWS), jnp.float32),
-        in_specs=[SMEM] + [VMEM] * 5,
+        in_specs=[SMEM] + [VMEM] * 3,
         out_specs=VMEM,
         compiler_params=pltpu.CompilerParams(vmem_limit_bytes=4 * 2**20),
-    )(where, own, own_far, other, other_far, slot).reshape(ROWS)
+    )(where, own, other, slot).reshape(ROWS)
 
 
 def device(z, x, core, y):
@@ -352,11 +362,11 @@
     )
 
 
-def passed_along(array, by, cross=0):
+def passed_along(array, by):
     pairs = []
     for z, x, y in PLACES:
-        pairs.append((device(z, x, 0, y), device(z, x, cross, (y + by) % Y)))
-        pairs.append((device(z, x, 1, y), device(z, (x + by) % X, 1 - cross, y)))
+        pairs.append((device(z, x, 0, y), device(z, x, 0, (y + by) % Y)))
+        pairs.append((device(z, x, 1, y), device(z, (x + by) % X, 1, y)))
     return lax.ppermute(array, AXES, pairs)
 
 
@@ -376,11 +386,12 @@
     below_first, above_first = passed_along(own_first, 1), passed_along(own_first, -1)
     own_second = to_owners(second)
     below_second, above_second = passed_along(own_second, 1), passed_along(own_second, -1)
-    head = score_head(own_first, below_first, above_first)
+    own_below, own_above, below_above, inverse = score_head(own_first, below_first, above_first)
     best = score_own(own_first, own_second)
-    block = to_owners(score_tail(best, head, own_second, below_second, above_second))
-    near, far, across = other_core(block), passed_along(block, -1), passed_along(block, -1, 1)
-    return unpack(where, block, far, near, across, slot)
+    far = passed_along(score_far(below_above, inverse, below_second, above_second), -1)
+    near = score_near(best, own_below, own_above, inverse, own_second, below_second, above_second)
+    block = to_owners(jnp.maximum(near, far))
+    return unpack(where, block, other_core(block), slot)
 
 
 def solution(mesh):

time: 119 us -> 117 us (0.983)
  waiting for transfers between devices: 2.35 us -> 0.86 us
    ppermute x6 -> x5, waiting for transfers between devices: 2.34 us -> 0.01 us  [passed_along(): return lax.ppermute(array, AXES, pairs)]
    ppermute x6 -> x5, starting transfers between devices: 7.17 us -> 6.76 us  [passed_along(): return lax.ppermute(array, AXES, pairs)]
    pallas_call x1 -> x2, Pallas kernels: 2.52 us -> 2.44 us  [the longest x1 1.61 us: score_near(): pl.pallas_call(near_kernel, out_shape=jax.ShapeDtypeStruct((GROUPS, LANES...]
  transfers between devices with their start and end apart: 9 -> 8, of which waited for: 1 -> 1; matrix products, arithmetic and copies ran while one was open for 1% -> 1% of each run, Pallas kernels for 9% -> 10%
where the time goes in v5:
time: 117 us
  blocking collectives  83.4 us (71%)
  Pallas kernels  15.9 us (14%)
  starting transfers between devices  14.3 us (12%)
  local copies, waits for them, and re-layouts  1.23 us (1%)
    all_to_all x3, blocking collectives, to_owners(): lax.all_to_all(array, AXES, split_axis=0, concat_axis=0, tiled=True, axis...  83.4 us
    ppermute x3, starting transfers between devices, other_core(): return lax.ppermute(array, 'shard', [(i, i ^ 1) for i in range(size)])  7.56 us
    ppermute x5, starting transfers between devices, passed_along(): return lax.ppermute(array, AXES, pairs)  6.76 us
    pallas_call x1, Pallas kernels, score_head(): pl.pallas_call(head_kernel, out_shape=(SQUARE, SQUARE, SQUARE, jax.ShapeD...  5.58 us
    pallas_call x1, Pallas kernels, score_own(): pl.pallas_call(own_kernel, out_shape=LINE, in_specs=[VMEM] * 2, out_specs...  2.82 us
  transfers between devices with their start and end apart: 8, of which 1 were waited for; matrix products, arithmetic and copies ran while one was open for 1% of the time, Pallas kernels for 10%

profile of v5, /device:TPU:1, one launch (start us, length us, event | category | flops | bytes accessed | tf_op | source)
XLA Modules:
  0.0 116.6 jit_solution(7083429594025084361)
XLA Ops:
  0.0 3.2 %collective-permute-start = (bf16[512,1024]{1,0:T(8,128)(2,1)}, bf16[512,1024]{1,0:T(8,128)(2,1)S(1)}, u32[]{:S(2)}, u32[]{:S(2)}) collective-permute-start(bf16[512,1024]{1,0:T(8,128)(2,1)} %rows_ref.1), channel_id=1, source_target_pairs={{0,4},{4,0},{8,12},{12,8},{16,20},{20,16},{24,28},{28,24},{32,36},... | collective-permute-start | bytes 3145736 | tf_op jit(solution)/shard_map/ppermute | solution.py:375
  3.2 0.7 multiply_add_fusion
  3.9 0.0 collective-permute-start.1
  3.9 0.1 pad_add_fusion.where_ref
  4.0 0.0 copy-start
  4.0 1.2 %copy-done = bf16[512,1024]{1,0:T(8,128)(2,1)S(1)} copy-done((bf16[512,1024]{1,0:T(8,128)(2,1)S(1)}, bf16[512,1024]{1,0:T(8,128)(2,1)}, u32[]{:S(2)}) %copy-start) | copy-done | bytes 1048600
  5.2 1.8 %shard_map.37 = (bf16[32,128,128]{2,1,0:T(8,128)(2,1)S(1)}, f32[32,8,128]{2,1,0:T(8,128)S(1)}, s32[1,512]{1,0:T(1,128)S(1)}) custom-call(s32[3]{0:T(128)S(1)} %pad_add_fusion.where_ref, bf16[512,1024]{1,0:T(8,128)(2,1)S(1)} %copy-done, s32[1,512]{1,0:T(1,128)S(1)} %bitcast.12), custom_call_target="tpu_custom_call" | custom-call | flops 1073741824 | bytes 2097152 | tf_op jit(solution)/shard_map/pallas_call | solution.py:118
  7.0 0.0 collective-permute-done.1.label_ref
  7.1 0.0 collective-permute-done.rows_ref
  7.1 1.9 %shard_map.38 = (bf16[32,200,128]{2,1,0:T(8,128)(2,1)S(1)}, bf16[32,64,128]{2,1,0:T(8,128)(2,1)S(1)}) custom-call(s32[3]{0:T(128)S(1)} %pad_add_fusion.where_ref, bf16[512,1024]{1,0:T(8,128)(2,1)S(1)} %collective-permute-done.rows_ref, s32[1,512]{1,0:T(1,128)S(1)} %collective-permute-done.1.label_ref, bf16[32,128,128]{2,1,0:T(8,128)(2,1)S(1)} %get-tuple-element.14.half_ref, ...), custom_call_target="tpu_custom_call" | custom-call | tf_op jit(solution)/shard_map/pallas_call | solution.py:150
  8.9 48.6 %all_to_all.21.first_ref = bf16[32,200,128]{2,1,0:T(8,128)(2,1)S(1)} all-to-all(bf16[32,200,128]{2,1,0:T(8,128)(2,1)S(1)} %get-tuple-element.16), channel_id=1, replica_groups={{0,8,16,24,32,40,48,56,64,72,80,88,96,104,112,120,128,136,144,152,160,1..., dimensions={0} | all-to-all | bytes 3276800 | tf_op jit(solution)/shard_map/all_to_all | solution.py:360
  57.5 1.6 %collective-permute-start.2 = (bf16[32,200,128]{2,1,0:T(8,128)(2,1)S(1)}, bf16[32,200,128]{2,1,0:T(8,128)(2,1)S(1)}, u32[]{:S(2)}, u32[]{:S(2)}) collective-permute-start(bf16[32,200,128]{2,1,0:T(8,128)(2,1)S(1)} %all_to_all.21.first_ref), channel_id=1, source_target_pairs={{0,1},{4,12},{1,2},{5,13},{2,3},{6,14},{3,0},{7,15},{8,9},{12,20},... | collective-permute-start | bytes 4915208 | tf_op jit(solution)/shard_map/ppermute | solution.py:370
  59.1 1.3 %collective-permute-start.3 = (bf16[32,200,128]{2,1,0:T(8,128)(2,1)S(1)}, bf16[32,200,128]{2,1,0:T(8,128)(2,1)S(1)}, u32[]{:S(2)}, u32[]{:S(2)}) collective-permute-start(bf16[32,200,128]{2,1,0:T(8,128)(2,1)S(1)} %all_to_all.21.first_ref), channel_id=1, source_target_pairs={{0,3},{4,28},{1,0},{5,29},{2,1},{6,30},{3,2},{7,31},{8,11},{12,4},... | collective-permute-start | bytes 4915208 | tf_op jit(solution)/shard_map/ppermute | solution.py:370
  60.5 20.8 %all_to_all.22.second_ref = bf16[32,64,128]{2,1,0:T(8,128)(2,1)S(1)} all-to-all(bf16[32,64,128]{2,1,0:T(8,128)(2,1)S(1)} %get-tuple-element.17), channel_id=1, replica_groups={{0,8,16,24,32,40,48,56,64,72,80,88,96,104,112,120,128,136,144,152,160,1..., dimensions={0} | all-to-all | bytes 1048576 | tf_op jit(solution)/shard_map/all_to_all | solution.py:360
  81.3 0.0 collective-permute-start.4
  81.3 2.7 %collective-permute-start.5 = (bf16[32,64,128]{2,1,0:T(8,128)(2,1)S(1)}, bf16[32,64,128]{2,1,0:T(8,128)(2,1)S(1)}, u32[]{:S(2)}, u32[]{:S(2)}) collective-permute-start(bf16[32,64,128]{2,1,0:T(8,128)(2,1)S(1)} %all_to_all.22.second_ref), channel_id=1, source_target_pairs={{0,3},{4,28},{1,0},{5,29},{2,1},{6,30},{3,2},{7,31},{8,11},{12,4},... | collective-permute-start | bytes 1572872 | tf_op jit(solution)/shard_map/ppermute | solution.py:370
  84.0 2.8 %shard_map.39.best_ref = f32[1,1024]{1,0:T(1,128)S(1)} custom-call(bf16[32,200,128]{2,1,0:T(8,128)(2,1)S(1)} %all_to_all.21.first_ref, bf16[32,64,128]{2,1,0:T(8,128)(2,1)S(1)} %all_to_all.22.second_ref), custom_call_target="tpu_custom_call" | custom-call | flops 3221225472 | bytes 4194304 | tf_op jit(solution)/shard_map/pallas_call | solution.py:240
  86.8 0.0 collective-permute-done.2.below_ref
  86.8 0.0 collective-permute-done.3.above_ref
  86.8 5.6 %shard_map.40 = (f32[1024,1024]{1,0:T(8,128)S(1)}, f32[1024,1024]{1,0:T(8,128)S(1)}, f32[1024,1024]{1,0:T(8,128)S(1)}, f32[8,1024]{1,0:T(8,128)S(1)}) custom-call(bf16[32,200,128]{2,1,0:T(8,128)(2,1)S(1)} %all_to_all.21.first_ref, bf16[32,200,128]{2,1,0:T(8,128)(2,1)S(1)} %collective-permute-done.2.below_ref, ...), custom_call_target="tpu_custom_call" | custom-call | flops 6442450944 | bytes 16777216 | tf_op jit(solution)/shard_map/pallas_call | solution.py:214
  92.4 0.0 collective-permute-done.4.below_ref
  92.4 0.0 collective-permute-done.5.above_ref
  92.4 0.8 shard_map.42
  93.3 1.2 collective-permute-start.6
  94.4 1.6 %shard_map.41 = f32[32,128]{1,0:T(8,128)S(1)} custom-call(f32[1,1024]{1,0:T(1,128)S(1)} %shard_map.39.best_ref, f32[1024,1024]{1,0:T(8,128)S(1)} %get-tuple-element.18.own_below, f32[1024,1024]{1,0:T(8,128)S(1)} %get-tuple-element.19.own_above, f32[8,1024]{1,0:T(8,128)S(1)} %get-tuple-element.20.inverse_ref, bf16[32,64,128]{2,1,0:T(8,128)(2,1)S(1)} %all_to_all.22.second_ref, ...), custom_call_target="tpu_custom_call" | custom-call | flops 1073741824 | bytes 16777216 | tf_op jit(solution)/shard_map/pallas_call | solution.py:310
  96.0 0.0 collective-permute-done.6
  96.1 14.0 %all_to_all.23 = f32[32,1,128]{2,1,0:T(1,128)S(1)} all-to-all(f32[32,1,128]{2,1,0:T(1,128)S(1)} %bitcast.13), channel_id=1, replica_groups={{0,8,16,24,32,40,48,56,64,72,80,88,96,104,112,120,128,136,144,152,160,1..., dimensions={0} | all-to-all | bytes 32768 | tf_op jit(solution)/shard_map/all_to_all | solution.py:360
  110.0 4.3 %collective-permute-start.7 = (f32[32,128]{1,0:T(8,128)S(1)}, f32[32,128]{1,0:T(8,128)S(1)}, u32[]{:S(2)}, u32[]{:S(2)}) collective-permute-start(f32[32,128]{1,0:T(8,128)S(1)} %bitcast.9), channel_id=1, source_target_pairs={{0,4},{4,0},{8,12},{12,8},{16,20},{20,16},{24,28},{28,24},{32,36},... | collective-permute-start | bytes 49160 | tf_op jit(solution)/shard_map/ppermute | solution.py:375
  114.3 0.8 collective-permute-done.7.other_ref
  115.2 1.4 %shard_map.43 = f32[1,512]{1,0:T(1,128)} custom-call(s32[3]{0:T(128)S(1)} %pad_add_fusion.where_ref, f32[32,128]{1,0:T(8,128)S(1)} %bitcast.10, f32[32,128]{1,0:T(8,128)S(1)} %collective-permute-done.7.other_ref, s32[1,512]{1,0:T(1,128)S(1)} %get-tuple-element.22.slot_ref), custom_call_target="tpu_custom_call" | custom-call | tf_op jit(solution)/shard_map/pallas_call | solution.py:340
  (1 shorter events, 0.0 us)
Async XLA Ops:
  0.0 7.1 %collective-permute-start = (bf16[512,1024]{1,0:T(8,128)(2,1)}, bf16[512,1024]{1,0:T(8,128)(2,1)S(1)}, u32[]{:S(2)}, u32[]{:S(2)}) collective-permute-start(bf16[512,1024]{1,0:T(8,128)(2,1)} %rows_ref.1), channel_id=1, source_target_pairs={{0,4},{4,0},{8,12},{12,8},{16,20},{20,16},{24,28},{28,24},{32,36},... | collective-permute-start | bytes 3145736 | tf_op jit(solution)/shard_map/ppermute | solution.py:375
  3.9 3.1 %collective-permute-start.1 = (s32[1,512]{1,0:T(1,128)S(1)}, s32[1,512]{1,0:T(1,128)S(1)}, u32[]{:S(2)}, u32[]{:S(2)}) collective-permute-start(s32[1,512]{1,0:T(1,128)S(1)} %bitcast.11), channel_id=1, source_target_pairs={{0,4},{4,0},{8,12},{12,8},{16,20},{20,16},{24,28},{28,24},{32,36},... | collective-permute-start | bytes 6152 | tf_op jit(solution)/shard_map/ppermute | solution.py:375
  4.0 1.2 %copy-start = (bf16[512,1024]{1,0:T(8,128)(2,1)S(1)}, bf16[512,1024]{1,0:T(8,128)(2,1)}, u32[]{:S(2)}) copy-start(bf16[512,1024]{1,0:T(8,128)(2,1)} %rows_ref.1) | copy-start | bytes 3145732
  57.5 29.3 %collective-permute-start.2 = (bf16[32,200,128]{2,1,0:T(8,128)(2,1)S(1)}, bf16[32,200,128]{2,1,0:T(8,128)(2,1)S(1)}, u32[]{:S(2)}, u32[]{:S(2)}) collective-permute-start(bf16[32,200,128]{2,1,0:T(8,128)(2,1)S(1)} %all_to_all.21.first_ref), channel_id=1, source_target_pairs={{0,1},{4,12},{1,2},{5,13},{2,3},{6,14},{3,0},{7,15},{8,9},{12,20},... | collective-permute-start | bytes 4915208 | tf_op jit(solution)/shard_map/ppermute | solution.py:370
  59.1 27.7 %collective-permute-start.3 = (bf16[32,200,128]{2,1,0:T(8,128)(2,1)S(1)}, bf16[32,200,128]{2,1,0:T(8,128)(2,1)S(1)}, u32[]{:S(2)}, u32[]{:S(2)}) collective-permute-start(bf16[32,200,128]{2,1,0:T(8,128)(2,1)S(1)} %all_to_all.21.first_ref), channel_id=1, source_target_pairs={{0,3},{4,28},{1,0},{5,29},{2,1},{6,30},{3,2},{7,31},{8,11},{12,4},... | collective-permute-start | bytes 4915208 | tf_op jit(solution)/shard_map/ppermute | solution.py:370
  81.3 11.1 %collective-permute-start.4 = (bf16[32,64,128]{2,1,0:T(8,128)(2,1)S(1)}, bf16[32,64,128]{2,1,0:T(8,128)(2,1)S(1)}, u32[]{:S(2)}, u32[]{:S(2)}) collective-permute-start(bf16[32,64,128]{2,1,0:T(8,128)(2,1)S(1)} %all_to_all.22.second_ref), channel_id=1, source_target_pairs={{0,1},{4,12},{1,2},{5,13},{2,3},{6,14},{3,0},{7,15},{8,9},{12,20},... | collective-permute-start | bytes 1572872 | tf_op jit(solution)/shard_map/ppermute | solution.py:370
  81.3 11.1 %collective-permute-start.5 = (bf16[32,64,128]{2,1,0:T(8,128)(2,1)S(1)}, bf16[32,64,128]{2,1,0:T(8,128)(2,1)S(1)}, u32[]{:S(2)}, u32[]{:S(2)}) collective-permute-start(bf16[32,64,128]{2,1,0:T(8,128)(2,1)S(1)} %all_to_all.22.second_ref), channel_id=1, source_target_pairs={{0,3},{4,28},{1,0},{5,29},{2,1},{6,30},{3,2},{7,31},{8,11},{12,4},... | collective-permute-start | bytes 1572872 | tf_op jit(solution)/shard_map/ppermute | solution.py:370
  93.3 2.8 %collective-permute-start.6 = (f32[32,128]{1,0:T(8,128)S(1)}, f32[32,128]{1,0:T(8,128)S(1)}, u32[]{:S(2)}, u32[]{:S(2)}) collective-permute-start(f32[32,128]{1,0:T(8,128)S(1)} %shard_map.42), channel_id=1, source_target_pairs={{0,3},{4,28},{1,0},{5,29},{2,1},{6,30},{3,2},{7,31},{8,11},{12,4},... | collective-permute-start | bytes 49160 | tf_op jit(solution)/shard_map/ppermute | solution.py:370
  110.0 5.2 %collective-permute-start.7 = (f32[32,128]{1,0:T(8,128)S(1)}, f32[32,128]{1,0:T(8,128)S(1)}, u32[]{:S(2)}, u32[]{:S(2)}) collective-permute-start(f32[32,128]{1,0:T(8,128)S(1)} %bitcast.9), channel_id=1, source_target_pairs={{0,4},{4,0},{8,12},{12,8},{16,20},{20,16},{24,28},{28,24},{32,36},... | collective-permute-start | bytes 49160 | tf_op jit(solution)/shard_map/ppermute | solution.py:375

commit v6 on v5

--- a/solution.py
+++ b/solution.py
@@ -27,7 +27,6 @@
 Z, X, Y = 8, 4, 4
 AXES = ("shard", "clus")
 VMEM = pl.BlockSpec(memory_space=pltpu.VMEM)
-SMEM = pl.BlockSpec(memory_space=pltpu.SMEM)
 LINE = jax.ShapeDtypeStruct((1, PANEL), jnp.float32)
 SQUARE = jax.ShapeDtypeStruct((PANEL, PANEL), jnp.float32)
 
@@ -68,7 +67,14 @@
     return value.astype(jnp.bfloat16).astype(jnp.float32)
 
 
-def pack_half(half, core, place, rows, label, put):
+def whereabouts():
+    shard, y = lax.axis_index("shard"), lax.axis_index("clus")
+    core, x = shard % 2, shard // 2 % X
+    return core, jnp.where(core == 0, x, y), jnp.where(core == 0, y, x)
+
+
+def pack_half(half, rows, label, put):
+    core, place, _ = whereabouts()
     cluster, arrival = label // SPAN, label % SPAN
     owner = cluster % OWNERS
     earlier = (iota((ROWS, ROWS), 0) < iota((ROWS, ROWS), 1)).astype(jnp.bfloat16)
@@ -90,31 +96,33 @@
     begin = place * SLOTS + half * CAPACITY
     window = (lane >= begin) & (lane < begin + CAPACITY)
     labels = []
-    step = LANES // CAPACITY
+    step = GROUPS
     for g in range(0, GROUPS, step):
-        pick = (iota((LANES, ROWS), 0) + g * CAPACITY == jnp.where(mine, slot, -1)).astype(jnp.bfloat16)
+        count = step * CAPACITY
+        pick = (iota((count, ROWS), 0) + g * CAPACITY == jnp.where(mine, slot, -1)).astype(jnp.bfloat16)
         moved = jnp.dot(pick, rows[...], preferred_element_type=jnp.float32).astype(jnp.bfloat16)
         moved = moved.reshape(step, CAPACITY, D)
         for k in range(TILES):
             put(g, step, k, moved[:, :, k * LANES : (k + 1) * LANES])
         line = nt(digits, pick)
-        for j in range(step):
-            turn = (begin + LANES - j * CAPACITY) % LANES
-            labels.append(jnp.where(window, pltpu.roll(line, turn, 1), 0.0))
+        for j in range(0, count, CAPACITY):
+            tile = line[:, j // LANES * LANES : (j // LANES + 1) * LANES]
+            turn = (begin + LANES - j % LANES) % LANES
+            labels.append(jnp.where(window, pltpu.roll(tile, turn, 1), 0.0))
     return jnp.where(mine, slot, slot + HALF), labels
 
 
-def pack_own_kernel(where_ref, rows_ref, label_ref, half_ref, labels_ref, slot_ref):
+def pack_own_kernel(rows_ref, label_ref, half_ref, labels_ref, slot_ref):
     def put(g, step, k, value):
         half_ref[g : g + step, k * CAPACITY : (k + 1) * CAPACITY, :] = value
 
-    slot, labels = pack_half(0, where_ref[0], where_ref[1], rows_ref, label_ref[...], put)
+    slot, labels = pack_half(0, rows_ref, label_ref[...], put)
     slot_ref[...] = slot
     for g in range(GROUPS):
         labels_ref[g] = labels[g]
 
 
-def pack_own(where, rows, label):
+def pack_own(rows, label):
     return pl.pallas_call(
         pack_own_kernel,
         out_shape=(
@@ -122,14 +130,14 @@
             jax.ShapeDtypeStruct((GROUPS, 8, LANES), jnp.float32),
             jax.ShapeDtypeStruct((1, ROWS), jnp.int32),
         ),
-        in_specs=[SMEM] + [VMEM] * 2,
+        in_specs=[VMEM] * 2,
         out_specs=(VMEM,) * 3,
         compiler_params=pltpu.CompilerParams(vmem_limit_bytes=16 * 2**20),
         cost_estimate=pl.CostEstimate(flops=2**30, bytes_accessed=2**21, transcendentals=0),
-    )(where, rows, label)
-
-
-def pack_other_kernel(where_ref, rows_ref, label_ref, half_ref, labels_ref, first_ref, second_ref):
+    )(rows, label)
+
+
+def pack_other_kernel(rows_ref, label_ref, half_ref, labels_ref, first_ref, second_ref):
     def place(k, half):
         out_ref, tile = (first_ref, k) if k < PARTS[0] else (second_ref, k - PARTS[0])
         return out_ref, tile * SLOTS + half * CAPACITY
@@ -141,21 +149,21 @@
     for k in range(TILES):
         out_ref, at = place(k, 0)
         out_ref[:, at : at + CAPACITY, :] = half_ref[:, k * CAPACITY : (k + 1) * CAPACITY, :]
-    _, labels = pack_half(1, where_ref[0], where_ref[1], rows_ref, label_ref[...], put)
+    _, labels = pack_half(1, rows_ref, label_ref[...], put)
     for g in range(GROUPS):
         first_ref[g, LABELS:, :] = (labels[g] + labels_ref[g]).astype(jnp.bfloat16)
 
 
-def pack_other(where, rows, label, half, labels):
+def pack_other(rows, label, half, labels):
     return pl.pallas_call(
         pack_other_kernel,
         out_shape=tuple(
             jax.ShapeDtypeStruct((GROUPS, height, LANES), jnp.bfloat16) for height in HEIGHTS
         ),
-        in_specs=[SMEM] + [VMEM] * 4,
+        in_specs=[VMEM] * 4,
         out_specs=(VMEM,) * 2,
         compiler_params=pltpu.CompilerParams(vmem_limit_bytes=16 * 2**20),
-    )(where, rows, label, half, labels)
+    )(rows, label, half, labels)
 
 
 def info(ref):
@@ -183,7 +191,7 @@
         ].reshape(PANEL, LANES)
 
 
-WIDTH = 256
+WIDTH = 512
 CUTS = [slice(start, start + WIDTH) for start in range(0, PANEL, WIDTH)]
 
 
@@ -318,7 +326,7 @@
     )(best, own_below, own_above, inverse, second, below, above)
 
 
-def unpack_kernel(where_ref, own_ref, other_ref, slot_ref, out_ref):
+def unpack_kernel(own_ref, other_ref, slot_ref, out_ref):
     slot = slot_ref[...]
     half = slot // HALF
     blocks = jnp.concatenate([own_ref[...], other_ref[...]], axis=0)
@@ -329,21 +337,22 @@
     every = lax.dot_general(
         parts, member, (((0,), (0,)), ((), ())), preferred_element_type=jnp.float32
     )
-    place = jnp.where(half == 0, where_ref[1], where_ref[2])
+    _, place, other_place = whereabouts()
+    place = jnp.where(half == 0, place, other_place)
     lane = place * SLOTS + half * CAPACITY + slot % CAPACITY
     out_ref[...] = jnp.sum(
         jnp.where(iota((3 * LANES, ROWS), 0) % LANES == lane, every, 0.0), axis=0, keepdims=True
     )
 
 
-def unpack(where, own, other, slot):
+def unpack(own, other, slot):
     return pl.pallas_call(
         unpack_kernel,
         out_shape=jax.ShapeDtypeStruct((1, ROWS), jnp.float32),
-        in_specs=[SMEM] + [VMEM] * 3,
+        in_specs=[VMEM] * 3,
         out_specs=VMEM,
         compiler_params=pltpu.CompilerParams(vmem_limit_bytes=4 * 2**20),
-    )(where, own, other, slot).reshape(ROWS)
+    )(own, other, slot).reshape(ROWS)
 
 
 def device(z, x, core, y):
@@ -377,11 +386,8 @@
 
 def per_device(embeddings, cluster, arrival):
     label = (cluster * SPAN + arrival).reshape(1, ROWS)
-    shard, y = lax.axis_index("shard"), lax.axis_index("clus")
-    core, x = shard % 2, shard // 2 % X
-    where = jnp.stack([core, jnp.where(core == 0, x, y), jnp.where(core == 0, y, x)])
-    half, labels, slot = pack_own(where, embeddings, label)
-    first, second = pack_other(where, other_core(embeddings), other_core(label), half, labels)
+    half, labels, slot = pack_own(embeddings, label)
+    first, second = pack_other(other_core(embeddings), other_core(label), half, labels)
     own_first = to_owners(first)
     below_first, above_first = passed_along(own_first, 1), passed_along(own_first, -1)
     own_second = to_owners(second)
@@ -391,7 +397,7 @@
     far = passed_along(score_far(below_above, inverse, below_second, above_second), -1)
     near = score_near(best, own_below, own_above, inverse, own_second, below_second, above_second)
     block = to_owners(jnp.maximum(near, far))
-    return unpack(where, block, other_core(block), slot)
+    return unpack(block, other_core(block), slot)
 
 
 def solution(mesh):

time: 117 us -> 115 us (0.983)
  Pallas kernels: 15.9 us -> 13.7 us
  transfers between devices with their start and end apart: 8 -> 8, of which waited for: 1 -> 1; matrix products, arithmetic and copies ran while one was open for 1% -> 1% of each run, Pallas kernels for 10% -> 9%
where the time goes in v6:
time: 115 us; the launch traced here: 114 us
  blocking collectives  83.2 us (72%)
  starting transfers between devices  14.5 us (13%)
  Pallas kernels  13.7 us (12%)
  local copies, waits for them, and re-layouts  1.22 us (1%)
    all_to_all x3, blocking collectives, to_owners(): lax.all_to_all(array, AXES, split_axis=0, concat_axis=0, tiled=True, axis...  83.2 us
    ppermute x3, starting transfers between devices, other_core(): return lax.ppermute(array, 'shard', [(i, i ^ 1) for i in range(size)])  7.55 us
    ppermute x5, starting transfers between devices, passed_along(): return lax.ppermute(array, AXES, pairs)  6.99 us
    pallas_call x1, Pallas kernels, score_head(): pl.pallas_call(head_kernel, out_shape=(SQUARE, SQUARE, SQUARE, jax.ShapeD...  5.51 us
    pallas_call x1, Pallas kernels, score_own(): pl.pallas_call(own_kernel, out_shape=LINE, in_specs=[VMEM] * 2, out_specs...  2.67 us
  transfers between devices with their start and end apart: 8, of which 1 were waited for; matrix products, arithmetic and copies ran while one was open for 1% of the time, Pallas kernels for 9%

profile of v6, /device:TPU:1, one launch (start us, length us, event | category | flops | bytes accessed | tf_op | source)
XLA Modules:
  0.0 114.4 jit_solution(4986914054501167270)
XLA Ops:
  0.0 3.2 %collective-permute-start = (bf16[512,1024]{1,0:T(8,128)(2,1)}, bf16[512,1024]{1,0:T(8,128)(2,1)S(1)}, u32[]{:S(2)}, u32[]{:S(2)}) collective-permute-start(bf16[512,1024]{1,0:T(8,128)(2,1)} %rows_ref.1), channel_id=1, source_target_pairs={{0,4},{4,0},{8,12},{12,8},{16,20},{20,16},{24,28},{28,24},{32,36},... | collective-permute-start | bytes 3145736 | tf_op jit(solution)/shard_map/ppermute | solution.py:384
  3.2 0.7 multiply_add_fusion
  3.9 0.0 collective-permute-start.1
  3.9 0.0 copy-start
  3.9 1.2 %copy-done = bf16[512,1024]{1,0:T(8,128)(2,1)S(1)} copy-done((bf16[512,1024]{1,0:T(8,128)(2,1)S(1)}, bf16[512,1024]{1,0:T(8,128)(2,1)}, u32[]{:S(2)}) %copy-start) | copy-done | bytes 1048600
  5.2 1.1 shard_map.37
  6.3 0.0 collective-permute-done.1.label_ref
  6.3 0.0 collective-permute-done.rows_ref
  6.3 1.2 %shard_map.38 = (bf16[32,200,128]{2,1,0:T(8,128)(2,1)S(1)}, bf16[32,64,128]{2,1,0:T(8,128)(2,1)S(1)}) custom-call(bf16[512,1024]{1,0:T(8,128)(2,1)S(1)} %collective-permute-done.rows_ref, s32[1,512]{1,0:T(1,128)S(1)} %collective-permute-done.1.label_ref, bf16[32,128,128]{2,1,0:T(8,128)(2,1)S(1)} %get-tuple-element.14.half_ref, ...), custom_call_target="tpu_custom_call" | custom-call | tf_op jit(solution)/shard_map/pallas_call | solution.py:158
  7.5 48.6 %all_to_all.21.first_ref = bf16[32,200,128]{2,1,0:T(8,128)(2,1)S(1)} all-to-all(bf16[32,200,128]{2,1,0:T(8,128)(2,1)S(1)} %get-tuple-element.16), channel_id=1, replica_groups={{0,8,16,24,32,40,48,56,64,72,80,88,96,104,112,120,128,136,144,152,160,1..., dimensions={0} | all-to-all | bytes 3276800 | tf_op jit(solution)/shard_map/all_to_all | solution.py:369
  56.0 1.6 %collective-permute-start.2 = (bf16[32,200,128]{2,1,0:T(8,128)(2,1)S(1)}, bf16[32,200,128]{2,1,0:T(8,128)(2,1)S(1)}, u32[]{:S(2)}, u32[]{:S(2)}) collective-permute-start(bf16[32,200,128]{2,1,0:T(8,128)(2,1)S(1)} %all_to_all.21.first_ref), channel_id=1, source_target_pairs={{0,1},{4,12},{1,2},{5,13},{2,3},{6,14},{3,0},{7,15},{8,9},{12,20},... | collective-permute-start | bytes 4915208 | tf_op jit(solution)/shard_map/ppermute | solution.py:379
  57.6 1.4 %collective-permute-start.3 = (bf16[32,200,128]{2,1,0:T(8,128)(2,1)S(1)}, bf16[32,200,128]{2,1,0:T(8,128)(2,1)S(1)}, u32[]{:S(2)}, u32[]{:S(2)}) collective-permute-start(bf16[32,200,128]{2,1,0:T(8,128)(2,1)S(1)} %all_to_all.21.first_ref), channel_id=1, source_target_pairs={{0,3},{4,28},{1,0},{5,29},{2,1},{6,30},{3,2},{7,31},{8,11},{12,4},... | collective-permute-start | bytes 4915208 | tf_op jit(solution)/shard_map/ppermute | solution.py:379
  59.0 20.8 %all_to_all.22.second_ref = bf16[32,64,128]{2,1,0:T(8,128)(2,1)S(1)} all-to-all(bf16[32,64,128]{2,1,0:T(8,128)(2,1)S(1)} %get-tuple-element.17), channel_id=1, replica_groups={{0,8,16,24,32,40,48,56,64,72,80,88,96,104,112,120,128,136,144,152,160,1..., dimensions={0} | all-to-all | bytes 1048576 | tf_op jit(solution)/shard_map/all_to_all | solution.py:369
  79.8 0.0 collective-permute-start.4
  79.8 2.7 %collective-permute-start.5 = (bf16[32,64,128]{2,1,0:T(8,128)(2,1)S(1)}, bf16[32,64,128]{2,1,0:T(8,128)(2,1)S(1)}, u32[]{:S(2)}, u32[]{:S(2)}) collective-permute-start(bf16[32,64,128]{2,1,0:T(8,128)(2,1)S(1)} %all_to_all.22.second_ref), channel_id=1, source_target_pairs={{0,3},{4,28},{1,0},{5,29},{2,1},{6,30},{3,2},{7,31},{8,11},{12,4},... | collective-permute-start | bytes 1572872 | tf_op jit(solution)/shard_map/ppermute | solution.py:379
  82.5 2.7 %shard_map.39.best_ref = f32[1,1024]{1,0:T(1,128)S(1)} custom-call(bf16[32,200,128]{2,1,0:T(8,128)(2,1)S(1)} %all_to_all.21.first_ref, bf16[32,64,128]{2,1,0:T(8,128)(2,1)S(1)} %all_to_all.22.second_ref), custom_call_target="tpu_custom_call" | custom-call | flops 3221225472 | bytes 4194304 | tf_op jit(solution)/shard_map/pallas_call | solution.py:248
  85.2 0.0 collective-permute-done.2.below_ref
  85.2 0.0 collective-permute-done.3.above_ref
  85.2 5.5 %shard_map.40 = (f32[1024,1024]{1,0:T(8,128)S(1)}, f32[1024,1024]{1,0:T(8,128)S(1)}, f32[1024,1024]{1,0:T(8,128)S(1)}, f32[8,1024]{1,0:T(8,128)S(1)}) custom-call(bf16[32,200,128]{2,1,0:T(8,128)(2,1)S(1)} %all_to_all.21.first_ref, bf16[32,200,128]{2,1,0:T(8,128)(2,1)S(1)} %collective-permute-done.2.below_ref, ...), custom_call_target="tpu_custom_call" | custom-call | flops 6442450944 | bytes 16777216 | tf_op jit(solution)/shard_map/pallas_call | solution.py:222
  90.7 0.0 collective-permute-done.4.below_ref
  90.7 0.0 collective-permute-done.5.above_ref
  90.7 0.8 shard_map.42
  91.6 1.4 %collective-permute-start.6 = (f32[32,128]{1,0:T(8,128)S(1)}, f32[32,128]{1,0:T(8,128)S(1)}, u32[]{:S(2)}, u32[]{:S(2)}) collective-permute-start(f32[32,128]{1,0:T(8,128)S(1)} %shard_map.42), channel_id=1, source_target_pairs={{0,3},{4,28},{1,0},{5,29},{2,1},{6,30},{3,2},{7,31},{8,11},{12,4},... | collective-permute-start | bytes 49160 | tf_op jit(solution)/shard_map/ppermute | solution.py:379
  92.9 1.6 %shard_map.41 = f32[32,128]{1,0:T(8,128)S(1)} custom-call(f32[1,1024]{1,0:T(1,128)S(1)} %shard_map.39.best_ref, f32[1024,1024]{1,0:T(8,128)S(1)} %get-tuple-element.18.own_below, f32[1024,1024]{1,0:T(8,128)S(1)} %get-tuple-element.19.own_above, f32[8,1024]{1,0:T(8,128)S(1)} %get-tuple-element.20.inverse_ref, bf16[32,64,128]{2,1,0:T(8,128)(2,1)S(1)} %all_to_all.22.second_ref, ...), custom_call_target="tpu_custom_call" | custom-call | flops 1073741824 | bytes 16777216 | tf_op jit(solution)/shard_map/pallas_call | solution.py:318
  94.5 0.0 collective-permute-done.6
  94.5 13.8 %all_to_all.23 = f32[32,1,128]{2,1,0:T(1,128)S(1)} all-to-all(f32[32,1,128]{2,1,0:T(1,128)S(1)} %bitcast.10), channel_id=1, replica_groups={{0,8,16,24,32,40,48,56,64,72,80,88,96,104,112,120,128,136,144,152,160,1..., dimensions={0} | all-to-all | bytes 32768 | tf_op jit(solution)/shard_map/all_to_all | solution.py:369
  108.3 4.3 %collective-permute-start.7 = (f32[32,128]{1,0:T(8,128)S(1)}, f32[32,128]{1,0:T(8,128)S(1)}, u32[]{:S(2)}, u32[]{:S(2)}) collective-permute-start(f32[32,128]{1,0:T(8,128)S(1)} %bitcast.6), channel_id=1, source_target_pairs={{0,4},{4,0},{8,12},{12,8},{16,20},{20,16},{24,28},{28,24},{32,36},... | collective-permute-start | bytes 49160 | tf_op jit(solution)/shard_map/ppermute | solution.py:384
  112.7 0.8 collective-permute-done.7.other_ref
  113.5 0.9 shard_map.43
  (1 shorter events, 0.0 us)
Async XLA Ops:
  0.0 6.3 %collective-permute-start = (bf16[512,1024]{1,0:T(8,128)(2,1)}, bf16[512,1024]{1,0:T(8,128)(2,1)S(1)}, u32[]{:S(2)}, u32[]{:S(2)}) collective-permute-start(bf16[512,1024]{1,0:T(8,128)(2,1)} %rows_ref.1), channel_id=1, source_target_pairs={{0,4},{4,0},{8,12},{12,8},{16,20},{20,16},{24,28},{28,24},{32,36},... | collective-permute-start | bytes 3145736 | tf_op jit(solution)/shard_map/ppermute | solution.py:384
  3.9 2.3 %collective-permute-start.1 = (s32[1,512]{1,0:T(1,128)S(1)}, s32[1,512]{1,0:T(1,128)S(1)}, u32[]{:S(2)}, u32[]{:S(2)}) collective-permute-start(s32[1,512]{1,0:T(1,128)S(1)} %bitcast.8), channel_id=1, source_target_pairs={{0,4},{4,0},{8,12},{12,8},{16,20},{20,16},{24,28},{28,24},{32,36},... | collective-permute-start | bytes 6152 | tf_op jit(solution)/shard_map/ppermute | solution.py:384
  3.9 1.2 %copy-start = (bf16[512,1024]{1,0:T(8,128)(2,1)S(1)}, bf16[512,1024]{1,0:T(8,128)(2,1)}, u32[]{:S(2)}) copy-start(bf16[512,1024]{1,0:T(8,128)(2,1)} %rows_ref.1) | copy-start | bytes 3145732
  56.0 29.1 %collective-permute-start.2 = (bf16[32,200,128]{2,1,0:T(8,128)(2,1)S(1)}, bf16[32,200,128]{2,1,0:T(8,128)(2,1)S(1)}, u32[]{:S(2)}, u32[]{:S(2)}) collective-permute-start(bf16[32,200,128]{2,1,0:T(8,128)(2,1)S(1)} %all_to_all.21.first_ref), channel_id=1, source_target_pairs={{0,1},{4,12},{1,2},{5,13},{2,3},{6,14},{3,0},{7,15},{8,9},{12,20},... | collective-permute-start | bytes 4915208 | tf_op jit(solution)/shard_map/ppermute | solution.py:379
  57.6 27.6 %collective-permute-start.3 = (bf16[32,200,128]{2,1,0:T(8,128)(2,1)S(1)}, bf16[32,200,128]{2,1,0:T(8,128)(2,1)S(1)}, u32[]{:S(2)}, u32[]{:S(2)}) collective-permute-start(bf16[32,200,128]{2,1,0:T(8,128)(2,1)S(1)} %all_to_all.21.first_ref), channel_id=1, source_target_pairs={{0,3},{4,28},{1,0},{5,29},{2,1},{6,30},{3,2},{7,31},{8,11},{12,4},... | collective-permute-start | bytes 4915208 | tf_op jit(solution)/shard_map/ppermute | solution.py:379
  79.8 10.9 %collective-permute-start.4 = (bf16[32,64,128]{2,1,0:T(8,128)(2,1)S(1)}, bf16[32,64,128]{2,1,0:T(8,128)(2,1)S(1)}, u32[]{:S(2)}, u32[]{:S(2)}) collective-permute-start(bf16[32,64,128]{2,1,0:T(8,128)(2,1)S(1)} %all_to_all.22.second_ref), channel_id=1, source_target_pairs={{0,1},{4,12},{1,2},{5,13},{2,3},{6,14},{3,0},{7,15},{8,9},{12,20},... | collective-permute-start | bytes 1572872 | tf_op jit(solution)/shard_map/ppermute | solution.py:379
  79.8 10.9 %collective-permute-start.5 = (bf16[32,64,128]{2,1,0:T(8,128)(2,1)S(1)}, bf16[32,64,128]{2,1,0:T(8,128)(2,1)S(1)}, u32[]{:S(2)}, u32[]{:S(2)}) collective-permute-start(bf16[32,64,128]{2,1,0:T(8,128)(2,1)S(1)} %all_to_all.22.second_ref), channel_id=1, source_target_pairs={{0,3},{4,28},{1,0},{5,29},{2,1},{6,30},{3,2},{7,31},{8,11},{12,4},... | collective-permute-start | bytes 1572872 | tf_op jit(solution)/shard_map/ppermute | solution.py:379
  91.6 3.0 %collective-permute-start.6 = (f32[32,128]{1,0:T(8,128)S(1)}, f32[32,128]{1,0:T(8,128)S(1)}, u32[]{:S(2)}, u32[]{:S(2)}) collective-permute-start(f32[32,128]{1,0:T(8,128)S(1)} %shard_map.42), channel_id=1, source_target_pairs={{0,3},{4,28},{1,0},{5,29},{2,1},{6,30},{3,2},{7,31},{8,11},{12,4},... | collective-permute-start | bytes 49160 | tf_op jit(solution)/shard_map/ppermute | solution.py:379
  108.3 5.1 %collective-permute-start.7 = (f32[32,128]{1,0:T(8,128)S(1)}, f32[32,128]{1,0:T(8,128)S(1)}, u32[]{:S(2)}, u32[]{:S(2)}) collective-permute-start(f32[32,128]{1,0:T(8,128)S(1)} %bitcast.6), channel_id=1, source_target_pairs={{0,4},{4,0},{8,12},{12,8},{16,20},{20,16},{24,28},{28,24},{32,36},... | collective-permute-start | bytes 49160 | tf_op jit(solution)/shard_map/ppermute | solution.py:384

commit v7 on v6

--- a/solution.py
+++ b/solution.py
@@ -26,6 +26,7 @@
 NONE = float("-inf")
 Z, X, Y = 8, 4, 4
 AXES = ("shard", "clus")
+FIRST = (5, 2)
 VMEM = pl.BlockSpec(memory_space=pltpu.VMEM)
 LINE = jax.ShapeDtypeStruct((1, PANEL), jnp.float32)
 SQUARE = jax.ShapeDtypeStruct((PANEL, PANEL), jnp.float32)
@@ -70,12 +71,12 @@
 def whereabouts():
     shard, y = lax.axis_index("shard"), lax.axis_index("clus")
     core, x = shard % 2, shard // 2 % X
+    x, y = ((i + PER_TILE - FIRST[1]) % PER_TILE for i in (x, y))
     return core, jnp.where(core == 0, x, y), jnp.where(core == 0, y, x)
 
 
-def pack_half(half, rows, label, put):
+def pack_half(half, rows, cluster, arrival, put, wait=lambda: None):
     core, place, _ = whereabouts()
-    cluster, arrival = label // SPAN, label % SPAN
     owner = cluster % OWNERS
     earlier = (iota((ROWS, ROWS), 0) < iota((ROWS, ROWS), 1)).astype(jnp.bfloat16)
     member = iota((OWNERS, ROWS), 0) == owner
@@ -84,6 +85,7 @@
     mine = owner % 2 == core
     slot = owner // 2 * CAPACITY + within
 
+    wait()
     wide = rows[...].astype(jnp.float32)
     norm = as_row(jnp.sum(wide * wide, axis=1, keepdims=True))
     high = narrow(norm)
@@ -112,17 +114,26 @@
     return jnp.where(mine, slot, slot + HALF), labels
 
 
-def pack_own_kernel(rows_ref, label_ref, half_ref, labels_ref, slot_ref):
+def pack_own_kernel(
+    rows_ref, cluster_ref, arrival_ref, half_ref, labels_ref, slot_ref, rows, cluster, arrival, done
+):
     def put(g, step, k, value):
         half_ref[g : g + step, k * CAPACITY : (k + 1) * CAPACITY, :] = value
 
-    slot, labels = pack_half(0, rows_ref, label_ref[...], put)
+    pairs = ((cluster_ref, cluster), (arrival_ref, arrival), (rows_ref, rows))
+    copies = [pltpu.make_async_copy(a, b, done.at[i]) for i, (a, b) in enumerate(pairs)]
+    for copy in copies:
+        copy.start()
+    copies[0].wait()
+    copies[1].wait()
+    slot, labels = pack_half(0, rows, cluster[...], arrival[...], put, copies[2].wait)
     slot_ref[...] = slot
     for g in range(GROUPS):
         labels_ref[g] = labels[g]
 
 
-def pack_own(rows, label):
+def pack_own(*arrays):
+    arrays = [pltpu.with_memory_space_constraint(array, pltpu.HBM) for array in arrays]
     return pl.pallas_call(
         pack_own_kernel,
         out_shape=(
@@ -130,14 +141,22 @@
             jax.ShapeDtypeStruct((GROUPS, 8, LANES), jnp.float32),
             jax.ShapeDtypeStruct((1, ROWS), jnp.int32),
         ),
-        in_specs=[VMEM] * 2,
+        in_specs=[pl.BlockSpec(memory_space=pltpu.HBM)] * 3,
         out_specs=(VMEM,) * 3,
+        scratch_shapes=[
+            pltpu.VMEM((ROWS, D), jnp.bfloat16),
+            pltpu.VMEM((1, ROWS), jnp.int32),
+            pltpu.VMEM((1, ROWS), jnp.int32),
+            pltpu.SemaphoreType.DMA((3,)),
+        ],
         compiler_params=pltpu.CompilerParams(vmem_limit_bytes=16 * 2**20),
         cost_estimate=pl.CostEstimate(flops=2**30, bytes_accessed=2**21, transcendentals=0),
-    )(rows, label)
-
-
-def pack_other_kernel(rows_ref, label_ref, half_ref, labels_ref, first_ref, second_ref):
+    )(*arrays)
+
+
+def pack_other_kernel(
+    rows_ref, cluster_ref, arrival_ref, half_ref, labels_ref, first_ref, second_ref
+):
     def place(k, half):
         out_ref, tile = (first_ref, k) if k < PARTS[0] else (second_ref, k - PARTS[0])
         return out_ref, tile * SLOTS + half * CAPACITY
@@ -149,21 +168,21 @@
     for k in range(TILES):
         out_ref, at = place(k, 0)
         out_ref[:, at : at + CAPACITY, :] = half_ref[:, k * CAPACITY : (k + 1) * CAPACITY, :]
-    _, labels = pack_half(1, rows_ref, label_ref[...], put)
+    _, labels = pack_half(1, rows_ref, cluster_ref[...], arrival_ref[...], put)
     for g in range(GROUPS):
         first_ref[g, LABELS:, :] = (labels[g] + labels_ref[g]).astype(jnp.bfloat16)
 
 
-def pack_other(rows, label, half, labels):
+def pack_other(rows, cluster, arrival, half, labels):
     return pl.pallas_call(
         pack_other_kernel,
         out_shape=tuple(
             jax.ShapeDtypeStruct((GROUPS, height, LANES), jnp.bfloat16) for height in HEIGHTS
         ),
-        in_specs=[VMEM] * 4,
+        in_specs=[VMEM] * 5,
         out_specs=(VMEM,) * 2,
         compiler_params=pltpu.CompilerParams(vmem_limit_bytes=16 * 2**20),
-    )(rows, label, half, labels)
+    )(rows, cluster, arrival, half, labels)
 
 
 def info(ref):
@@ -360,8 +379,10 @@
 
 
 PLACES = [(z, x, y) for z in range(Z) for x in range(X) for y in range(Y)]
-OWNER_GROUPS = [[device(z, x, 0, y) for z in range(Z) for x in range(X)] for y in range(Y)] + [
-    [device(z, x, 1, y) for z in range(Z) for y in range(Y)] for x in range(X)
+ORDER = [(z + FIRST[0]) % Z for z in range(Z)]
+TURN = [(i + FIRST[1]) % PER_TILE for i in range(PER_TILE)]
+OWNER_GROUPS = [[device(z, x, 0, y) for z in ORDER for x in TURN] for y in range(Y)] + [
+    [device(z, x, 1, y) for z in ORDER for y in TURN] for x in range(X)
 ]
 
 
@@ -385,9 +406,9 @@
 
 
 def per_device(embeddings, cluster, arrival):
-    label = (cluster * SPAN + arrival).reshape(1, ROWS)
-    half, labels, slot = pack_own(embeddings, label)
-    first, second = pack_other(other_core(embeddings), other_core(label), half, labels)
+    arrays = (embeddings, cluster.reshape(1, ROWS), arrival.reshape(1, ROWS))
+    half, labels, slot = pack_own(*arrays)
+    first, second = pack_other(*[other_core(array) for array in arrays], half, labels)
     own_first = to_owners(first)
     below_first, above_first = passed_along(own_first, 1), passed_along(own_first, -1)
     own_second = to_owners(second)

time: 115 us -> 111 us (0.965)
  blocking collectives: 83.2 us -> 79.6 us
  local copies, waits for them, and re-layouts: 1.22 us -> 0 us
  Pallas kernels: 13.7 us -> 14.9 us
    all_to_all x3, blocking collectives: 83.2 us -> 79.6 us  [to_owners(): lax.all_to_all(array, AXES, split_axis=0, concat_axis=0, tiled=True, axis...]
    unnamed x2 -> x0, local copies, waits for them, and re-layouts: 1.22 us -> none
    ppermute x3 -> x4, starting transfers between devices: 7.55 us -> 8.21 us  [other_core(): return lax.ppermute(array, 'shard', [(i, i ^ 1) for i in range(size)])]
  transfers between devices with their start and end apart: 8 -> 9, of which waited for: 1 -> 1; matrix products, arithmetic and copies ran while one was open for 1% -> 0% of each run, Pallas kernels for 9% -> 11%
where the time goes in v7:
time: 111 us; the launch traced here: 110 us
  blocking collectives  79.6 us (72%)
  starting transfers between devices  14.9 us (13%)
  Pallas kernels  14.9 us (13%)
    all_to_all x3, blocking collectives, to_owners(): lax.all_to_all(array, AXES, split_axis=0, concat_axis=0, tiled=True, axis...  79.6 us
    ppermute x4, starting transfers between devices, other_core(): return lax.ppermute(array, 'shard', [(i, i ^ 1) for i in range(size)])  8.21 us
    ppermute x5, starting transfers between devices, passed_along(): return lax.ppermute(array, AXES, pairs)  6.72 us
    pallas_call x1, Pallas kernels, score_head(): pl.pallas_call(head_kernel, out_shape=(SQUARE, SQUARE, SQUARE, jax.ShapeD...  5.51 us
    pallas_call x1, Pallas kernels, score_own(): pl.pallas_call(own_kernel, out_shape=LINE, in_specs=[VMEM] * 2, out_specs...  2.68 us
  transfers between devices with their start and end apart: 9, of which 1 were waited for; matrix products, arithmetic and copies ran while one was open for 0% of the time, Pallas kernels for 11%

profile of v7, /device:TPU:1, one launch (start us, length us, event | category | flops | bytes accessed | tf_op | source)
XLA Modules:
  0.0 110.4 jit_solution(7950662325463086915)
XLA Ops:
  0.0 3.2 %collective-permute-start = (bf16[512,1024]{1,0:T(8,128)(2,1)}, bf16[512,1024]{1,0:T(8,128)(2,1)S(1)}, u32[]{:S(2)}, u32[]{:S(2)}) collective-permute-start(bf16[512,1024]{1,0:T(8,128)(2,1)} %rows_ref.1), channel_id=1, source_target_pairs={{0,4},{4,0},{8,12},{12,8},{16,20},{20,16},{24,28},{28,24},{32,36},... | collective-permute-start | bytes 3145736 | tf_op jit(solution)/shard_map/ppermute | solution.py:405
  3.2 0.0 collective-permute-start.1
  3.2 0.5 collective-permute-start.2
  3.8 2.2 %shard_map.37 = (bf16[32,128,128]{2,1,0:T(8,128)(2,1)S(1)}, f32[32,8,128]{2,1,0:T(8,128)S(1)}, s32[1,512]{1,0:T(1,128)S(1)}) custom-call(bf16[512,1024]{1,0:T(8,128)(2,1)} %rows_ref.1, s32[1,512]{1,0:T(1,128)} %bitcast.11, s32[1,512]{1,0:T(1,128)} %bitcast.13), custom_call_target="tpu_custom_call" | custom-call | flops 1073741824 | bytes 2097152 | tf_op jit(solution)/shard_map/pallas_call | solution.py:137
  5.9 0.0 collective-permute-done.1.cluster_ref
  6.0 0.0 collective-permute-done.2.arrival_ref
  6.0 0.0 collective-permute-done.rows_ref
  6.0 1.2 %shard_map.38 = (bf16[32,200,128]{2,1,0:T(8,128)(2,1)S(1)}, bf16[32,64,128]{2,1,0:T(8,128)(2,1)S(1)}) custom-call(bf16[512,1024]{1,0:T(8,128)(2,1)S(1)} %collective-permute-done.rows_ref, s32[1,512]{1,0:T(1,128)S(1)} %collective-permute-done.1.cluster_ref, s32[1,512]{1,0:T(1,128)S(1)} %collective-permute-done.2.arrival_ref, ...), custom_call_target="tpu_custom_call" | custom-call | tf_op jit(solution)/shard_map/pallas_call | solution.py:177
  7.2 46.2 %all_to_all.21.first_ref = bf16[32,200,128]{2,1,0:T(8,128)(2,1)S(1)} all-to-all(bf16[32,200,128]{2,1,0:T(8,128)(2,1)S(1)} %get-tuple-element.16), channel_id=1, replica_groups={{176,184,160,168,208,216,192,200,240,248,224,232,16,24,0,8,48,56,32,40,..., dimensions={0} | all-to-all | bytes 3276800 | tf_op jit(solution)/shard_map/all_to_all | solution.py:390
  53.4 0.6 collective-permute-start.3
  54.0 2.1 %collective-permute-start.4 = (bf16[32,200,128]{2,1,0:T(8,128)(2,1)S(1)}, bf16[32,200,128]{2,1,0:T(8,128)(2,1)S(1)}, u32[]{:S(2)}, u32[]{:S(2)}) collective-permute-start(bf16[32,200,128]{2,1,0:T(8,128)(2,1)S(1)} %all_to_all.21.first_ref), channel_id=1, source_target_pairs={{0,3},{4,28},{1,0},{5,29},{2,1},{6,30},{3,2},{7,31},{8,11},{12,4},... | collective-permute-start | bytes 4915208 | tf_op jit(solution)/shard_map/ppermute | solution.py:400
  56.0 21.1 %all_to_all.22.second_ref = bf16[32,64,128]{2,1,0:T(8,128)(2,1)S(1)} all-to-all(bf16[32,64,128]{2,1,0:T(8,128)(2,1)S(1)} %get-tuple-element.17), channel_id=1, replica_groups={{176,184,160,168,208,216,192,200,240,248,224,232,16,24,0,8,48,56,32,40,..., dimensions={0} | all-to-all | bytes 1048576 | tf_op jit(solution)/shard_map/all_to_all | solution.py:390
  77.1 0.0 collective-permute-start.5
  77.1 2.7 %collective-permute-start.6 = (bf16[32,64,128]{2,1,0:T(8,128)(2,1)S(1)}, bf16[32,64,128]{2,1,0:T(8,128)(2,1)S(1)}, u32[]{:S(2)}, u32[]{:S(2)}) collective-permute-start(bf16[32,64,128]{2,1,0:T(8,128)(2,1)S(1)} %all_to_all.22.second_ref), channel_id=1, source_target_pairs={{0,3},{4,28},{1,0},{5,29},{2,1},{6,30},{3,2},{7,31},{8,11},{12,4},... | collective-permute-start | bytes 1572872 | tf_op jit(solution)/shard_map/ppermute | solution.py:400
  79.8 2.7 %shard_map.39.best_ref = f32[1,1024]{1,0:T(1,128)S(1)} custom-call(bf16[32,200,128]{2,1,0:T(8,128)(2,1)S(1)} %all_to_all.21.first_ref, bf16[32,64,128]{2,1,0:T(8,128)(2,1)S(1)} %all_to_all.22.second_ref), custom_call_target="tpu_custom_call" | custom-call | flops 3221225472 | bytes 4194304 | tf_op jit(solution)/shard_map/pallas_call | solution.py:267
  82.5 0.0 collective-permute-done.3.below_ref
  82.5 0.0 collective-permute-done.4.above_ref
  82.5 5.5 %shard_map.40 = (f32[1024,1024]{1,0:T(8,128)S(1)}, f32[1024,1024]{1,0:T(8,128)S(1)}, f32[1024,1024]{1,0:T(8,128)S(1)}, f32[8,1024]{1,0:T(8,128)S(1)}) custom-call(bf16[32,200,128]{2,1,0:T(8,128)(2,1)S(1)} %all_to_all.21.first_ref, bf16[32,200,128]{2,1,0:T(8,128)(2,1)S(1)} %collective-permute-done.3.below_ref, ...), custom_call_target="tpu_custom_call" | custom-call | flops 6442450944 | bytes 16777216 | tf_op jit(solution)/shard_map/pallas_call | solution.py:241
  88.0 0.0 collective-permute-done.5.below_ref
  88.0 0.0 collective-permute-done.6.above_ref
  88.0 0.8 shard_map.42
  88.9 1.4 %collective-permute-start.7 = (f32[32,128]{1,0:T(8,128)S(1)}, f32[32,128]{1,0:T(8,128)S(1)}, u32[]{:S(2)}, u32[]{:S(2)}) collective-permute-start(f32[32,128]{1,0:T(8,128)S(1)} %shard_map.42), channel_id=1, source_target_pairs={{0,3},{4,28},{1,0},{5,29},{2,1},{6,30},{3,2},{7,31},{8,11},{12,4},... | collective-permute-start | bytes 49160 | tf_op jit(solution)/shard_map/ppermute | solution.py:400
  90.2 1.6 %shard_map.41 = f32[32,128]{1,0:T(8,128)S(1)} custom-call(f32[1,1024]{1,0:T(1,128)S(1)} %shard_map.39.best_ref, f32[1024,1024]{1,0:T(8,128)S(1)} %get-tuple-element.18.own_below, f32[1024,1024]{1,0:T(8,128)S(1)} %get-tuple-element.19.own_above, f32[8,1024]{1,0:T(8,128)S(1)} %get-tuple-element.20.inverse_ref, bf16[32,64,128]{2,1,0:T(8,128)(2,1)S(1)} %all_to_all.22.second_ref, ...), custom_call_target="tpu_custom_call" | custom-call | flops 1073741824 | bytes 16777216 | tf_op jit(solution)/shard_map/pallas_call | solution.py:337
  91.8 0.0 collective-permute-done.7
  91.9 12.3 %all_to_all.23 = f32[32,1,128]{2,1,0:T(1,128)S(1)} all-to-all(f32[32,1,128]{2,1,0:T(1,128)S(1)} %bitcast.9), channel_id=1, replica_groups={{176,184,160,168,208,216,192,200,240,248,224,232,16,24,0,8,48,56,32,40,..., dimensions={0} | all-to-all | bytes 32768 | tf_op jit(solution)/shard_map/all_to_all | solution.py:390
  104.2 4.5 %collective-permute-start.8 = (f32[32,128]{1,0:T(8,128)S(1)}, f32[32,128]{1,0:T(8,128)S(1)}, u32[]{:S(2)}, u32[]{:S(2)}) collective-permute-start(f32[32,128]{1,0:T(8,128)S(1)} %bitcast.7), channel_id=1, source_target_pairs={{0,4},{4,0},{8,12},{12,8},{16,20},{20,16},{24,28},{28,24},{32,36},... | collective-permute-start | bytes 49160 | tf_op jit(solution)/shard_map/ppermute | solution.py:405
  108.6 0.8 collective-permute-done.8.other_ref
  109.5 0.9 shard_map.43
  (1 shorter events, 0.0 us)
Async XLA Ops:
  0.0 6.0 %collective-permute-start = (bf16[512,1024]{1,0:T(8,128)(2,1)}, bf16[512,1024]{1,0:T(8,128)(2,1)S(1)}, u32[]{:S(2)}, u32[]{:S(2)}) collective-permute-start(bf16[512,1024]{1,0:T(8,128)(2,1)} %rows_ref.1), channel_id=1, source_target_pairs={{0,4},{4,0},{8,12},{12,8},{16,20},{20,16},{24,28},{28,24},{32,36},... | collective-permute-start | bytes 3145736 | tf_op jit(solution)/shard_map/ppermute | solution.py:405
  3.2 2.7 %collective-permute-start.1 = (s32[1,512]{1,0:T(1,128)}, s32[1,512]{1,0:T(1,128)S(1)}, u32[]{:S(2)}, u32[]{:S(2)}) collective-permute-start(s32[1,512]{1,0:T(1,128)} %bitcast.10), channel_id=1, source_target_pairs={{0,4},{4,0},{8,12},{12,8},{16,20},{20,16},{24,28},{28,24},{32,36},... | collective-permute-start | bytes 6152 | tf_op jit(solution)/shard_map/ppermute | solution.py:405
  3.2 2.7 %collective-permute-start.2 = (s32[1,512]{1,0:T(1,128)}, s32[1,512]{1,0:T(1,128)S(1)}, u32[]{:S(2)}, u32[]{:S(2)}) collective-permute-start(s32[1,512]{1,0:T(1,128)} %bitcast.12), channel_id=1, source_target_pairs={{0,4},{4,0},{8,12},{12,8},{16,20},{20,16},{24,28},{28,24},{32,36},... | collective-permute-start | bytes 6152 | tf_op jit(solution)/shard_map/ppermute | solution.py:405
  53.4 29.1 %collective-permute-start.3 = (bf16[32,200,128]{2,1,0:T(8,128)(2,1)S(1)}, bf16[32,200,128]{2,1,0:T(8,128)(2,1)S(1)}, u32[]{:S(2)}, u32[]{:S(2)}) collective-permute-start(bf16[32,200,128]{2,1,0:T(8,128)(2,1)S(1)} %all_to_all.21.first_ref), channel_id=1, source_target_pairs={{0,1},{4,12},{1,2},{5,13},{2,3},{6,14},{3,0},{7,15},{8,9},{12,20},... | collective-permute-start | bytes 4915208 | tf_op jit(solution)/shard_map/ppermute | solution.py:400
  54.0 28.5 %collective-permute-start.4 = (bf16[32,200,128]{2,1,0:T(8,128)(2,1)S(1)}, bf16[32,200,128]{2,1,0:T(8,128)(2,1)S(1)}, u32[]{:S(2)}, u32[]{:S(2)}) collective-permute-start(bf16[32,200,128]{2,1,0:T(8,128)(2,1)S(1)} %all_to_all.21.first_ref), channel_id=1, source_target_pairs={{0,3},{4,28},{1,0},{5,29},{2,1},{6,30},{3,2},{7,31},{8,11},{12,4},... | collective-permute-start | bytes 4915208 | tf_op jit(solution)/shard_map/ppermute | solution.py:400
  77.1 10.9 %collective-permute-start.5 = (bf16[32,64,128]{2,1,0:T(8,128)(2,1)S(1)}, bf16[32,64,128]{2,1,0:T(8,128)(2,1)S(1)}, u32[]{:S(2)}, u32[]{:S(2)}) collective-permute-start(bf16[32,64,128]{2,1,0:T(8,128)(2,1)S(1)} %all_to_all.22.second_ref), channel_id=1, source_target_pairs={{0,1},{4,12},{1,2},{5,13},{2,3},{6,14},{3,0},{7,15},{8,9},{12,20},... | collective-permute-start | bytes 1572872 | tf_op jit(solution)/shard_map/ppermute | solution.py:400
  77.1 10.9 %collective-permute-start.6 = (bf16[32,64,128]{2,1,0:T(8,128)(2,1)S(1)}, bf16[32,64,128]{2,1,0:T(8,128)(2,1)S(1)}, u32[]{:S(2)}, u32[]{:S(2)}) collective-permute-start(bf16[32,64,128]{2,1,0:T(8,128)(2,1)S(1)} %all_to_all.22.second_ref), channel_id=1, source_target_pairs={{0,3},{4,28},{1,0},{5,29},{2,1},{6,30},{3,2},{7,31},{8,11},{12,4},... | collective-permute-start | bytes 1572872 | tf_op jit(solution)/shard_map/ppermute | solution.py:400
  88.9 3.0 %collective-permute-start.7 = (f32[32,128]{1,0:T(8,128)S(1)}, f32[32,128]{1,0:T(8,128)S(1)}, u32[]{:S(2)}, u32[]{:S(2)}) collective-permute-start(f32[32,128]{1,0:T(8,128)S(1)} %shard_map.42), channel_id=1, source_target_pairs={{0,3},{4,28},{1,0},{5,29},{2,1},{6,30},{3,2},{7,31},{8,11},{12,4},... | collective-permute-start | bytes 49160 | tf_op jit(solution)/shard_map/ppermute | solution.py:400
  104.2 5.3 %collective-permute-start.8 = (f32[32,128]{1,0:T(8,128)S(1)}, f32[32,128]{1,0:T(8,128)S(1)}, u32[]{:S(2)}, u32[]{:S(2)}) collective-permute-start(f32[32,128]{1,0:T(8,128)S(1)} %bitcast.7), channel_id=1, source_target_pairs={{0,4},{4,0},{8,12},{12,8},{16,20},{20,16},{24,28},{28,24},{32,36},... | collective-permute-start | bytes 49160 | tf_op jit(solution)/shard_map/ppermute | solution.py:405

commit v8 on v7

--- a/solution.py
+++ b/solution.py
@@ -215,7 +215,18 @@
 
 
 def head_kernel(
-    first_ref, below_ref, above_ref, own_below, own_above, below_above, inverse_ref, own, below, above
+    first_ref,
+    below_ref,
+    above_ref,
+    own_below,
+    own_above,
+    below_above,
+    inverse_ref,
+    below_scale,
+    above_scale,
+    own,
+    below,
+    above,
 ):
     unfold(first_ref, own, PARTS[0])
     unfold(below_ref, below, PARTS[0])
@@ -227,6 +238,8 @@
     below_key = column_keys(cluster, arrival)
     cluster, arrival, inverse_ref[2:3] = info(above_ref)
     above_key = column_keys(cluster, arrival)
+    below_scale[...] = as_column(inverse_ref[1:2])
+    above_scale[...] = as_column(inverse_ref[2:3])
 
     def masked(key, base, limit, scores):
         return jnp.where((key < limit) & (key >= base), scores, NONE)
@@ -240,9 +253,10 @@
 def score_head(first, below, above):
     return pl.pallas_call(
         head_kernel,
-        out_shape=(SQUARE, SQUARE, SQUARE, jax.ShapeDtypeStruct((8, PANEL), jnp.float32)),
+        out_shape=(SQUARE, SQUARE, SQUARE, jax.ShapeDtypeStruct((8, PANEL), jnp.float32))
+        + (jax.ShapeDtypeStruct((PANEL, 1), jnp.float32),) * 2,
         in_specs=[VMEM] * 3,
-        out_specs=(VMEM,) * 4,
+        out_specs=(VMEM,) * 6,
         scratch_shapes=[pltpu.VMEM((PANEL, HEAD), jnp.bfloat16)] * 3,
         compiler_params=pltpu.CompilerParams(vmem_limit_bytes=32 * 2**20),
         cost_estimate=pl.CostEstimate(flops=6 * 2**30, bytes_accessed=2**24, transcendentals=0),
@@ -293,24 +307,24 @@
     return best
 
 
-def far_kernel(below_above, inverse_ref, below_ref, above_ref, out_ref, below, above):
+def far_kernel(below_above, inverse_ref, scale, below_ref, above_ref, out_ref, below, above):
     unfold(below_ref, below, PARTS[1])
     unfold(above_ref, above, PARTS[1])
     best = jnp.full((1, PANEL), NONE, jnp.float32)
-    best = fold(best, below_above, above, below, as_column(inverse_ref[2:3]))
+    best = fold(best, below_above, above, below, scale)
     out_ref[...] = finish(best, inverse_ref[1:2])
 
 
-def score_far(below_above, inverse, below, above):
+def score_far(below_above, inverse, scale, below, above):
     return pl.pallas_call(
         far_kernel,
         out_shape=jax.ShapeDtypeStruct((GROUPS, LANES), jnp.float32),
-        in_specs=[VMEM] * 4,
+        in_specs=[VMEM] * 5,
         out_specs=VMEM,
         scratch_shapes=[pltpu.VMEM((PANEL, TAIL), jnp.bfloat16)] * 2,
         compiler_params=pltpu.CompilerParams(vmem_limit_bytes=16 * 2**20),
         cost_estimate=pl.CostEstimate(flops=2**29, bytes_accessed=2**23, transcendentals=0),
-    )(below_above, inverse, below, above)
+    )(below_above, inverse, scale, below, above)
 
 
 def near_kernel(
@@ -318,6 +332,8 @@
     own_below,
     own_above,
     inverse_ref,
+    below_scale,
+    above_scale,
     second_ref,
     below_ref,
     above_ref,
@@ -328,21 +344,21 @@
 ):
     for source, target in ((second_ref, own), (below_ref, below), (above_ref, above)):
         unfold(source, target, PARTS[1])
-    best = fold(best_ref[...], own_below, below, own, as_column(inverse_ref[1:2]))
-    best = fold(best, own_above, above, own, as_column(inverse_ref[2:3]))
+    best = fold(best_ref[...], own_below, below, own, below_scale)
+    best = fold(best, own_above, above, own, above_scale)
     out_ref[...] = finish(best, inverse_ref[0:1])
 
 
-def score_near(best, own_below, own_above, inverse, second, below, above):
+def score_near(best, own_below, own_above, inverse, scales, second, below, above):
     return pl.pallas_call(
         near_kernel,
         out_shape=jax.ShapeDtypeStruct((GROUPS, LANES), jnp.float32),
-        in_specs=[VMEM] * 7,
+        in_specs=[VMEM] * 9,
         out_specs=VMEM,
         scratch_shapes=[pltpu.VMEM((PANEL, TAIL), jnp.bfloat16)] * 3,
         compiler_params=pltpu.CompilerParams(vmem_limit_bytes=24 * 2**20),
         cost_estimate=pl.CostEstimate(flops=2**30, bytes_accessed=2**24, transcendentals=0),
-    )(best, own_below, own_above, inverse, second, below, above)
+    )(best, own_below, own_above, inverse, *scales, second, below, above)
 
 
 def unpack_kernel(own_ref, other_ref, slot_ref, out_ref):
@@ -413,10 +429,12 @@
     below_first, above_first = passed_along(own_first, 1), passed_along(own_first, -1)
     own_second = to_owners(second)
     below_second, above_second = passed_along(own_second, 1), passed_along(own_second, -1)
-    own_below, own_above, below_above, inverse = score_head(own_first, below_first, above_first)
+    own_below, own_above, below_above, inverse, *scales = score_head(own_first, below_first, above_first)
     best = score_own(own_first, own_second)
-    far = passed_along(score_far(below_above, inverse, below_second, above_second), -1)
-    near = score_near(best, own_below, own_above, inverse, own_second, below_second, above_second)
+    far = passed_along(score_far(below_above, inverse, scales[1], below_second, above_second), -1)
+    near = score_near(
+        best, own_below, own_above, inverse, scales, own_second, below_second, above_second
+    )
     block = to_owners(jnp.maximum(near, far))
     return unpack(block, other_core(block), slot)
 

time: 111 us -> 111 us (level)
  transfers between devices with their start and end apart: 9 -> 9, of which waited for: 1 -> 2; matrix products, arithmetic and copies ran while one was open for 0% -> 0% of each run, Pallas kernels for 11% -> 11%
where the time goes in v8:
time: 111 us; the launch traced here: 110 us
  blocking collectives  79.6 us (72%)
  starting transfers between devices  15.1 us (14%)
  Pallas kernels  14.8 us (13%)
    all_to_all x3, blocking collectives, to_owners(): lax.all_to_all(array, AXES, split_axis=0, concat_axis=0, tiled=True, axis...  79.6 us
    ppermute x4, starting transfers between devices, other_core(): return lax.ppermute(array, 'shard', [(i, i ^ 1) for i in range(size)])  8.52 us
    ppermute x5, starting transfers between devices, passed_along(): return lax.ppermute(array, AXES, pairs)  6.53 us
    pallas_call x1, Pallas kernels, score_head(): pl.pallas_call(head_kernel, out_shape=(SQUARE, SQUARE, SQUARE, jax.ShapeD...  5.7 us
    pallas_call x1, Pallas kernels, score_own(): pl.pallas_call(own_kernel, out_shape=LINE, in_specs=[VMEM] * 2, out_specs...  2.68 us
  transfers between devices with their start and end apart: 9, of which 2 were waited for; matrix products, arithmetic and copies ran while one was open for 0% of the time, Pallas kernels for 11%

profile of v8, /device:TPU:1, one launch (start us, length us, event | category | flops | bytes accessed | tf_op | source)
XLA Modules:
  0.0 110.5 jit_solution(14119809680803054349)
XLA Ops:
  0.0 3.2 %collective-permute-start = (bf16[512,1024]{1,0:T(8,128)(2,1)}, bf16[512,1024]{1,0:T(8,128)(2,1)S(1)}, u32[]{:S(2)}, u32[]{:S(2)}) collective-permute-start(bf16[512,1024]{1,0:T(8,128)(2,1)} %rows_ref.1), channel_id=1, source_target_pairs={{0,4},{4,0},{8,12},{12,8},{16,20},{20,16},{24,28},{28,24},{32,36},... | collective-permute-start | bytes 3145736 | tf_op jit(solution)/shard_map/ppermute | solution.py:421
  3.2 0.0 collective-permute-start.1
  3.2 0.5 collective-permute-start.2
  3.8 2.2 %shard_map.37 = (bf16[32,128,128]{2,1,0:T(8,128)(2,1)S(1)}, f32[32,8,128]{2,1,0:T(8,128)S(1)}, s32[1,512]{1,0:T(1,128)S(1)}) custom-call(bf16[512,1024]{1,0:T(8,128)(2,1)} %rows_ref.1, s32[1,512]{1,0:T(1,128)} %bitcast.11, s32[1,512]{1,0:T(1,128)} %bitcast.13), custom_call_target="tpu_custom_call" | custom-call | flops 1073741824 | bytes 2097152 | tf_op jit(solution)/shard_map/pallas_call | solution.py:137
  5.9 0.0 collective-permute-done.1.cluster_ref
  6.0 0.0 collective-permute-done.2.arrival_ref
  6.0 0.0 collective-permute-done.rows_ref
  6.0 1.2 %shard_map.38 = (bf16[32,200,128]{2,1,0:T(8,128)(2,1)S(1)}, bf16[32,64,128]{2,1,0:T(8,128)(2,1)S(1)}) custom-call(bf16[512,1024]{1,0:T(8,128)(2,1)S(1)} %collective-permute-done.rows_ref, s32[1,512]{1,0:T(1,128)S(1)} %collective-permute-done.1.cluster_ref, s32[1,512]{1,0:T(1,128)S(1)} %collective-permute-done.2.arrival_ref, ...), custom_call_target="tpu_custom_call" | custom-call | tf_op jit(solution)/shard_map/pallas_call | solution.py:177
  7.2 46.2 %all_to_all.21.first_ref = bf16[32,200,128]{2,1,0:T(8,128)(2,1)S(1)} all-to-all(bf16[32,200,128]{2,1,0:T(8,128)(2,1)S(1)} %get-tuple-element.18), channel_id=1, replica_groups={{176,184,160,168,208,216,192,200,240,248,224,232,16,24,0,8,48,56,32,40,..., dimensions={0} | all-to-all | bytes 3276800 | tf_op jit(solution)/shard_map/all_to_all | solution.py:406
  53.4 0.6 collective-permute-start.3
  54.0 2.1 %collective-permute-start.4 = (bf16[32,200,128]{2,1,0:T(8,128)(2,1)S(1)}, bf16[32,200,128]{2,1,0:T(8,128)(2,1)S(1)}, u32[]{:S(2)}, u32[]{:S(2)}) collective-permute-start(bf16[32,200,128]{2,1,0:T(8,128)(2,1)S(1)} %all_to_all.21.first_ref), channel_id=1, source_target_pairs={{0,3},{4,28},{1,0},{5,29},{2,1},{6,30},{3,2},{7,31},{8,11},{12,4},... | collective-permute-start | bytes 4915208 | tf_op jit(solution)/shard_map/ppermute | solution.py:416
  56.0 21.1 %all_to_all.22.second_ref = bf16[32,64,128]{2,1,0:T(8,128)(2,1)S(1)} all-to-all(bf16[32,64,128]{2,1,0:T(8,128)(2,1)S(1)} %get-tuple-element.19), channel_id=1, replica_groups={{176,184,160,168,208,216,192,200,240,248,224,232,16,24,0,8,48,56,32,40,..., dimensions={0} | all-to-all | bytes 1048576 | tf_op jit(solution)/shard_map/all_to_all | solution.py:406
  77.1 0.0 collective-permute-start.5
  77.1 2.7 %collective-permute-start.6 = (bf16[32,64,128]{2,1,0:T(8,128)(2,1)S(1)}, bf16[32,64,128]{2,1,0:T(8,128)(2,1)S(1)}, u32[]{:S(2)}, u32[]{:S(2)}) collective-permute-start(bf16[32,64,128]{2,1,0:T(8,128)(2,1)S(1)} %all_to_all.22.second_ref), channel_id=1, source_target_pairs={{0,3},{4,28},{1,0},{5,29},{2,1},{6,30},{3,2},{7,31},{8,11},{12,4},... | collective-permute-start | bytes 1572872 | tf_op jit(solution)/shard_map/ppermute | solution.py:416
  79.8 2.7 %shard_map.39.best_ref = f32[1,1024]{1,0:T(1,128)S(1)} custom-call(bf16[32,200,128]{2,1,0:T(8,128)(2,1)S(1)} %all_to_all.21.first_ref, bf16[32,64,128]{2,1,0:T(8,128)(2,1)S(1)} %all_to_all.22.second_ref), custom_call_target="tpu_custom_call" | custom-call | flops 3221225472 | bytes 4194304 | tf_op jit(solution)/shard_map/pallas_call | solution.py:281
  82.5 0.0 collective-permute-done.3.below_ref
  82.5 0.0 collective-permute-done.4.above_ref
  82.5 5.7 %shard_map.40 = (f32[1024,1024]{1,0:T(8,128)S(1)}, f32[1024,1024]{1,0:T(8,128)S(1)}, f32[1024,1024]{1,0:T(8,128)S(1)}, f32[8,1024]{1,0:T(8,128)S(1)}, f32[1024,1]{1,0:T(8,128)S(1)}, /*index=5*/f32[1024,1]{1,0:T(8,128)S(1)}) custom-call(bf16[32,200,128]{2,1,0:T(8,128)(2,1)S(1)} %all_to_all.21.first_ref, ...), custom_call_target="tpu_custom_call" | custom-call | flops 6442450944 | bytes 16777216 | tf_op jit(solution)/shard_map/pallas_call | solution.py:254
  88.2 0.0 collective-permute-done.5.below_ref
  88.2 0.0 collective-permute-done.6.above_ref
  88.2 0.8 shard_map.42
  89.0 1.2 %collective-permute-start.7 = (f32[32,128]{1,0:T(8,128)S(1)}, f32[32,128]{1,0:T(8,128)S(1)}, u32[]{:S(2)}, u32[]{:S(2)}) collective-permute-start(f32[32,128]{1,0:T(8,128)S(1)} %shard_map.42), channel_id=1, source_target_pairs={{0,3},{4,28},{1,0},{5,29},{2,1},{6,30},{3,2},{7,31},{8,11},{12,4},... | collective-permute-start | bytes 49160 | tf_op jit(solution)/shard_map/ppermute | solution.py:416
  90.2 1.3 %shard_map.41 = f32[32,128]{1,0:T(8,128)S(1)} custom-call(f32[1,1024]{1,0:T(1,128)S(1)} %shard_map.39.best_ref, f32[1024,1024]{1,0:T(8,128)S(1)} %get-tuple-element.20.own_below, f32[1024,1024]{1,0:T(8,128)S(1)} %get-tuple-element.21.own_above, f32[8,1024]{1,0:T(8,128)S(1)} %get-tuple-element.22.inverse_ref, f32[1024,1]{1,0:T(8,128)S(1)} %get-tuple-element.23.below_scale, ...), custom_call_target="tpu_custom_call" | custom-call | flops 1073741824 | bytes 16777216 | tf_op jit(solution)/shard_map/pallas_call | solution.py:353
  91.5 0.1 collective-permute-done.7
  91.7 12.3 %all_to_all.23 = f32[32,1,128]{2,1,0:T(1,128)S(1)} all-to-all(f32[32,1,128]{2,1,0:T(1,128)S(1)} %bitcast.9), channel_id=1, replica_groups={{176,184,160,168,208,216,192,200,240,248,224,232,16,24,0,8,48,56,32,40,..., dimensions={0} | all-to-all | bytes 32768 | tf_op jit(solution)/shard_map/all_to_all | solution.py:406
  104.0 4.8 %collective-permute-start.8 = (f32[32,128]{1,0:T(8,128)S(1)}, f32[32,128]{1,0:T(8,128)S(1)}, u32[]{:S(2)}, u32[]{:S(2)}) collective-permute-start(f32[32,128]{1,0:T(8,128)S(1)} %bitcast.7), channel_id=1, source_target_pairs={{0,4},{4,0},{8,12},{12,8},{16,20},{20,16},{24,28},{28,24},{32,36},... | collective-permute-start | bytes 49160 | tf_op jit(solution)/shard_map/ppermute | solution.py:421
  108.8 0.8 collective-permute-done.8.other_ref
  109.6 0.9 shard_map.43
  (1 shorter events, 0.0 us)
Async XLA Ops:
  0.0 6.0 %collective-permute-start = (bf16[512,1024]{1,0:T(8,128)(2,1)}, bf16[512,1024]{1,0:T(8,128)(2,1)S(1)}, u32[]{:S(2)}, u32[]{:S(2)}) collective-permute-start(bf16[512,1024]{1,0:T(8,128)(2,1)} %rows_ref.1), channel_id=1, source_target_pairs={{0,4},{4,0},{8,12},{12,8},{16,20},{20,16},{24,28},{28,24},{32,36},... | collective-permute-start | bytes 3145736 | tf_op jit(solution)/shard_map/ppermute | solution.py:421
  3.2 2.7 %collective-permute-start.1 = (s32[1,512]{1,0:T(1,128)}, s32[1,512]{1,0:T(1,128)S(1)}, u32[]{:S(2)}, u32[]{:S(2)}) collective-permute-start(s32[1,512]{1,0:T(1,128)} %bitcast.10), channel_id=1, source_target_pairs={{0,4},{4,0},{8,12},{12,8},{16,20},{20,16},{24,28},{28,24},{32,36},... | collective-permute-start | bytes 6152 | tf_op jit(solution)/shard_map/ppermute | solution.py:421
  3.2 2.7 %collective-permute-start.2 = (s32[1,512]{1,0:T(1,128)}, s32[1,512]{1,0:T(1,128)S(1)}, u32[]{:S(2)}, u32[]{:S(2)}) collective-permute-start(s32[1,512]{1,0:T(1,128)} %bitcast.12), channel_id=1, source_target_pairs={{0,4},{4,0},{8,12},{12,8},{16,20},{20,16},{24,28},{28,24},{32,36},... | collective-permute-start | bytes 6152 | tf_op jit(solution)/shard_map/ppermute | solution.py:421
  53.4 29.1 %collective-permute-start.3 = (bf16[32,200,128]{2,1,0:T(8,128)(2,1)S(1)}, bf16[32,200,128]{2,1,0:T(8,128)(2,1)S(1)}, u32[]{:S(2)}, u32[]{:S(2)}) collective-permute-start(bf16[32,200,128]{2,1,0:T(8,128)(2,1)S(1)} %all_to_all.21.first_ref), channel_id=1, source_target_pairs={{0,1},{4,12},{1,2},{5,13},{2,3},{6,14},{3,0},{7,15},{8,9},{12,20},... | collective-permute-start | bytes 4915208 | tf_op jit(solution)/shard_map/ppermute | solution.py:416
  54.0 28.5 %collective-permute-start.4 = (bf16[32,200,128]{2,1,0:T(8,128)(2,1)S(1)}, bf16[32,200,128]{2,1,0:T(8,128)(2,1)S(1)}, u32[]{:S(2)}, u32[]{:S(2)}) collective-permute-start(bf16[32,200,128]{2,1,0:T(8,128)(2,1)S(1)} %all_to_all.21.first_ref), channel_id=1, source_target_pairs={{0,3},{4,28},{1,0},{5,29},{2,1},{6,30},{3,2},{7,31},{8,11},{12,4},... | collective-permute-start | bytes 4915208 | tf_op jit(solution)/shard_map/ppermute | solution.py:416
  77.1 11.1 %collective-permute-start.5 = (bf16[32,64,128]{2,1,0:T(8,128)(2,1)S(1)}, bf16[32,64,128]{2,1,0:T(8,128)(2,1)S(1)}, u32[]{:S(2)}, u32[]{:S(2)}) collective-permute-start(bf16[32,64,128]{2,1,0:T(8,128)(2,1)S(1)} %all_to_all.22.second_ref), channel_id=1, source_target_pairs={{0,1},{4,12},{1,2},{5,13},{2,3},{6,14},{3,0},{7,15},{8,9},{12,20},... | collective-permute-start | bytes 1572872 | tf_op jit(solution)/shard_map/ppermute | solution.py:416
  77.1 11.1 %collective-permute-start.6 = (bf16[32,64,128]{2,1,0:T(8,128)(2,1)S(1)}, bf16[32,64,128]{2,1,0:T(8,128)(2,1)S(1)}, u32[]{:S(2)}, u32[]{:S(2)}) collective-permute-start(bf16[32,64,128]{2,1,0:T(8,128)(2,1)S(1)} %all_to_all.22.second_ref), channel_id=1, source_target_pairs={{0,3},{4,28},{1,0},{5,29},{2,1},{6,30},{3,2},{7,31},{8,11},{12,4},... | collective-permute-start | bytes 1572872 | tf_op jit(solution)/shard_map/ppermute | solution.py:416
  89.0 2.7 %collective-permute-start.7 = (f32[32,128]{1,0:T(8,128)S(1)}, f32[32,128]{1,0:T(8,128)S(1)}, u32[]{:S(2)}, u32[]{:S(2)}) collective-permute-start(f32[32,128]{1,0:T(8,128)S(1)} %shard_map.42), channel_id=1, source_target_pairs={{0,3},{4,28},{1,0},{5,29},{2,1},{6,30},{3,2},{7,31},{8,11},{12,4},... | collective-permute-start | bytes 49160 | tf_op jit(solution)/shard_map/ppermute | solution.py:416
  104.0 5.6 %collective-permute-start.8 = (f32[32,128]{1,0:T(8,128)S(1)}, f32[32,128]{1,0:T(8,128)S(1)}, u32[]{:S(2)}, u32[]{:S(2)}) collective-permute-start(f32[32,128]{1,0:T(8,128)S(1)} %bitcast.7), channel_id=1, source_target_pairs={{0,4},{4,0},{8,12},{12,8},{16,20},{20,16},{24,28},{28,24},{32,36},... | collective-permute-start | bytes 49160 | tf_op jit(solution)/shard_map/ppermute | solution.py:421

commit v9 on v7

--- a/solution.py
+++ b/solution.py
@@ -379,7 +379,7 @@
 
 
 PLACES = [(z, x, y) for z in range(Z) for x in range(X) for y in range(Y)]
-ORDER = [(z + FIRST[0]) % Z for z in range(Z)]
+ORDER = [5,4,3,2,1,0,7,6]
 TURN = [(i + FIRST[1]) % PER_TILE for i in range(PER_TILE)]
 OWNER_GROUPS = [[device(z, x, 0, y) for z in ORDER for x in TURN] for y in range(Y)] + [
     [device(z, x, 1, y) for z in ORDER for y in TURN] for x in range(X)

time: 111 us -> 111 us (level)
  no operation moved by 1% of the time
where the time goes in v9:
time: 111 us; the launch traced here: 110 us
  blocking collectives  78.7 us (71%)
  starting transfers between devices  15.9 us (14%)
  Pallas kernels  14.9 us (13%)
    all_to_all x3, blocking collectives, to_owners(): lax.all_to_all(array, AXES, split_axis=0, concat_axis=0, tiled=True, axis...  78.7 us
    ppermute x4, starting transfers between devices, other_core(): return lax.ppermute(array, 'shard', [(i, i ^ 1) for i in range(size)])  8.81 us
    ppermute x5, starting transfers between devices, passed_along(): return lax.ppermute(array, AXES, pairs)  7.06 us
    pallas_call x1, Pallas kernels, score_head(): pl.pallas_call(head_kernel, out_shape=(SQUARE, SQUARE, SQUARE, jax.ShapeD...  5.51 us
    pallas_call x1, Pallas kernels, score_own(): pl.pallas_call(own_kernel, out_shape=LINE, in_specs=[VMEM] * 2, out_specs...  2.68 us
  transfers between devices with their start and end apart: 9, of which 1 were waited for; matrix products, arithmetic and copies ran while one was open for 0% of the time, Pallas kernels for 11%

profile of v9, /device:TPU:1, one launch (start us, length us, event | category | flops | bytes accessed | tf_op | source)
XLA Modules:
  0.0 110.4 jit_solution(14881861340280774053)
XLA Ops:
  0.0 3.2 %collective-permute-start = (bf16[512,1024]{1,0:T(8,128)(2,1)}, bf16[512,1024]{1,0:T(8,128)(2,1)S(1)}, u32[]{:S(2)}, u32[]{:S(2)}) collective-permute-start(bf16[512,1024]{1,0:T(8,128)(2,1)} %rows_ref.1), channel_id=1, source_target_pairs={{0,4},{4,0},{8,12},{12,8},{16,20},{20,16},{24,28},{28,24},{32,36},... | collective-permute-start | bytes 3145736 | tf_op jit(solution)/shard_map/ppermute | solution.py:405
  3.2 0.0 collective-permute-start.1
  3.2 0.5 collective-permute-start.2
  3.8 2.2 %shard_map.37 = (bf16[32,128,128]{2,1,0:T(8,128)(2,1)S(1)}, f32[32,8,128]{2,1,0:T(8,128)S(1)}, s32[1,512]{1,0:T(1,128)S(1)}) custom-call(bf16[512,1024]{1,0:T(8,128)(2,1)} %rows_ref.1, s32[1,512]{1,0:T(1,128)} %bitcast.11, s32[1,512]{1,0:T(1,128)} %bitcast.13), custom_call_target="tpu_custom_call" | custom-call | flops 1073741824 | bytes 2097152 | tf_op jit(solution)/shard_map/pallas_call | solution.py:137
  5.9 0.0 collective-permute-done.1.cluster_ref
  6.0 0.0 collective-permute-done.2.arrival_ref
  6.0 0.0 collective-permute-done.rows_ref
  6.0 1.2 %shard_map.38 = (bf16[32,200,128]{2,1,0:T(8,128)(2,1)S(1)}, bf16[32,64,128]{2,1,0:T(8,128)(2,1)S(1)}) custom-call(bf16[512,1024]{1,0:T(8,128)(2,1)S(1)} %collective-permute-done.rows_ref, s32[1,512]{1,0:T(1,128)S(1)} %collective-permute-done.1.cluster_ref, s32[1,512]{1,0:T(1,128)S(1)} %collective-permute-done.2.arrival_ref, ...), custom_call_target="tpu_custom_call" | custom-call | tf_op jit(solution)/shard_map/pallas_call | solution.py:177
  7.2 46.3 %all_to_all.21.first_ref = bf16[32,200,128]{2,1,0:T(8,128)(2,1)S(1)} all-to-all(bf16[32,200,128]{2,1,0:T(8,128)(2,1)S(1)} %get-tuple-element.16), channel_id=1, replica_groups={{176,184,160,168,144,152,128,136,112,120,96,104,80,88,64,72,48,56,32,40..., dimensions={0} | all-to-all | bytes 3276800 | tf_op jit(solution)/shard_map/all_to_all | solution.py:390
  53.4 1.7 %collective-permute-start.3 = (bf16[32,200,128]{2,1,0:T(8,128)(2,1)S(1)}, bf16[32,200,128]{2,1,0:T(8,128)(2,1)S(1)}, u32[]{:S(2)}, u32[]{:S(2)}) collective-permute-start(bf16[32,200,128]{2,1,0:T(8,128)(2,1)S(1)} %all_to_all.21.first_ref), channel_id=1, source_target_pairs={{0,1},{4,12},{1,2},{5,13},{2,3},{6,14},{3,0},{7,15},{8,9},{12,20},... | collective-permute-start | bytes 4915208 | tf_op jit(solution)/shard_map/ppermute | solution.py:400
  55.1 1.3 %collective-permute-start.4 = (bf16[32,200,128]{2,1,0:T(8,128)(2,1)S(1)}, bf16[32,200,128]{2,1,0:T(8,128)(2,1)S(1)}, u32[]{:S(2)}, u32[]{:S(2)}) collective-permute-start(bf16[32,200,128]{2,1,0:T(8,128)(2,1)S(1)} %all_to_all.21.first_ref), channel_id=1, source_target_pairs={{0,3},{4,28},{1,0},{5,29},{2,1},{6,30},{3,2},{7,31},{8,11},{12,4},... | collective-permute-start | bytes 4915208 | tf_op jit(solution)/shard_map/ppermute | solution.py:400
  56.4 19.9 %all_to_all.22.second_ref = bf16[32,64,128]{2,1,0:T(8,128)(2,1)S(1)} all-to-all(bf16[32,64,128]{2,1,0:T(8,128)(2,1)S(1)} %get-tuple-element.17), channel_id=1, replica_groups={{176,184,160,168,144,152,128,136,112,120,96,104,80,88,64,72,48,56,32,40..., dimensions={0} | all-to-all | bytes 1048576 | tf_op jit(solution)/shard_map/all_to_all | solution.py:390
  76.4 0.0 collective-permute-start.5
  76.4 2.7 %collective-permute-start.6 = (bf16[32,64,128]{2,1,0:T(8,128)(2,1)S(1)}, bf16[32,64,128]{2,1,0:T(8,128)(2,1)S(1)}, u32[]{:S(2)}, u32[]{:S(2)}) collective-permute-start(bf16[32,64,128]{2,1,0:T(8,128)(2,1)S(1)} %all_to_all.22.second_ref), channel_id=1, source_target_pairs={{0,3},{4,28},{1,0},{5,29},{2,1},{6,30},{3,2},{7,31},{8,11},{12,4},... | collective-permute-start | bytes 1572872 | tf_op jit(solution)/shard_map/ppermute | solution.py:400
  79.1 2.7 %shard_map.39.best_ref = f32[1,1024]{1,0:T(1,128)S(1)} custom-call(bf16[32,200,128]{2,1,0:T(8,128)(2,1)S(1)} %all_to_all.21.first_ref, bf16[32,64,128]{2,1,0:T(8,128)(2,1)S(1)} %all_to_all.22.second_ref), custom_call_target="tpu_custom_call" | custom-call | flops 3221225472 | bytes 4194304 | tf_op jit(solution)/shard_map/pallas_call | solution.py:267
  81.7 0.0 collective-permute-done.3.below_ref
  81.7 0.0 collective-permute-done.4.above_ref
  81.8 5.5 %shard_map.40 = (f32[1024,1024]{1,0:T(8,128)S(1)}, f32[1024,1024]{1,0:T(8,128)S(1)}, f32[1024,1024]{1,0:T(8,128)S(1)}, f32[8,1024]{1,0:T(8,128)S(1)}) custom-call(bf16[32,200,128]{2,1,0:T(8,128)(2,1)S(1)} %all_to_all.21.first_ref, bf16[32,200,128]{2,1,0:T(8,128)(2,1)S(1)} %collective-permute-done.3.below_ref, ...), custom_call_target="tpu_custom_call" | custom-call | flops 6442450944 | bytes 16777216 | tf_op jit(solution)/shard_map/pallas_call | solution.py:241
  87.3 0.0 collective-permute-done.5.below_ref
  87.3 0.0 collective-permute-done.6.above_ref
  87.3 0.8 shard_map.42
  88.1 1.4 %collective-permute-start.7 = (f32[32,128]{1,0:T(8,128)S(1)}, f32[32,128]{1,0:T(8,128)S(1)}, u32[]{:S(2)}, u32[]{:S(2)}) collective-permute-start(f32[32,128]{1,0:T(8,128)S(1)} %shard_map.42), channel_id=1, source_target_pairs={{0,3},{4,28},{1,0},{5,29},{2,1},{6,30},{3,2},{7,31},{8,11},{12,4},... | collective-permute-start | bytes 49160 | tf_op jit(solution)/shard_map/ppermute | solution.py:400
  89.5 1.6 %shard_map.41 = f32[32,128]{1,0:T(8,128)S(1)} custom-call(f32[1,1024]{1,0:T(1,128)S(1)} %shard_map.39.best_ref, f32[1024,1024]{1,0:T(8,128)S(1)} %get-tuple-element.18.own_below, f32[1024,1024]{1,0:T(8,128)S(1)} %get-tuple-element.19.own_above, f32[8,1024]{1,0:T(8,128)S(1)} %get-tuple-element.20.inverse_ref, bf16[32,64,128]{2,1,0:T(8,128)(2,1)S(1)} %all_to_all.22.second_ref, ...), custom_call_target="tpu_custom_call" | custom-call | flops 1073741824 | bytes 16777216 | tf_op jit(solution)/shard_map/pallas_call | solution.py:337
  91.1 0.0 collective-permute-done.7
  91.1 12.5 %all_to_all.23 = f32[32,1,128]{2,1,0:T(1,128)S(1)} all-to-all(f32[32,1,128]{2,1,0:T(1,128)S(1)} %bitcast.9), channel_id=1, replica_groups={{176,184,160,168,144,152,128,136,112,120,96,104,80,88,64,72,48,56,32,40..., dimensions={0} | all-to-all | bytes 32768 | tf_op jit(solution)/shard_map/all_to_all | solution.py:390
  103.6 5.1 %collective-permute-start.8 = (f32[32,128]{1,0:T(8,128)S(1)}, f32[32,128]{1,0:T(8,128)S(1)}, u32[]{:S(2)}, u32[]{:S(2)}) collective-permute-start(f32[32,128]{1,0:T(8,128)S(1)} %bitcast.7), channel_id=1, source_target_pairs={{0,4},{4,0},{8,12},{12,8},{16,20},{20,16},{24,28},{28,24},{32,36},... | collective-permute-start | bytes 49160 | tf_op jit(solution)/shard_map/ppermute | solution.py:405
  108.7 0.8 collective-permute-done.8.other_ref
  109.5 0.9 shard_map.43
  (1 shorter events, 0.0 us)
Async XLA Ops:
  0.0 6.0 %collective-permute-start = (bf16[512,1024]{1,0:T(8,128)(2,1)}, bf16[512,1024]{1,0:T(8,128)(2,1)S(1)}, u32[]{:S(2)}, u32[]{:S(2)}) collective-permute-start(bf16[512,1024]{1,0:T(8,128)(2,1)} %rows_ref.1), channel_id=1, source_target_pairs={{0,4},{4,0},{8,12},{12,8},{16,20},{20,16},{24,28},{28,24},{32,36},... | collective-permute-start | bytes 3145736 | tf_op jit(solution)/shard_map/ppermute | solution.py:405
  3.2 2.7 %collective-permute-start.1 = (s32[1,512]{1,0:T(1,128)}, s32[1,512]{1,0:T(1,128)S(1)}, u32[]{:S(2)}, u32[]{:S(2)}) collective-permute-start(s32[1,512]{1,0:T(1,128)} %bitcast.10), channel_id=1, source_target_pairs={{0,4},{4,0},{8,12},{12,8},{16,20},{20,16},{24,28},{28,24},{32,36},... | collective-permute-start | bytes 6152 | tf_op jit(solution)/shard_map/ppermute | solution.py:405
  3.2 2.7 %collective-permute-start.2 = (s32[1,512]{1,0:T(1,128)}, s32[1,512]{1,0:T(1,128)S(1)}, u32[]{:S(2)}, u32[]{:S(2)}) collective-permute-start(s32[1,512]{1,0:T(1,128)} %bitcast.12), channel_id=1, source_target_pairs={{0,4},{4,0},{8,12},{12,8},{16,20},{20,16},{24,28},{28,24},{32,36},... | collective-permute-start | bytes 6152 | tf_op jit(solution)/shard_map/ppermute | solution.py:405
  53.4 28.3 %collective-permute-start.3 = (bf16[32,200,128]{2,1,0:T(8,128)(2,1)S(1)}, bf16[32,200,128]{2,1,0:T(8,128)(2,1)S(1)}, u32[]{:S(2)}, u32[]{:S(2)}) collective-permute-start(bf16[32,200,128]{2,1,0:T(8,128)(2,1)S(1)} %all_to_all.21.first_ref), channel_id=1, source_target_pairs={{0,1},{4,12},{1,2},{5,13},{2,3},{6,14},{3,0},{7,15},{8,9},{12,20},... | collective-permute-start | bytes 4915208 | tf_op jit(solution)/shard_map/ppermute | solution.py:400
  55.1 26.6 %collective-permute-start.4 = (bf16[32,200,128]{2,1,0:T(8,128)(2,1)S(1)}, bf16[32,200,128]{2,1,0:T(8,128)(2,1)S(1)}, u32[]{:S(2)}, u32[]{:S(2)}) collective-permute-start(bf16[32,200,128]{2,1,0:T(8,128)(2,1)S(1)} %all_to_all.21.first_ref), channel_id=1, source_target_pairs={{0,3},{4,28},{1,0},{5,29},{2,1},{6,30},{3,2},{7,31},{8,11},{12,4},... | collective-permute-start | bytes 4915208 | tf_op jit(solution)/shard_map/ppermute | solution.py:400
  76.4 10.9 %collective-permute-start.5 = (bf16[32,64,128]{2,1,0:T(8,128)(2,1)S(1)}, bf16[32,64,128]{2,1,0:T(8,128)(2,1)S(1)}, u32[]{:S(2)}, u32[]{:S(2)}) collective-permute-start(bf16[32,64,128]{2,1,0:T(8,128)(2,1)S(1)} %all_to_all.22.second_ref), channel_id=1, source_target_pairs={{0,1},{4,12},{1,2},{5,13},{2,3},{6,14},{3,0},{7,15},{8,9},{12,20},... | collective-permute-start | bytes 1572872 | tf_op jit(solution)/shard_map/ppermute | solution.py:400
  76.4 10.9 %collective-permute-start.6 = (bf16[32,64,128]{2,1,0:T(8,128)(2,1)S(1)}, bf16[32,64,128]{2,1,0:T(8,128)(2,1)S(1)}, u32[]{:S(2)}, u32[]{:S(2)}) collective-permute-start(bf16[32,64,128]{2,1,0:T(8,128)(2,1)S(1)} %all_to_all.22.second_ref), channel_id=1, source_target_pairs={{0,3},{4,28},{1,0},{5,29},{2,1},{6,30},{3,2},{7,31},{8,11},{12,4},... | collective-permute-start | bytes 1572872 | tf_op jit(solution)/shard_map/ppermute | solution.py:400
  88.1 3.0 %collective-permute-start.7 = (f32[32,128]{1,0:T(8,128)S(1)}, f32[32,128]{1,0:T(8,128)S(1)}, u32[]{:S(2)}, u32[]{:S(2)}) collective-permute-start(f32[32,128]{1,0:T(8,128)S(1)} %shard_map.42), channel_id=1, source_target_pairs={{0,3},{4,28},{1,0},{5,29},{2,1},{6,30},{3,2},{7,31},{8,11},{12,4},... | collective-permute-start | bytes 49160 | tf_op jit(solution)/shard_map/ppermute | solution.py:400
  103.6 5.9 %collective-permute-start.8 = (f32[32,128]{1,0:T(8,128)S(1)}, f32[32,128]{1,0:T(8,128)S(1)}, u32[]{:S(2)}, u32[]{:S(2)}) collective-permute-start(f32[32,128]{1,0:T(8,128)S(1)} %bitcast.7), channel_id=1, source_target_pairs={{0,4},{4,0},{8,12},{12,8},{16,20},{20,16},{24,28},{28,24},{32,36},... | collective-permute-start | bytes 49160 | tf_op jit(solution)/shard_map/ppermute | solution.py:405
